TPU v7x, 256 devices: a whole 4x4x8 slice. The times are simulated.
256 devices in a mesh: dp: 2 (over x_lo), resp: 16 (over z, core), tensor: 8 (over y, x_hi).
Axes of the slice: x: 4 (x_hi: 2, x_lo: 2; x = x_hi * 2 + x_lo), y: 4, z: 8, core: 2. Of those that a mesh axis runs over, the one named last changes fastest.
Arguments:
- queries: bfloat16 [8192, 8192], P(('dp', 'resp'), 'tensor'), parts along dimension 0, may hold values from -200 to 200
- resp_keys: bfloat16 [8192, 1024], P(('dp', 'resp'), 'tensor'), parts along dimension 0, may hold values from -6 to 6
- resp_values: bfloat16 [8192, 1024], P(('dp', 'resp'), 'tensor'), parts along dimension 0, may hold values from -6 to 6
- prompt_keys: bfloat16 [4096, 1024], P(('dp', 'resp'), 'tensor'), parts along dimension 0, may hold values from -6 to 6
- prompt_values: bfloat16 [4096, 1024], P(('dp', 'resp'), 'tensor'), parts along dimension 0, may hold values from -6 to 6
- out_grad: bfloat16 [8192, 8192], P(('dp', 'resp'), 'tensor'), parts along dimension 0, may hold values from -6 to 6
- pref_table: bfloat16 [16, 8192], P(None, 'tensor'), may hold values from -6 to 6
- pref_ids: int32 [32], P(('dp', 'resp')), parts along dimension 0, may hold values from 0 to 15
- resp_len: int32 [32], P(('dp', 'resp')), parts along dimension 0, may hold values from 1 to 256, 3072 in all
Outputs:
- query_grad: bfloat16 [8192, 8192], P(('dp', 'resp'), 'tensor'), parts along dimension 0
- resp_key_grad: bfloat16 [8192, 1024], P(('dp', 'resp'), 'tensor'), parts along dimension 0
- resp_value_grad: bfloat16 [8192, 1024], P(('dp', 'resp'), 'tensor'), parts along dimension 0
- prompt_key_grad: bfloat16 [4096, 1024], P(('dp', 'resp'), 'tensor'), parts along dimension 0
- prompt_value_grad: bfloat16 [4096, 1024], P(('dp', 'resp'), 'tensor'), parts along dimension 0
- pref_grad: float32 [32, 8192], P('dp', 'tensor'), parts along dimension 0
There are 2 independent parts, one for each index of `dp`. A program takes and returns all parts, laid end to end along the dimension named above; an argument that names none is the same for every part. Nothing has to cross between parts.
Inputs may be any that keep to these rules, and one draw needn't show every extreme that they name: `resp_len`: in each group the lengths sum to 3072 and one of them is 256.
All inputs are finite; a program needn't handle non-finite values.
Results may differ from a plain program's by a relative error of at most 0.023.
Values may be sent and summed in bfloat16 or wider, within the bound.
No kernel may reach another device: no remote copies, remote signals or barrier semaphores. Data moves between devices by JAX's collectives and lax.ppermute only.
A program may use at most 64 MiB of HBM per device.

v0:
```python
import jax
import jax.numpy as jnp
from jax import lax
from jax.sharding import PartitionSpec as P

HEAD_DIM = 128
GROUP = 8


def pair_layout(block, kv_count, row_count):
    shaped = block.reshape(row_count, kv_count, GROUP // 2, 2, HEAD_DIM).transpose(1, 2, 3, 0, 4)
    return shaped.reshape(kv_count, GROUP // 2, 2 * row_count, HEAD_DIM)


def shards(
    queries,
    resp_keys,
    resp_values,
    prompt_keys,
    prompt_values,
    out_grad,
    pref_table,
    pref_ids,
    resp_len,
):
    row_count = queries.shape[0]
    kv_count = resp_keys.shape[1] // HEAD_DIM
    scaling = HEAD_DIM ** (-0.5)
    chosen = (jnp.arange(pref_table.shape[0], dtype=jnp.int32) == pref_ids[0]).astype(jnp.float32)
    pref_vector = jnp.sum(chosen[:, None] * pref_table.astype(jnp.float32), axis=0)
    biased = (queries.astype(jnp.float32) + pref_vector[None, :]).astype(jnp.bfloat16)
    is_valid = jnp.arange(row_count, dtype=jnp.int32) < resp_len[0]
    masked_grad = jnp.where(is_valid[:, None], out_grad, jnp.zeros((), jnp.bfloat16))
    query_pairs = pair_layout(biased, kv_count, row_count)
    grad_pairs = pair_layout(masked_grad, kv_count, row_count)
    whole_keys, whole_values = (
        lax.all_gather(prompt_keys, "resp", axis=0, tiled=True),
        lax.all_gather(prompt_values, "resp", axis=0, tiled=True),
    )
    prompt_rows = whole_keys.shape[0]
    positions = jnp.arange(row_count, dtype=jnp.int32)
    causal = positions[:, None] >= positions[None, :]
    mask_single = jnp.concatenate([jnp.ones((row_count, prompt_rows), bool), causal], axis=1)
    mask_double = jnp.concatenate([mask_single, mask_single], axis=0)
    stat_heads = []
    key_block = jnp.concatenate([whole_keys, resp_keys], axis=0)
    value_block = jnp.concatenate([whole_values, resp_values], axis=0)

    def pair_step(running, pieces):
        query_rows, grad_rows = pieces
        scores = jnp.dot(query_rows, key_block.T, preferred_element_type=jnp.float32) * scaling
        scores = jnp.where(mask_double, scores, -1e30)
        row_max = jnp.max(scores, axis=1, keepdims=True)
        exponent = jnp.exp(scores - row_max)
        row_total = jnp.sum(exponent, axis=1, keepdims=True)
        weights = exponent / row_total
        low_weights = weights.astype(jnp.bfloat16)
        output = jnp.dot(low_weights, value_block, preferred_element_type=jnp.float32)
        row_delta = jnp.sum(grad_rows.astype(jnp.float32) * output, axis=1, keepdims=True)
        grad_weights = jnp.dot(grad_rows, value_block.T, preferred_element_type=jnp.float32)
        grad_scores = (weights * (grad_weights - row_delta)).astype(jnp.bfloat16)
        grad_query = jnp.dot(grad_scores, key_block, preferred_element_type=jnp.float32) * scaling
        grad_keys = (
            running[0]
            + jnp.dot(grad_scores.T, query_rows, preferred_element_type=jnp.float32) * scaling
        )
        grad_values = running[1] + jnp.dot(
            low_weights.T, grad_rows, preferred_element_type=jnp.float32
        )
        return ((grad_keys, grad_values), (grad_query, row_max, row_total, row_delta))

    zero_block = jnp.zeros((key_block.shape[0], HEAD_DIM), jnp.float32)
    (grad_keys, grad_values), (grad_query, row_max, row_total, row_delta) = lax.scan(
        pair_step, (zero_block, zero_block), (query_pairs[0], grad_pairs[0])
    )
    query_heads = [grad_query]
    key_heads = [grad_keys]
    value_heads = [grad_values]
    stat_heads.append((row_max, row_total, row_delta))
    grad_all = jnp.stack(query_heads).reshape(kv_count, GROUP // 2, 2, row_count, HEAD_DIM)
    grad_all = grad_all.transpose(3, 0, 1, 2, 4).reshape(row_count, kv_count * GROUP * HEAD_DIM)
    query_grad = grad_all.astype(jnp.bfloat16)
    row_sums = jnp.sum(grad_all, axis=0)
    pref_grad = lax.psum((chosen[:, None] * row_sums[None, :]).astype(jnp.bfloat16), "resp").astype(
        jnp.float32
    )
    resp_key_grad = jnp.concatenate([block[-row_count:] for block in key_heads], axis=1).astype(
        jnp.bfloat16
    )
    resp_value_grad = jnp.concatenate([block[-row_count:] for block in value_heads], axis=1).astype(
        jnp.bfloat16
    )
    terms = jnp.concatenate(
        [block[:prompt_rows] for block in key_heads]
        + [block[:prompt_rows] for block in value_heads],
        axis=1,
    )
    summed = lax.psum_scatter(
        terms.astype(jnp.bfloat16), "resp", scatter_dimension=0, tiled=True
    ).astype(jnp.float32)
    width = kv_count * HEAD_DIM
    prompt_key_grad = summed[:, :width].astype(jnp.bfloat16)
    prompt_value_grad = summed[:, width:].astype(jnp.bfloat16)
    return (
        query_grad,
        resp_key_grad,
        resp_value_grad,
        prompt_key_grad,
        prompt_value_grad,
        pref_grad,
    )


def solution(mesh):
    in_specs = (
        P(("dp", "resp"), "tensor"),
        P(("dp", "resp"), "tensor"),
        P(("dp", "resp"), "tensor"),
        P(("dp", "resp"), "tensor"),
        P(("dp", "resp"), "tensor"),
        P(("dp", "resp"), "tensor"),
        P(None, "tensor"),
        P(("dp", "resp")),
        P(("dp", "resp")),
    )
    out_specs = (
        P(("dp", "resp"), "tensor"),
        P(("dp", "resp"), "tensor"),
        P(("dp", "resp"), "tensor"),
        P(("dp", "resp"), "tensor"),
        P(("dp", "resp"), "tensor"),
        P("dp", "tensor"),
    )
    return jax.shard_map(shards, mesh=mesh, in_specs=in_specs, out_specs=out_specs, check_vma=False)
```

profile of v0, /device:TPU:1, one launch (start us, length us, event | category | flops | bytes accessed | tf_op | source)
XLA Modules:
  0.0 185.6 jit_solution(17191258952016347495)
XLA Ops:
  8.0 0.8 multiply_reduce_fusion
  8.8 1.1 add_convert_fusion
  10.4 0.9 copy.15
  12.4 1.0 copy.16
  13.4 1.1 squeeze_reshape.7
  15.0 22.8 %all_gather.6 = bf16[2048,128]{1,0:T(8,128)(2,1)S(1)} all-gather(bf16[128,128]{1,0:T(8,128)(2,1)S(1)} %copy-done.12), channel_id=1, replica_groups=mesh['dp'=2,'resp'=16,'tensor'=8] {'resp'}, dimensions={0}, use_global_device_ids=true | all-gather | bytes 557056 | tf_op jit(solution)/shard_map/all_gather | solution.py:37
  37.8 17.3 %all_gather.7 = bf16[2048,128]{1,0:T(8,128)(2,1)} all-gather(bf16[128,128]{1,0:T(8,128)(2,1)S(1)} %copy-done.13), channel_id=1, replica_groups=mesh['dp'=2,'resp'=16,'tensor'=8] {'resp'}, dimensions={0}, use_global_device_ids=true | all-gather | bytes 557056 | tf_op jit(solution)/shard_map/all_gather | solution.py:38
  55.1 1.1 pad_maximum_fusion.2
  56.2 65.5 %while.15 = (s32[]{:T(128)}, f32[2304,128]{1,0:T(8,128)S(1)}, f32[2304,128]{1,0:T(8,128)}, f32[4,512,128]{2,1,0:T(8,128)}, bf16[4,512,128]{2,1,0:T(8,128)(2,1)},...) while((s32[]{:T(128)}, f32[2304,128]{1,0:T(8,128)S(1)}, ...), condition=%wide.region_5.6_spmd.clone, body=%wide.region_1.5_spmd.clone.sunk | while | flops 1827830272 | bytes 108020104 | solution.py:73
  56.3 2.2 %fusion.66 = (f32[512]{0:T(512)S(1)}, f32[512,2304]{1,0:T(8,128)S(1)}) fusion(pred[512,2304]{1,0:T(32,128)(4,1)S(1)} %get-tuple-element.197, bf16[2304,128]{1,0:T(8,128)(2,1)S(1)} %get-tuple-element.196, bf16[4,512,128]{2,1,0:T(8,128)(2,1)} %get-tuple-element.195, s32[]{:T(128)} %get-tuple-element.180), kind=kOutput, calls=%fused_computation.44.clone.1 | convolution fusion | flops 305528320 | bytes 6621696 | tf_op jit(solution)/shard_map/while/body/eval_jaxpr/dot_general | solution.py:51
  59.2 1.0 fusion.68
  60.3 0.9 fusion.69
  61.2 1.1 copy-done
  62.3 2.1 %fusion.70 = bf16[512,2304]{1,0:T(8,128)(2,1)S(1)} fusion(f32[512,2304]{1,0:T(8,128)S(1)} %fusion.68, bf16[2304,128]{1,0:T(8,128)(2,1)} %copy-done.2, f32[512]{0:T(512)S(1)} %fusion.69, bf16[4,512,128]{1,2,0:T(8,128)(2,1)S(1)} %copy-done.8, s32[]{:T(128)} %get-tuple-element.180), kind=kOutput, calls=%fused_computation.5.clone.1 | convolution fusion | flops 305528832 | bytes 7800836 | tf_op jit(solution)/shard_map/while/body/eval_jaxpr/dot_general | solution.py:60
  64.5 2.3 %fusion.71 = f32[2304,128]{1,0:T(8,128)S(1)} fusion(bf16[512,2304]{1,0:T(8,128)(2,1)S(1)} %fusion.70, f32[2304,128]{1,0:T(8,128)S(1)} %get-tuple-element.181, pred[]{:T(512)S(6)} %compare.4, bf16[4,512,128]{2,1,0:T(8,128)(2,1)} %get-tuple-element.195, s32[]{:T(128)} %get-tuple-element.180), kind=kOutput, calls=%fused_computation.10.clone.1 | convolution fusion | flops 302874624 | bytes 4850177 | tf_op jit(solution)/shard_map/while/body/eval_jaxpr/dot_general | solution.py:65
  66.8 2.6 %fusion.72 = f32[4,512,128]{2,1,0:T(8,128)} fusion(f32[4,512,128]{2,1,0:T(8,128)} %get-tuple-element.183, s32[]{:T(128)} %get-tuple-element.180, bf16[512,2304]{1,0:T(8,128)(2,1)S(1)} %fusion.70, bf16[2304,128]{1,0:T(8,128)(2,1)} %copy-done.6), kind=kOutput, calls=%fused_computation.16.clone.1 | convolution fusion | flops 302055424 | bytes 3211776 | tf_op jit(solution)/shard_map/while/body/eval_jaxpr/dot_general | solution.py:62
  69.3 2.9 %convolution_add_fusion.2 = f32[2304,128]{1,0:T(8,128)} fusion(f32[2304,128]{1,0:T(8,128)} %get-tuple-element.182, f32[512,2304]{1,0:T(8,128)S(1)} %copy-done.1, pred[]{:T(512)S(6)} %compare.4, bf16[4,512,128]{1,2,0:T(8,128)(2,1)} %get-tuple-element.198, s32[]{:T(128)} %get-tuple-element.180), kind=kOutput, calls=%fused_computation.8.clone.1 | convolution fusion | flops 303759360 | bytes 7209473 | tf_op jit(solution)/shard_map/while/body/eval_jaxpr/dot_general | solution.py:67
  72.3 2.2 %fusion.66 = (f32[512]{0:T(512)S(1)}, f32[512,2304]{1,0:T(8,128)S(1)}) fusion(pred[512,2304]{1,0:T(32,128)(4,1)S(1)} %get-tuple-element.197, bf16[2304,128]{1,0:T(8,128)(2,1)S(1)} %get-tuple-element.196, bf16[4,512,128]{2,1,0:T(8,128)(2,1)} %get-tuple-element.195, s32[]{:T(128)} %get-tuple-element.180), kind=kOutput, calls=%fused_computation.44.clone.1 | convolution fusion | flops 305528320 | bytes 6621696 | tf_op jit(solution)/shard_map/while/body/eval_jaxpr/dot_general | solution.py:51
  75.3 1.0 fusion.68
  76.3 0.9 fusion.69
  77.3 1.1 copy-done
  78.4 2.1 %fusion.70 = bf16[512,2304]{1,0:T(8,128)(2,1)S(1)} fusion(f32[512,2304]{1,0:T(8,128)S(1)} %fusion.68, bf16[2304,128]{1,0:T(8,128)(2,1)} %copy-done.2, f32[512]{0:T(512)S(1)} %fusion.69, bf16[4,512,128]{1,2,0:T(8,128)(2,1)S(1)} %copy-done.8, s32[]{:T(128)} %get-tuple-element.180), kind=kOutput, calls=%fused_computation.5.clone.1 | convolution fusion | flops 305528832 | bytes 7800836 | tf_op jit(solution)/shard_map/while/body/eval_jaxpr/dot_general | solution.py:60
  80.5 2.3 %fusion.71 = f32[2304,128]{1,0:T(8,128)S(1)} fusion(bf16[512,2304]{1,0:T(8,128)(2,1)S(1)} %fusion.70, f32[2304,128]{1,0:T(8,128)S(1)} %get-tuple-element.181, pred[]{:T(512)S(6)} %compare.4, bf16[4,512,128]{2,1,0:T(8,128)(2,1)} %get-tuple-element.195, s32[]{:T(128)} %get-tuple-element.180), kind=kOutput, calls=%fused_computation.10.clone.1 | convolution fusion | flops 302874624 | bytes 4850177 | tf_op jit(solution)/shard_map/while/body/eval_jaxpr/dot_general | solution.py:65
  82.8 2.5 %fusion.72 = f32[4,512,128]{2,1,0:T(8,128)} fusion(f32[4,512,128]{2,1,0:T(8,128)} %get-tuple-element.183, s32[]{:T(128)} %get-tuple-element.180, bf16[512,2304]{1,0:T(8,128)(2,1)S(1)} %fusion.70, bf16[2304,128]{1,0:T(8,128)(2,1)} %copy-done.6), kind=kOutput, calls=%fused_computation.16.clone.1 | convolution fusion | flops 302055424 | bytes 3211776 | tf_op jit(solution)/shard_map/while/body/eval_jaxpr/dot_general | solution.py:62
  85.4 3.4 %convolution_add_fusion.2 = f32[2304,128]{1,0:T(8,128)} fusion(f32[2304,128]{1,0:T(8,128)} %get-tuple-element.182, f32[512,2304]{1,0:T(8,128)S(1)} %copy-done.1, pred[]{:T(512)S(6)} %compare.4, bf16[4,512,128]{1,2,0:T(8,128)(2,1)} %get-tuple-element.198, s32[]{:T(128)} %get-tuple-element.180), kind=kOutput, calls=%fused_computation.8.clone.1 | convolution fusion | flops 303759360 | bytes 7209473 | tf_op jit(solution)/shard_map/while/body/eval_jaxpr/dot_general | solution.py:67
  88.8 2.2 %fusion.66 = (f32[512]{0:T(512)S(1)}, f32[512,2304]{1,0:T(8,128)S(1)}) fusion(pred[512,2304]{1,0:T(32,128)(4,1)S(1)} %get-tuple-element.197, bf16[2304,128]{1,0:T(8,128)(2,1)S(1)} %get-tuple-element.196, bf16[4,512,128]{2,1,0:T(8,128)(2,1)} %get-tuple-element.195, s32[]{:T(128)} %get-tuple-element.180), kind=kOutput, calls=%fused_computation.44.clone.1 | convolution fusion | flops 305528320 | bytes 6621696 | tf_op jit(solution)/shard_map/while/body/eval_jaxpr/dot_general | solution.py:51
  91.8 1.0 fusion.68
  92.8 0.9 fusion.69
  93.7 1.1 copy-done
  94.9 2.1 %fusion.70 = bf16[512,2304]{1,0:T(8,128)(2,1)S(1)} fusion(f32[512,2304]{1,0:T(8,128)S(1)} %fusion.68, bf16[2304,128]{1,0:T(8,128)(2,1)} %copy-done.2, f32[512]{0:T(512)S(1)} %fusion.69, bf16[4,512,128]{1,2,0:T(8,128)(2,1)S(1)} %copy-done.8, s32[]{:T(128)} %get-tuple-element.180), kind=kOutput, calls=%fused_computation.5.clone.1 | convolution fusion | flops 305528832 | bytes 7800836 | tf_op jit(solution)/shard_map/while/body/eval_jaxpr/dot_general | solution.py:60
  97.0 2.3 %fusion.71 = f32[2304,128]{1,0:T(8,128)S(1)} fusion(bf16[512,2304]{1,0:T(8,128)(2,1)S(1)} %fusion.70, f32[2304,128]{1,0:T(8,128)S(1)} %get-tuple-element.181, pred[]{:T(512)S(6)} %compare.4, bf16[4,512,128]{2,1,0:T(8,128)(2,1)} %get-tuple-element.195, s32[]{:T(128)} %get-tuple-element.180), kind=kOutput, calls=%fused_computation.10.clone.1 | convolution fusion | flops 302874624 | bytes 4850177 | tf_op jit(solution)/shard_map/while/body/eval_jaxpr/dot_general | solution.py:65
  99.3 2.5 %fusion.72 = f32[4,512,128]{2,1,0:T(8,128)} fusion(f32[4,512,128]{2,1,0:T(8,128)} %get-tuple-element.183, s32[]{:T(128)} %get-tuple-element.180, bf16[512,2304]{1,0:T(8,128)(2,1)S(1)} %fusion.70, bf16[2304,128]{1,0:T(8,128)(2,1)} %copy-done.6), kind=kOutput, calls=%fused_computation.16.clone.1 | convolution fusion | flops 302055424 | bytes 3211776 | tf_op jit(solution)/shard_map/while/body/eval_jaxpr/dot_general | solution.py:62
  101.8 3.4 %convolution_add_fusion.2 = f32[2304,128]{1,0:T(8,128)} fusion(f32[2304,128]{1,0:T(8,128)} %get-tuple-element.182, f32[512,2304]{1,0:T(8,128)S(1)} %copy-done.1, pred[]{:T(512)S(6)} %compare.4, bf16[4,512,128]{1,2,0:T(8,128)(2,1)} %get-tuple-element.198, s32[]{:T(128)} %get-tuple-element.180), kind=kOutput, calls=%fused_computation.8.clone.1 | convolution fusion | flops 303759360 | bytes 7209473 | tf_op jit(solution)/shard_map/while/body/eval_jaxpr/dot_general | solution.py:67
  105.3 2.2 %fusion.66 = (f32[512]{0:T(512)S(1)}, f32[512,2304]{1,0:T(8,128)S(1)}) fusion(pred[512,2304]{1,0:T(32,128)(4,1)S(1)} %get-tuple-element.197, bf16[2304,128]{1,0:T(8,128)(2,1)S(1)} %get-tuple-element.196, bf16[4,512,128]{2,1,0:T(8,128)(2,1)} %get-tuple-element.195, s32[]{:T(128)} %get-tuple-element.180), kind=kOutput, calls=%fused_computation.44.clone.1 | convolution fusion | flops 305528320 | bytes 6621696 | tf_op jit(solution)/shard_map/while/body/eval_jaxpr/dot_general | solution.py:51
  108.2 1.0 fusion.68
  109.3 0.9 fusion.69
  110.2 1.1 copy-done
  111.3 2.1 %fusion.70 = bf16[512,2304]{1,0:T(8,128)(2,1)S(1)} fusion(f32[512,2304]{1,0:T(8,128)S(1)} %fusion.68, bf16[2304,128]{1,0:T(8,128)(2,1)} %copy-done.2, f32[512]{0:T(512)S(1)} %fusion.69, bf16[4,512,128]{1,2,0:T(8,128)(2,1)S(1)} %copy-done.8, s32[]{:T(128)} %get-tuple-element.180), kind=kOutput, calls=%fused_computation.5.clone.1 | convolution fusion | flops 305528832 | bytes 7800836 | tf_op jit(solution)/shard_map/while/body/eval_jaxpr/dot_general | solution.py:60
  113.5 2.3 %fusion.71 = f32[2304,128]{1,0:T(8,128)S(1)} fusion(bf16[512,2304]{1,0:T(8,128)(2,1)S(1)} %fusion.70, f32[2304,128]{1,0:T(8,128)S(1)} %get-tuple-element.181, pred[]{:T(512)S(6)} %compare.4, bf16[4,512,128]{2,1,0:T(8,128)(2,1)} %get-tuple-element.195, s32[]{:T(128)} %get-tuple-element.180), kind=kOutput, calls=%fused_computation.10.clone.1 | convolution fusion | flops 302874624 | bytes 4850177 | tf_op jit(solution)/shard_map/while/body/eval_jaxpr/dot_general | solution.py:65
  115.8 2.5 %fusion.72 = f32[4,512,128]{2,1,0:T(8,128)} fusion(f32[4,512,128]{2,1,0:T(8,128)} %get-tuple-element.183, s32[]{:T(128)} %get-tuple-element.180, bf16[512,2304]{1,0:T(8,128)(2,1)S(1)} %fusion.70, bf16[2304,128]{1,0:T(8,128)(2,1)} %copy-done.6), kind=kOutput, calls=%fused_computation.16.clone.1 | convolution fusion | flops 302055424 | bytes 3211776 | tf_op jit(solution)/shard_map/while/body/eval_jaxpr/dot_general | solution.py:62
  118.3 3.4 %convolution_add_fusion.2 = f32[2304,128]{1,0:T(8,128)} fusion(f32[2304,128]{1,0:T(8,128)} %get-tuple-element.182, f32[512,2304]{1,0:T(8,128)S(1)} %copy-done.1, pred[]{:T(512)S(6)} %compare.4, bf16[4,512,128]{1,2,0:T(8,128)(2,1)} %get-tuple-element.198, s32[]{:T(128)} %get-tuple-element.180), kind=kOutput, calls=%fused_computation.8.clone.1 | convolution fusion | flops 303759360 | bytes 7209473 | tf_op jit(solution)/shard_map/while/body/eval_jaxpr/dot_general | solution.py:67
  121.8 1.3 convert.13
  123.2 1.1 pad_maximum_fusion
  125.6 0.8 copy.20
  127.2 43.9 %psum.7 = bf16[16,1024]{1,0:T(8,128)(2,1)S(1)} all-reduce(bf16[16,1024]{1,0:T(8,128)(2,1)S(1)} %multiply_convert_fusion), channel_id=1, replica_groups=mesh['dp'=2,'resp'=16,'tensor'=8] {'resp'}, use_global_device_ids=true, to_apply=%region_8.9 | all-reduce | flops 16384 | bytes 65536 | tf_op jit(solution)/shard_map/psum | solution.py:84
  171.8 1.2 convert_element_type.48
  172.9 4.5 %reduce-scatter.2.cloned.1.call-done = bf16[128,256]{1,0:T(8,128)(2,1)} async-done(((bf16[2048,256]{1,0:T(8,128)(2,1)}), bf16[128,256]{1,0:T(8,128)(2,1)}) %reduce-scatter.2.cloned.1.call-update) | async-done | bytes 65552 | tf_op jit(solution)/shard_map/reduce_scatter | solution.py:98
  177.4 1.4 fusion.30
  (104 shorter events, 7.6 us)
Async XLA Ops:
  7.2 4.7 %copy-start.10 = (bf16[256,1024]{1,0:T(8,128)(2,1)S(1)}, bf16[256,1024]{1,0:T(8,128)(2,1)}, u32[]{:S(2)}) copy-start(bf16[256,1024]{1,0:T(8,128)(2,1)} %param.16) | copy-start | bytes 1572868
  7.2 170.2 %reduce-scatter.2.cloned.1.call-start = ((), (), s32[]{:S(2)}) async-start(), calls=%async_computation.1 | async-start | bytes 1114112 | tf_op jit(solution)/shard_map/reduce_scatter | solution.py:98
  12.4 2.6 %copy-start.12 = (bf16[128,128]{1,0:T(8,128)(2,1)S(1)}, bf16[128,128]{1,0:T(8,128)(2,1)}, u32[]{:S(2)}) copy-start(bf16[128,128]{1,0:T(8,128)(2,1)} %param.14) | copy-start | bytes 98308
  13.4 24.4 %copy-start.13 = (bf16[128,128]{1,0:T(8,128)(2,1)S(1)}, bf16[128,128]{1,0:T(8,128)(2,1)}, u32[]{:S(2)}) copy-start(bf16[128,128]{1,0:T(8,128)(2,1)} %param.15) | copy-start | bytes 98308
  13.4 41.7 %copy-start.11 = (bf16[256,128]{1,0:T(8,128)(2,1)S(1)}, bf16[256,128]{1,0:T(8,128)(2,1)}, u32[]{:S(2)}) copy-start(bf16[256,128]{1,0:T(8,128)(2,1)} %param.12) | copy-start | bytes 196612
  56.2 2.2 %copy-start.4 = (pred[512,2304]{1,0:T(32,128)(4,1)}, pred[512,2304]{1,0:T(32,128)(4,1)S(1)}, u32[]{:S(2)}) copy-start(pred[512,2304]{1,0:T(32,128)(4,1)S(1)} %get-tuple-element.197) | copy-start | bytes 3538948 | tf_op jit(solution)/shard_map/while
  56.3 2.2 %copy-start.6 = (bf16[2304,128]{1,0:T(8,128)(2,1)}, bf16[2304,128]{1,0:T(8,128)(2,1)S(1)}, u32[]{:S(2)}) copy-start(bf16[2304,128]{1,0:T(8,128)(2,1)S(1)} %get-tuple-element.196) | copy-start | bytes 1769476 | tf_op jit(solution)/shard_map/while
  56.3 4.0 %copy-start.2 = (bf16[2304,128]{1,0:T(8,128)(2,1)}, bf16[2304,128]{1,0:T(8,128)(2,1)S(1)}, u32[]{:S(2)}) copy-start(bf16[2304,128]{1,0:T(8,128)(2,1)S(1)} %get-tuple-element.199) | copy-start | bytes 1769476 | tf_op jit(solution)/shard_map/while
  59.2 1.0 copy-start.8
  60.2 2.1 %copy-start = (f32[512,2304]{1,0:T(8,128)}, f32[512,2304]{1,0:T(8,128)S(1)}, u32[]{:S(2)}) copy-start(f32[512,2304]{1,0:T(8,128)S(1)} %fusion.68) | copy-start | bytes 14155780 | tf_op jit(solution)/shard_map/while
  64.5 4.9 %copy-start.1 = (f32[512,2304]{1,0:T(8,128)S(1)}, f32[512,2304]{1,0:T(8,128)}, u32[]{:S(2)}) copy-start(f32[512,2304]{1,0:T(8,128)} %copy-done) | copy-start | bytes 14155780 | tf_op jit(solution)/shard_map/while
  69.3 2.9 %copy-start.3 = (bf16[2304,128]{1,0:T(8,128)(2,1)S(1)}, bf16[2304,128]{1,0:T(8,128)(2,1)}, u32[]{:S(2)}) copy-start(bf16[2304,128]{1,0:T(8,128)(2,1)} %copy-done.2) | copy-start | bytes 1769476 | tf_op jit(solution)/shard_map/while
  69.3 2.9 %copy-start.5 = (pred[512,2304]{1,0:T(32,128)(4,1)S(1)}, pred[512,2304]{1,0:T(32,128)(4,1)}, u32[]{:S(2)}) copy-start(pred[512,2304]{1,0:T(32,128)(4,1)} %copy-done.4) | copy-start | bytes 3538948 | tf_op jit(solution)/shard_map/while
  69.3 2.9 %copy-start.7 = (bf16[2304,128]{1,0:T(8,128)(2,1)S(1)}, bf16[2304,128]{1,0:T(8,128)(2,1)}, u32[]{:S(2)}) copy-start(bf16[2304,128]{1,0:T(8,128)(2,1)} %copy-done.6) | copy-start | bytes 1769476 | tf_op jit(solution)/shard_map/while
  72.3 2.2 %copy-start.4 = (pred[512,2304]{1,0:T(32,128)(4,1)}, pred[512,2304]{1,0:T(32,128)(4,1)S(1)}, u32[]{:S(2)}) copy-start(pred[512,2304]{1,0:T(32,128)(4,1)S(1)} %get-tuple-element.197) | copy-start | bytes 3538948 | tf_op jit(solution)/shard_map/while
  72.3 2.2 %copy-start.6 = (bf16[2304,128]{1,0:T(8,128)(2,1)}, bf16[2304,128]{1,0:T(8,128)(2,1)S(1)}, u32[]{:S(2)}) copy-start(bf16[2304,128]{1,0:T(8,128)(2,1)S(1)} %get-tuple-element.196) | copy-start | bytes 1769476 | tf_op jit(solution)/shard_map/while
  72.3 4.0 %copy-start.2 = (bf16[2304,128]{1,0:T(8,128)(2,1)}, bf16[2304,128]{1,0:T(8,128)(2,1)S(1)}, u32[]{:S(2)}) copy-start(bf16[2304,128]{1,0:T(8,128)(2,1)S(1)} %get-tuple-element.199) | copy-start | bytes 1769476 | tf_op jit(solution)/shard_map/while
  75.3 1.0 copy-start.8
  76.3 2.1 %copy-start = (f32[512,2304]{1,0:T(8,128)}, f32[512,2304]{1,0:T(8,128)S(1)}, u32[]{:S(2)}) copy-start(f32[512,2304]{1,0:T(8,128)S(1)} %fusion.68) | copy-start | bytes 14155780 | tf_op jit(solution)/shard_map/while
  80.5 4.8 %copy-start.1 = (f32[512,2304]{1,0:T(8,128)S(1)}, f32[512,2304]{1,0:T(8,128)}, u32[]{:S(2)}) copy-start(f32[512,2304]{1,0:T(8,128)} %copy-done) | copy-start | bytes 14155780 | tf_op jit(solution)/shard_map/while
  85.4 3.4 %copy-start.3 = (bf16[2304,128]{1,0:T(8,128)(2,1)S(1)}, bf16[2304,128]{1,0:T(8,128)(2,1)}, u32[]{:S(2)}) copy-start(bf16[2304,128]{1,0:T(8,128)(2,1)} %copy-done.2) | copy-start | bytes 1769476 | tf_op jit(solution)/shard_map/while
  85.4 3.4 %copy-start.5 = (pred[512,2304]{1,0:T(32,128)(4,1)S(1)}, pred[512,2304]{1,0:T(32,128)(4,1)}, u32[]{:S(2)}) copy-start(pred[512,2304]{1,0:T(32,128)(4,1)} %copy-done.4) | copy-start | bytes 3538948 | tf_op jit(solution)/shard_map/while
  85.4 3.4 %copy-start.7 = (bf16[2304,128]{1,0:T(8,128)(2,1)S(1)}, bf16[2304,128]{1,0:T(8,128)(2,1)}, u32[]{:S(2)}) copy-start(bf16[2304,128]{1,0:T(8,128)(2,1)} %copy-done.6) | copy-start | bytes 1769476 | tf_op jit(solution)/shard_map/while
  88.8 2.2 %copy-start.4 = (pred[512,2304]{1,0:T(32,128)(4,1)}, pred[512,2304]{1,0:T(32,128)(4,1)S(1)}, u32[]{:S(2)}) copy-start(pred[512,2304]{1,0:T(32,128)(4,1)S(1)} %get-tuple-element.197) | copy-start | bytes 3538948 | tf_op jit(solution)/shard_map/while
  88.8 2.2 %copy-start.6 = (bf16[2304,128]{1,0:T(8,128)(2,1)}, bf16[2304,128]{1,0:T(8,128)(2,1)S(1)}, u32[]{:S(2)}) copy-start(bf16[2304,128]{1,0:T(8,128)(2,1)S(1)} %get-tuple-element.196) | copy-start | bytes 1769476 | tf_op jit(solution)/shard_map/while
  88.8 4.0 %copy-start.2 = (bf16[2304,128]{1,0:T(8,128)(2,1)}, bf16[2304,128]{1,0:T(8,128)(2,1)S(1)}, u32[]{:S(2)}) copy-start(bf16[2304,128]{1,0:T(8,128)(2,1)S(1)} %get-tuple-element.199) | copy-start | bytes 1769476 | tf_op jit(solution)/shard_map/while
  91.8 1.0 copy-start.8
  92.7 2.1 %copy-start = (f32[512,2304]{1,0:T(8,128)}, f32[512,2304]{1,0:T(8,128)S(1)}, u32[]{:S(2)}) copy-start(f32[512,2304]{1,0:T(8,128)S(1)} %fusion.68) | copy-start | bytes 14155780 | tf_op jit(solution)/shard_map/while
  97.0 4.8 %copy-start.1 = (f32[512,2304]{1,0:T(8,128)S(1)}, f32[512,2304]{1,0:T(8,128)}, u32[]{:S(2)}) copy-start(f32[512,2304]{1,0:T(8,128)} %copy-done) | copy-start | bytes 14155780 | tf_op jit(solution)/shard_map/while
  101.8 3.4 %copy-start.3 = (bf16[2304,128]{1,0:T(8,128)(2,1)S(1)}, bf16[2304,128]{1,0:T(8,128)(2,1)}, u32[]{:S(2)}) copy-start(bf16[2304,128]{1,0:T(8,128)(2,1)} %copy-done.2) | copy-start | bytes 1769476 | tf_op jit(solution)/shard_map/while
  101.8 3.4 %copy-start.5 = (pred[512,2304]{1,0:T(32,128)(4,1)S(1)}, pred[512,2304]{1,0:T(32,128)(4,1)}, u32[]{:S(2)}) copy-start(pred[512,2304]{1,0:T(32,128)(4,1)} %copy-done.4) | copy-start | bytes 3538948 | tf_op jit(solution)/shard_map/while
  101.8 3.4 %copy-start.7 = (bf16[2304,128]{1,0:T(8,128)(2,1)S(1)}, bf16[2304,128]{1,0:T(8,128)(2,1)}, u32[]{:S(2)}) copy-start(bf16[2304,128]{1,0:T(8,128)(2,1)} %copy-done.6) | copy-start | bytes 1769476 | tf_op jit(solution)/shard_map/while
  105.2 2.2 %copy-start.4 = (pred[512,2304]{1,0:T(32,128)(4,1)}, pred[512,2304]{1,0:T(32,128)(4,1)S(1)}, u32[]{:S(2)}) copy-start(pred[512,2304]{1,0:T(32,128)(4,1)S(1)} %get-tuple-element.197) | copy-start | bytes 3538948 | tf_op jit(solution)/shard_map/while
  105.2 2.2 %copy-start.6 = (bf16[2304,128]{1,0:T(8,128)(2,1)}, bf16[2304,128]{1,0:T(8,128)(2,1)S(1)}, u32[]{:S(2)}) copy-start(bf16[2304,128]{1,0:T(8,128)(2,1)S(1)} %get-tuple-element.196) | copy-start | bytes 1769476 | tf_op jit(solution)/shard_map/while
  105.3 4.0 %copy-start.2 = (bf16[2304,128]{1,0:T(8,128)(2,1)}, bf16[2304,128]{1,0:T(8,128)(2,1)S(1)}, u32[]{:S(2)}) copy-start(bf16[2304,128]{1,0:T(8,128)(2,1)S(1)} %get-tuple-element.199) | copy-start | bytes 1769476 | tf_op jit(solution)/shard_map/while
  108.2 1.0 copy-start.8
  109.2 2.1 %copy-start = (f32[512,2304]{1,0:T(8,128)}, f32[512,2304]{1,0:T(8,128)S(1)}, u32[]{:S(2)}) copy-start(f32[512,2304]{1,0:T(8,128)S(1)} %fusion.68) | copy-start | bytes 14155780 | tf_op jit(solution)/shard_map/while
  113.5 4.8 %copy-start.1 = (f32[512,2304]{1,0:T(8,128)S(1)}, f32[512,2304]{1,0:T(8,128)}, u32[]{:S(2)}) copy-start(f32[512,2304]{1,0:T(8,128)} %copy-done) | copy-start | bytes 14155780 | tf_op jit(solution)/shard_map/while
  118.3 3.4 %copy-start.3 = (bf16[2304,128]{1,0:T(8,128)(2,1)S(1)}, bf16[2304,128]{1,0:T(8,128)(2,1)}, u32[]{:S(2)}) copy-start(bf16[2304,128]{1,0:T(8,128)(2,1)} %copy-done.2) | copy-start | bytes 1769476 | tf_op jit(solution)/shard_map/while
  118.3 3.4 %copy-start.5 = (pred[512,2304]{1,0:T(32,128)(4,1)S(1)}, pred[512,2304]{1,0:T(32,128)(4,1)}, u32[]{:S(2)}) copy-start(pred[512,2304]{1,0:T(32,128)(4,1)} %copy-done.4) | copy-start | bytes 3538948 | tf_op jit(solution)/shard_map/while
  118.3 3.4 %copy-start.7 = (bf16[2304,128]{1,0:T(8,128)(2,1)S(1)}, bf16[2304,128]{1,0:T(8,128)(2,1)}, u32[]{:S(2)}) copy-start(bf16[2304,128]{1,0:T(8,128)(2,1)} %copy-done.6) | copy-start | bytes 1769476 | tf_op jit(solution)/shard_map/while
  123.1 2.5 %copy-start.9 = (f32[4,512,128]{2,1,0:T(8,128)S(1)}, f32[4,512,128]{2,1,0:T(8,128)}, u32[]{:S(2)}) copy-start(f32[4,512,128]{2,1,0:T(8,128)} %get-tuple-element.55) | copy-start | bytes 3145732
Sparse Core Ops, SparseCore 0:
  124.4 52.9 reduce-scatter.1
where the time goes:
time: 189 us; the launch traced here: 186 us
  blocking collectives  84 us (44%)
  matrix products  53.2 us (28%)
  between operations  15.6 us (8%)
  other arithmetic  14.5 us (8%)
  local copies, waits for them, and re-layouts  13.4 us (7%)
  waiting for transfers between devices  4.49 us (2%)
    psum x1, blocking collectives, shards(): lax.psum((chosen[:, None] * row_sums[None, :]).astype(jnp.bfloat16), 'resp')  43.9 us
    all_gather x1, blocking collectives, shards(): lax.all_gather(prompt_keys, 'resp', axis=0, tiled=True)  22.8 us
    all_gather x1, blocking collectives, shards(): lax.all_gather(prompt_values, 'resp', axis=0, tiled=True)  17.3 us
    dot_general x4, matrix products, pair_step(): jnp.dot(low_weights.T, grad_rows, preferred_element_type=jnp.float32)  13 us
    dot_general x4, matrix products, pair_step(): jnp.dot(grad_scores, key_block, preferred_element_type=jnp.float32)  10.2 us
    dot_general x4, matrix products, pair_step(): jnp.dot(grad_scores.T, query_rows, preferred_element_type=jnp.float32)  9.12 us
    dot_general x4, matrix products, pair_step(): jnp.dot(query_rows, key_block.T, preferred_element_type=jnp.float32)  8.63 us
    dot_general x4, matrix products, pair_step(): jnp.dot(grad_rows, value_block.T, preferred_element_type=jnp.float32)  8.46 us
  transfers between devices with their start and end apart: 1, of which 1 were waited for; matrix products, arithmetic and copies ran while one was open for 3% of the time, Pallas kernels for 0%

commit v1 on v0

v1 whole, which is shorter than its diff:
```python
import functools

import jax
import jax.numpy as jnp
from jax import lax
from jax.experimental import pallas as pl
from jax.experimental.pallas import tpu as pltpu
from jax.sharding import PartitionSpec as P

F32 = jnp.float32
BF16 = jnp.bfloat16
HEAD_DIM = 128
SCALING = HEAD_DIM**-0.5
LOG2E = 1.4426950408889634
HEADS_PER_STEP = 2
CHUNK = 256
RTILE = 16
NT = (((1,), (1,)), ((), ()))
NN = (((1,), (0,)), ((), ()))
VMEM = pl.BlockSpec(memory_space=pltpu.VMEM)
SMEM = pl.BlockSpec(memory_space=pltpu.SMEM)


def ring_moves(n_resp):
    chips = n_resp // 2

    def index(chip, core):
        return (chip % chips) * 2 + core

    places = [(chip, core) for chip in range(chips) for core in range(2)]
    pair = [(index(z, c), index(z, 1 - c)) for z, c in places]
    far = [(index(z, c), index(z + chips // 2, c)) for z, c in places]
    out = [
        [(index(z, c), index(z + k if c == 0 else z - k, c)) for z, c in places]
        for k in range(1, chips // 2)
    ]
    back = [[(b, a) for a, b in moves] for moves in out]
    return pair, far, out, back


def attention_kernel(
    n_blocks,
    id_ref,
    len_ref,
    q_ref,
    g_ref,
    table_ref,
    rk_ref,
    rv_ref,
    *refs,
):
    block_refs = refs[:n_blocks]
    dq_ref, drk_ref, drv_ref, near_ref, direct_ref, via_ref, r_ref = refs[n_blocks : n_blocks + 7]
    keys, values, keys_t, s_scr, p_scr, dk_scr, dv_scr, pref_scr, sum_scr = refs[n_blocks + 7 :]
    rows = q_ref.shape[0]
    heads = q_ref.shape[1] // HEAD_DIM
    n_keys = keys.shape[0]
    n_prompt = n_keys - rows
    width = HEADS_PER_STEP * rows
    at = 0
    for block in block_refs:
        n = block.shape[0]
        keys[at : at + n, :] = block[:, :HEAD_DIM]
        values[at : at + n, :] = block[:, HEAD_DIM:]
        at += n
    keys[n_prompt:, :] = rk_ref[...]
    values[n_prompt:, :] = rv_ref[...]
    keys_t[...] = keys[...].T
    dk_scr[...] = jnp.zeros_like(dk_scr)
    dv_scr[...] = jnp.zeros_like(dv_scr)
    chosen = lax.broadcasted_iota(jnp.int32, table_ref.shape, 0) == id_ref[0]
    pref_scr[...] = jnp.sum(
        jnp.where(chosen, table_ref[...].astype(F32), 0.0), axis=0, keepdims=True
    )
    live = lax.broadcasted_iota(jnp.int32, (rows, HEAD_DIM), 0) < len_ref[0]
    chunks = [(a, min(CHUNK, n_keys - a)) for a in range(0, n_keys, CHUNK)]
    factor = SCALING * LOG2E

    def step(group, carry):
        q_parts, g_parts = [], []
        for i in range(HEADS_PER_STEP):
            cols = pl.ds(
                pl.multiple_of((group * HEADS_PER_STEP + i) * HEAD_DIM, HEAD_DIM), HEAD_DIM
            )
            q_parts.append((q_ref[:, cols].astype(F32) + pref_scr[:, cols]).astype(BF16))
            g_parts.append(jnp.where(live, g_ref[:, cols], jnp.zeros((), BF16)))
        q = jnp.concatenate(q_parts, axis=0)
        g = jnp.concatenate(g_parts, axis=0)
        top = jnp.full((8, width), -1e30, F32)
        for a, n in chunks:
            s = lax.dot_general(keys[a : a + n, :], q, NT, preferred_element_type=F32)
            if a + n > n_prompt:
                key_pos = lax.broadcasted_iota(jnp.int32, (n, width), 0) + (a - n_prompt)
                query_pos = lax.broadcasted_iota(jnp.int32, (n, width), 1) % rows
                s = jnp.where(key_pos <= query_pos, s, -1e30)
            s_scr[a : a + n, :] = s
            top = jnp.maximum(top, jnp.max(s.reshape(n // 8, 8, width), axis=0))
        row_max = jnp.max(top, axis=0, keepdims=True) * factor
        total = jnp.zeros((8, width), F32)
        dot = jnp.zeros((8, width), F32)
        for a, n in chunks:
            p = jnp.exp2(s_scr[a : a + n, :] * factor - row_max)
            dp = lax.dot_general(values[a : a + n, :], g, NT, preferred_element_type=F32)
            total = total + jnp.sum(p.reshape(n // 8, 8, width), axis=0)
            dot = dot + jnp.sum((p * dp).reshape(n // 8, 8, width), axis=0)
            s_scr[a : a + n, :] = dp
            p_scr[a : a + n, :] = p
        inverse = 1.0 / jnp.sum(total, axis=0, keepdims=True)
        delta = jnp.sum(dot, axis=0, keepdims=True) * inverse
        dq = jnp.zeros((HEAD_DIM, width), F32)
        for a, n in chunks:
            w = p_scr[a : a + n, :] * inverse
            ds = (w * (s_scr[a : a + n, :] - delta)).astype(BF16)
            dv_scr[a : a + n, :] += lax.dot_general(
                w.astype(BF16), g, NN, preferred_element_type=F32
            )
            dk_scr[a : a + n, :] += lax.dot_general(ds, q, NN, preferred_element_type=F32)
            dq = dq + lax.dot_general(keys_t[:, a : a + n], ds, NN, preferred_element_type=F32)
        dq = dq.T * SCALING
        for i in range(HEADS_PER_STEP):
            cols = pl.ds(
                pl.multiple_of((group * HEADS_PER_STEP + i) * HEAD_DIM, HEAD_DIM), HEAD_DIM
            )
            part = dq[i * rows : (i + 1) * rows]
            dq_ref[:, cols] = part.astype(BF16)
            sum_scr[:, cols] = jnp.sum(part, axis=0, keepdims=True)
        return carry

    lax.fori_loop(0, heads // HEADS_PER_STEP, step, 0)

    at = 0
    for ref in (near_ref, direct_ref, via_ref):
        n = ref.shape[0]
        if ref is via_ref:
            n -= RTILE
        ref[:n, :HEAD_DIM] = (dk_scr[at : at + n, :] * SCALING).astype(BF16)
        ref[:n, HEAD_DIM:] = dv_scr[at : at + n, :].astype(BF16)
        at += n
    drk_ref[...] = (dk_scr[n_prompt:, :] * SCALING).astype(BF16)
    drv_ref[...] = dv_scr[n_prompt:, :].astype(BF16)
    lanes = 2 * HEAD_DIM
    pieces = [sum_scr[:, j * lanes : (j + 1) * lanes] for j in range(heads // 2)]
    hot = (lax.broadcasted_iota(jnp.int32, (1, lanes), 1) == id_ref[0]).astype(F32)
    tile = jnp.concatenate(
        pieces + [hot, jnp.zeros((RTILE - heads // 2 - 1, lanes), F32)], axis=0
    ).astype(BF16)
    r_ref[...] = tile
    via_ref[via_ref.shape[0] - RTILE :, :] = tile


def attention(pref_ids, resp_len, queries, out_grad, table, resp_keys, resp_values, blocks):
    rows = queries.shape[0]
    block = blocks[0].shape[0] // 2
    n_prompt = sum(b.shape[0] for b in blocks)
    n_keys = n_prompt + rows
    far_rows = n_prompt // 2 - block
    width = HEADS_PER_STEP * rows
    lanes = 2 * HEAD_DIM
    shape = jax.ShapeDtypeStruct
    return pl.pallas_call(
        functools.partial(attention_kernel, len(blocks)),
        out_shape=[
            shape(queries.shape, BF16),
            shape(resp_keys.shape, BF16),
            shape(resp_keys.shape, BF16),
            shape((2 * block, lanes), BF16),
            shape((far_rows, lanes), BF16),
            shape((far_rows + RTILE, lanes), BF16),
            shape((RTILE, lanes), BF16),
        ],
        in_specs=[SMEM, SMEM] + [VMEM] * (5 + len(blocks)),
        out_specs=[VMEM] * 7,
        scratch_shapes=[
            pltpu.VMEM((n_keys, HEAD_DIM), BF16),
            pltpu.VMEM((n_keys, HEAD_DIM), BF16),
            pltpu.VMEM((HEAD_DIM, n_keys), BF16),
            pltpu.VMEM((n_keys, width), F32),
            pltpu.VMEM((n_keys, width), F32),
            pltpu.VMEM((n_keys, HEAD_DIM), F32),
            pltpu.VMEM((n_keys, HEAD_DIM), F32),
            pltpu.VMEM((1, queries.shape[1]), F32),
            pltpu.VMEM((1, queries.shape[1]), F32),
        ],
        compiler_params=pltpu.CompilerParams(vmem_limit_bytes=32 * 1024 * 1024),
        name="attention",
    )(pref_ids, resp_len, queries, out_grad, table, resp_keys, resp_values, *blocks)


def pair_sum_kernel(direct_ref, got_ref, r_ref, *out_refs):
    mate = got_ref[direct_ref.shape[0] :, :]
    at = 0
    for i, out in enumerate(out_refs):
        tiles = 1 if i == len(out_refs) - 1 else 2
        n = out.shape[0] - tiles * RTILE
        out[:n, :] = (
            direct_ref[at : at + n, :].astype(F32) + got_ref[at : at + n, :].astype(F32)
        ).astype(BF16)
        out[n : n + RTILE, :] = r_ref[...]
        if tiles == 2:
            out[n + RTILE :, :] = mate
        at += n


def pair_sum(direct, got, r_tile, block, near_count):
    lanes = direct.shape[1]
    shapes = [(2 * block + 2 * RTILE, lanes)] * near_count + [(block + RTILE, lanes)]
    return pl.pallas_call(
        pair_sum_kernel,
        out_shape=[jax.ShapeDtypeStruct(s, BF16) for s in shapes],
        in_specs=[VMEM] * 3,
        out_specs=[VMEM] * len(shapes),
        name="pair_sum",
    )(direct, got, r_tile)


def chip_sum_kernel(near_ref, *refs):
    block = near_ref.shape[0] // 2
    *got_refs, far_ref, mine_ref, other_ref = refs
    mine = near_ref[:block, :].astype(F32) + far_ref[:block, :].astype(F32)
    other = near_ref[block:, :].astype(F32)
    at = block
    for got in got_refs:
        mine = mine + got[:block, :].astype(F32)
        other = other + got[block : 2 * block, :].astype(F32)
        other_ref[at : at + 2 * RTILE, :] = got[2 * block :, :]
        at += 2 * RTILE
    other_ref[at:, :] = far_ref[block:, :]
    mine_ref[...] = mine
    other_ref[:block, :] = other.astype(BF16)


def chip_sum(near, gots, far):
    block, lanes = near.shape[0] // 2, near.shape[1]
    tiles = 2 * len(gots) + 1
    return pl.pallas_call(
        chip_sum_kernel,
        out_shape=[
            jax.ShapeDtypeStruct((block, lanes), F32),
            jax.ShapeDtypeStruct((block + tiles * RTILE, lanes), BF16),
        ],
        in_specs=[VMEM] * (len(gots) + 2),
        out_specs=[VMEM] * 2,
        name="chip_sum",
    )(near, *gots, far)


def last_sum_kernel(mine_ref, sent_ref, got_ref, r_ref, mate_ref, dk_ref, dv_ref, pref_ref):
    block = mine_ref.shape[0]
    total = mine_ref[...] + got_ref[:block, :].astype(F32)
    dk_ref[...] = total[:, :HEAD_DIM].astype(BF16)
    dv_ref[...] = total[:, HEAD_DIM:].astype(BF16)
    n_pref, columns = pref_ref.shape
    lanes = mine_ref.shape[1]
    tiles = [r_ref[...], mate_ref[...]]
    for ref in (sent_ref, got_ref):
        for at in range(block, ref.shape[0], RTILE):
            tiles.append(ref[at : at + RTILE, :])
    tiles = [t.astype(F32) for t in tiles]
    count = columns // lanes
    hot = jnp.concatenate([t[count : count + 1, :n_pref] for t in tiles], axis=0)
    hot = hot.astype(BF16)
    for j in range(count):
        sums = jnp.concatenate([t[j : j + 1, :] for t in tiles], axis=0).astype(BF16)
        pref_ref[:, j * lanes : (j + 1) * lanes] = lax.dot_general(
            hot, sums, (((0,), (0,)), ((), ())), preferred_element_type=F32
        )


def last_sum(mine, sent, got, r_tile, mate_tile, n_pref, columns):
    block = mine.shape[0]
    return pl.pallas_call(
        last_sum_kernel,
        out_shape=[
            jax.ShapeDtypeStruct((block, HEAD_DIM), BF16),
            jax.ShapeDtypeStruct((block, HEAD_DIM), BF16),
            jax.ShapeDtypeStruct((n_pref, columns), F32),
        ],
        in_specs=[VMEM] * 5,
        out_specs=[VMEM] * 3,
        name="last_sum",
    )(mine, sent, got, r_tile, mate_tile)


def shards(
    n_resp,
    queries,
    resp_keys,
    resp_values,
    prompt_keys,
    prompt_values,
    out_grad,
    pref_table,
    pref_ids,
    resp_len,
):
    pair, far, out, back = ring_moves(n_resp)

    def move(array, moves):
        return lax.ppermute(array, "resp", moves)

    block = prompt_keys.shape[0]
    own = jnp.concatenate([prompt_keys, prompt_values], axis=1)
    far_direct = move(own, far)
    chip = jnp.concatenate([own, move(own, pair)], axis=0)
    direct = [move(chip, moves) for moves in out] + [far_direct]
    via = [move(piece, pair) for piece in direct]
    query_grad, resp_key_grad, resp_value_grad, near, direct_sum, via_sum, r_tile = attention(
        pref_ids,
        resp_len,
        queries,
        out_grad,
        pref_table,
        resp_keys,
        resp_values,
        [chip] + direct + via,
    )
    got = move(via_sum, pair)
    *near_sums, far_sum = pair_sum(direct_sum, got, r_tile, block, len(out))
    far_got = move(far_sum, far)
    gots = [move(piece, moves) for piece, moves in zip(near_sums, back)]
    mine, sent = chip_sum(near, gots, far_got)
    last = move(sent, pair)
    prompt_key_grad, prompt_value_grad, pref_grad = last_sum(
        mine, sent, last, r_tile, got[-RTILE:], pref_table.shape[0], queries.shape[1]
    )
    return (
        query_grad,
        resp_key_grad,
        resp_value_grad,
        prompt_key_grad,
        prompt_value_grad,
        pref_grad,
    )


def solution(mesh):
    rows = P(("dp", "resp"), "tensor")
    in_specs = (rows,) * 6 + (P(None, "tensor"), P(("dp", "resp")), P(("dp", "resp")))
    out_specs = (rows,) * 5 + (P("dp", "tensor"),)
    return jax.shard_map(
        functools.partial(shards, mesh.shape["resp"]),
        mesh=mesh,
        in_specs=in_specs,
        out_specs=out_specs,
        check_vma=False,
    )
```

time: 189 us -> 79 us (0.42); the launches traced: 186 us -> 78.2 us
  blocking collectives: 84 us -> 0 us
  matrix products: 53.2 us -> 0 us
  Pallas kernels: 0 us -> 25.2 us
  starting transfers between devices: 0.04 us -> 24.4 us
  other arithmetic: 14.5 us -> 0.01 us
  waiting for transfers between devices: 4.49 us -> 18.2 us
  between operations: 15.6 us -> 2.07 us
  local copies, waits for them, and re-layouts: 13.4 us -> 8.29 us
    dot_general x24 -> x0, matrix products: 53.2 us -> none  [the longest x4 13 us: pair_step(): jnp.dot(low_weights.T, grad_rows, preferred_element_type=jnp.float32)]
    psum x1 -> x0, blocking collectives: 43.9 us -> none  [shards(): lax.psum((chosen[:, None] * row_sums[None, :]).astype(jnp.bfloat16), 'resp')]
    all_gather x2 -> x0, blocking collectives: 40 us -> none  [the longest x1 22.8 us: shards(): lax.all_gather(prompt_keys, 'resp', axis=0, tiled=True)]
    pallas_call x0 -> x4, Pallas kernels: none -> 25.2 us  [the longest x1 19.5 us: attention(): pl.pallas_call(functools.partial(attention_kernel, len(blocks)), out_shap...]
    ppermute x0 -> x15, starting transfers between devices: none -> 24.4 us  [move(): return lax.ppermute(array, 'resp', moves)]
    ppermute x0 -> x15, waiting for transfers between devices: none -> 18.2 us  [move(): return lax.ppermute(array, 'resp', moves)]
    unnamed x10 -> x31, local copies, waits for them, and re-layouts: 0.03 us -> 6.99 us
    while x72 -> x0, local copies, waits for them, and re-layouts: 4.77 us -> none
  transfers between devices with their start and end apart: 1 -> 15, of which waited for: 1 -> 7; matrix products, arithmetic and copies ran while one was open for 3% -> 2% of each run, Pallas kernels for 0% -> 0%
where the time goes in v1:
time: 79 us; the launch traced here: 78.2 us
  Pallas kernels  25.2 us (32%)
  starting transfers between devices  24.4 us (31%)
  waiting for transfers between devices  18.2 us (23%)
  local copies, waits for them, and re-layouts  8.29 us (10%)
  between operations  2.07 us (3%)
    ppermute x15, starting transfers between devices, move(): return lax.ppermute(array, 'resp', moves)  24.4 us
    pallas_call x1, Pallas kernels, attention(): pl.pallas_call(functools.partial(attention_kernel, len(blocks)), out_shap...  19.5 us
    ppermute x15, waiting for transfers between devices, move(): return lax.ppermute(array, 'resp', moves)  18.2 us
    unnamed x31, local copies, waits for them, and re-layouts  6.99 us
    pallas_call x1, Pallas kernels, pair_sum(): pl.pallas_call(pair_sum_kernel, out_shape=[jax.ShapeDtypeStruct(s, BF16)...  1.98 us
    pallas_call x1, Pallas kernels, chip_sum(): pl.pallas_call(chip_sum_kernel, out_shape=[jax.ShapeDtypeStruct((block, l...  1.9 us
    pallas_call x1, Pallas kernels, last_sum(): pl.pallas_call(last_sum_kernel, out_shape=[jax.ShapeDtypeStruct((block, H...  1.85 us
  transfers between devices with their start and end apart: 15, of which 7 were waited for; matrix products, arithmetic and copies ran while one was open for 2% of the time, Pallas kernels for 0%

profile of v1, /device:TPU:1, one launch (start us, length us, event | category | flops | bytes accessed | tf_op | source)
XLA Modules:
  0.0 78.2 jit_solution(7089677522368816398)
XLA Ops:
  0.6 0.8 constant_dynamic-update-slice_fusion.1
  1.4 0.0 copy-start.4
  1.4 0.0 copy-start.5
  1.5 0.0 copy-start.6
  1.5 3.3 %collective-permute-start = (bf16[128,256]{1,0:T(8,128)(2,1)S(1)}, bf16[128,256]{1,0:T(8,128)(2,1)S(1)}, u32[]{:S(2)}, u32[]{:S(2)}) collective-permute-start(bf16[128,256]{1,0:T(8,128)(2,1)S(1)} %constant_dynamic-update-slice_fusion), channel_id=1, source_target_pairs={{0,8},{8,0},{16,24},{24,16},{32,40},{40,32},{48,56},{56,48},{64,72... | collective-permute-start | bytes 196616 | tf_op jit(solution)/shard_map/ppermute | solution.py:299
  4.8 0.9 %collective-permute-done = bf16[128,256]{1,0:T(8,128)(2,1)S(1)} collective-permute-done((bf16[128,256]{1,0:T(8,128)(2,1)S(1)}, bf16[128,256]{1,0:T(8,128)(2,1)S(1)}, u32[]{:S(2)}, u32[]{:S(2)}) %collective-permute-start) | collective-permute-done | bytes 65568 | tf_op jit(solution)/shard_map/ppermute | solution.py:299
  5.7 4.8 %collective-permute-start.3 = (bf16[256,256]{1,0:T(8,128)(2,1)S(1)}, bf16[256,256]{1,0:T(8,128)(2,1)S(1)}, u32[]{:S(2)}, u32[]{:S(2)}) collective-permute-start(bf16[256,256]{1,0:T(8,128)(2,1)S(1)} %pad_maximum_fusion.refs_0_), channel_id=1, source_target_pairs={{0,48},{8,88},{16,64},{24,104},{32,80},{40,120},{48,96},{56,8},{64... | collective-permute-start | bytes 393224 | tf_op jit(solution)/shard_map/ppermute | solution.py:299
  10.5 0.3 collective-permute-start.2
  10.8 0.5 collective-permute-start.1
  11.3 4.5 %collective-permute-start.4 = (bf16[128,256]{1,0:T(8,128)(2,1)S(1)}, bf16[128,256]{1,0:T(8,128)(2,1)S(1)}, u32[]{:S(2)}, u32[]{:S(2)}) collective-permute-start(bf16[128,256]{1,0:T(8,128)(2,1)S(1)} %constant_dynamic-update-slice_fusion), channel_id=1, source_target_pairs={{0,64},{8,72},{16,80},{24,88},{32,96},{40,104},{48,112},{56,120},{... | collective-permute-start | bytes 196616 | tf_op jit(solution)/shard_map/ppermute | solution.py:299
  15.7 0.5 collective-permute-done.3.refs_3_
  16.2 0.0 collective-permute-start.7
  16.2 2.5 %collective-permute-done.2.refs_2_ = bf16[256,256]{1,0:T(8,128)(2,1)S(1)} collective-permute-done((bf16[256,256]{1,0:T(8,128)(2,1)S(1)}, bf16[256,256]{1,0:T(8,128)(2,1)S(1)}, u32[]{:S(2)}, u32[]{:S(2)}) %collective-permute-start.2) | collective-permute-done | bytes 131104 | tf_op jit(solution)/shard_map/ppermute | solution.py:299
  18.8 1.6 %collective-permute-start.6 = (bf16[256,256]{1,0:T(8,128)(2,1)S(1)}, bf16[256,256]{1,0:T(8,128)(2,1)S(1)}, u32[]{:S(2)}, u32[]{:S(2)}) collective-permute-start(bf16[256,256]{1,0:T(8,128)(2,1)S(1)} %collective-permute-done.2.refs_2_), channel_id=1, source_target_pairs={{0,8},{8,0},{16,24},{24,16},{32,40},{40,32},{48,56},{56,48},{64,72... | collective-permute-start | bytes 393224 | tf_op jit(solution)/shard_map/ppermute | solution.py:299
  20.4 1.9 %collective-permute-done.1.refs_1_ = bf16[256,256]{1,0:T(8,128)(2,1)S(1)} collective-permute-done((bf16[256,256]{1,0:T(8,128)(2,1)S(1)}, bf16[256,256]{1,0:T(8,128)(2,1)S(1)}, u32[]{:S(2)}, u32[]{:S(2)}) %collective-permute-start.1) | collective-permute-done | bytes 131104 | tf_op jit(solution)/shard_map/ppermute | solution.py:299
  22.3 1.3 %collective-permute-start.5 = (bf16[256,256]{1,0:T(8,128)(2,1)S(1)}, bf16[256,256]{1,0:T(8,128)(2,1)S(1)}, u32[]{:S(2)}, u32[]{:S(2)}) collective-permute-start(bf16[256,256]{1,0:T(8,128)(2,1)S(1)} %collective-permute-done.1.refs_1_), channel_id=1, source_target_pairs={{0,8},{8,0},{16,24},{24,16},{32,40},{40,32},{48,56},{56,48},{64,72... | collective-permute-start | bytes 393224 | tf_op jit(solution)/shard_map/ppermute | solution.py:299
  23.5 0.0 collective-permute-done.4.refs_4_
  23.5 2.1 %collective-permute-start.8 = (bf16[128,256]{1,0:T(8,128)(2,1)S(1)}, bf16[128,256]{1,0:T(8,128)(2,1)S(1)}, u32[]{:S(2)}, u32[]{:S(2)}) collective-permute-start(bf16[128,256]{1,0:T(8,128)(2,1)S(1)} %collective-permute-done.4.refs_4_), channel_id=1, source_target_pairs={{0,8},{8,0},{16,24},{24,16},{32,40},{40,32},{48,56},{56,48},{64,72... | collective-permute-start | bytes 196616 | tf_op jit(solution)/shard_map/ppermute | solution.py:299
  26.9 0.0 collective-permute-done.8.refs_8_
  27.0 0.0 collective-permute-done.7.refs_7_
  27.0 0.0 collective-permute-done.6.refs_6_
  27.0 0.0 copy-start
  27.0 1.0 %copy-done = bf16[256,1024]{1,0:T(8,128)(2,1)S(1)} copy-done((bf16[256,1024]{1,0:T(8,128)(2,1)S(1)}, bf16[256,1024]{1,0:T(8,128)(2,1)}, u32[]{:S(2)}) %copy-start) | copy-done | bytes 524312
  28.1 1.0 %copy-done.1 = bf16[256,1024]{1,0:T(8,128)(2,1)S(1)} copy-done((bf16[256,1024]{1,0:T(8,128)(2,1)S(1)}, bf16[256,1024]{1,0:T(8,128)(2,1)}, u32[]{:S(2)}) %copy-start.1) | copy-done | bytes 524312
  29.1 19.5 %attention.1 = (bf16[256,1024]{1,0:T(8,128)(2,1)}, bf16[256,128]{1,0:T(8,128)(2,1)}, bf16[256,128]{1,0:T(8,128)(2,1)}, bf16[256,256]{1,0:T(8,128)(2,1)S(1)}, bf1...) custom-call(s32[1]{0:T(128)S(6)} %copy.16.id_ref, s32[1]{0:T(128)S(6)} %copy.17.len_ref, ...), custom_call_target="tpu_custom_call" | custom-call | tf_op jit(solution)/shard_map/attention/pallas_call | solution.py:160
  48.6 0.8 %copy-done.2 = bf16[896,256]{1,0:T(8,128)(2,1)} copy-done((bf16[896,256]{1,0:T(8,128)(2,1)}, bf16[896,256]{1,0:T(8,128)(2,1)S(1)}, u32[]{:S(2)}) %copy-start.2) | copy-done | bytes 458776
  49.4 0.7 copy-done.3
  50.0 0.6 copy-done.7
  50.6 0.0 collective-permute-start.9
  50.6 1.8 %collective-permute-done.9.got_ref = bf16[912,256]{1,0:T(8,128)(2,1)S(1)} collective-permute-done((bf16[912,256]{1,0:T(8,128)(2,1)S(1)}, bf16[912,256]{1,0:T(8,128)(2,1)S(1)}, u32[]{:S(2)}, u32[]{:S(2)}) %collective-permute-start.9) | collective-permute-done | bytes 466976 | tf_op jit(solution)/shard_map/ppermute | solution.py:299
  52.5 0.8 copy-done.8
  53.2 2.0 %pair_sum.1 = (bf16[288,256]{1,0:T(8,128)(2,1)}, bf16[288,256]{1,0:T(8,128)(2,1)}, bf16[288,256]{1,0:T(8,128)(2,1)}, bf16[144,256]{1,0:T(8,128)(2,1)}) custom-call(bf16[896,256]{1,0:T(8,128)(2,1)} %copy-done.2, bf16[912,256]{1,0:T(8,128)(2,1)} %copy-done.8, bf16[16,256]{1,0:T(8,128)(2,1)} %copy-done.7), custom_call_target="tpu_custom_call" | custom-call | tf_op jit(solution)/shard_map/pair_sum/pallas_call | solution.py:207
  55.2 0.0 collective-permute-start.10
  55.2 0.6 collective-permute-start.11
  55.8 3.8 %collective-permute-start.12 = (bf16[288,256]{1,0:T(8,128)(2,1)}, bf16[288,256]{1,0:T(8,128)(2,1)S(1)}, u32[]{:S(2)}, u32[]{:S(2)}) collective-permute-start(bf16[288,256]{1,0:T(8,128)(2,1)} %get-tuple-element.31), channel_id=1, source_target_pairs={{48,0},{88,8},{64,16},{104,24},{80,32},{120,40},{96,48},{8,56},{11... | collective-permute-start | bytes 442376 | tf_op jit(solution)/shard_map/ppermute | solution.py:299
  59.6 1.2 %collective-permute-start.13 = (bf16[144,256]{1,0:T(8,128)(2,1)}, bf16[144,256]{1,0:T(8,128)(2,1)S(1)}, u32[]{:S(2)}, u32[]{:S(2)}) collective-permute-start(bf16[144,256]{1,0:T(8,128)(2,1)} %get-tuple-element.32), channel_id=1, source_target_pairs={{0,64},{8,72},{16,80},{24,88},{32,96},{40,104},{48,112},{56,120},{... | collective-permute-start | bytes 221192 | tf_op jit(solution)/shard_map/ppermute | solution.py:299
  60.9 10.4 %collective-permute-done.13.refs_3_ = bf16[144,256]{1,0:T(8,128)(2,1)S(1)} collective-permute-done((bf16[144,256]{1,0:T(8,128)(2,1)}, bf16[144,256]{1,0:T(8,128)(2,1)S(1)}, u32[]{:S(2)}, u32[]{:S(2)}) %collective-permute-start.13) | collective-permute-done | bytes 73760 | tf_op jit(solution)/shard_map/ppermute | solution.py:299
  71.3 0.0 collective-permute-done.10.refs_0_
  71.3 0.1 collective-permute-done.12.refs_2_
  71.5 0.5 copy-done.13
  71.9 0.1 copy-done.9
  72.0 0.1 copy-done.10
  72.1 0.1 copy-done.11
  72.1 1.9 %chip_sum.1 = (f32[128,256]{1,0:T(8,128)}, bf16[240,256]{1,0:T(8,128)(2,1)}) custom-call(bf16[256,256]{1,0:T(8,128)(2,1)} %copy-done.3, bf16[288,256]{1,0:T(8,128)(2,1)} %copy-done.9, bf16[288,256]{1,0:T(8,128)(2,1)} %copy-done.10, bf16[288,256]{1,0:T(8,128)(2,1)} %copy-done.11, bf16[144,256]{1,0:T(8,128)(2,1)} %copy-done.13), custom_call_target="tpu_custom_call" | custom-call | tf_op jit(solution)/shard_map/chip_sum/pallas_call | solution.py:235
  74.0 0.4 collective-permute-start.14
  74.4 1.3 %slice.4.mate_ref = bf16[16,256]{1,0:T(8,128)(2,1)} slice(bf16[912,256]{1,0:T(8,128)(2,1)} %copy-done.8), slice={[896:912], [0:256]} | slice | bytes 16384 | tf_op jit(solution)/shard_map/slice | solution.py:324
  75.7 0.7 copy-done.12
  76.4 1.9 %last_sum.1 = (bf16[128,128]{1,0:T(8,128)(2,1)}, bf16[128,128]{1,0:T(8,128)(2,1)}, f32[16,1024]{1,0:T(8,128)}) custom-call(f32[128,256]{1,0:T(8,128)} %get-tuple-element.33.mine_ref, bf16[240,256]{1,0:T(8,128)(2,1)} %get-tuple-element.34.sent_ref, bf16[240,256]{1,0:T(8,128)(2,1)} %copy-done.12, bf16[16,256]{1,0:T(8,128)(2,1)} %copy-done.7, ...), custom_call_target="tpu_custom_call" | custom-call | tf_op jit(solution)/shard_map/last_sum/pallas_call | solution.py:271
  (20 shorter events, 0.1 us)
Async XLA Ops:
  0.6 0.8 %copy-start.14 = (bf16[128,128]{1,0:T(8,128)(2,1)S(1)}, bf16[128,128]{1,0:T(8,128)(2,1)}, u32[]{:S(2)}) copy-start(bf16[128,128]{1,0:T(8,128)(2,1)} %param.13) | copy-start | bytes 98308
  1.4 25.6 %copy-start.4 = (bf16[256,128]{1,0:T(8,128)(2,1)S(1)}, bf16[256,128]{1,0:T(8,128)(2,1)}, u32[]{:S(2)}) copy-start(bf16[256,128]{1,0:T(8,128)(2,1)} %rk_ref.1) | copy-start | bytes 196612
  1.4 25.5 %copy-start.5 = (bf16[256,128]{1,0:T(8,128)(2,1)S(1)}, bf16[256,128]{1,0:T(8,128)(2,1)}, u32[]{:S(2)}) copy-start(bf16[256,128]{1,0:T(8,128)(2,1)} %rv_ref.1) | copy-start | bytes 196612
  1.5 25.5 %copy-start.6 = (bf16[16,1024]{1,0:T(8,128)(2,1)S(1)}, bf16[16,1024]{1,0:T(8,128)(2,1)}, u32[]{:S(2)}) copy-start(bf16[16,1024]{1,0:T(8,128)(2,1)} %table_ref.1) | copy-start | bytes 98308
  1.5 4.2 %collective-permute-start = (bf16[128,256]{1,0:T(8,128)(2,1)S(1)}, bf16[128,256]{1,0:T(8,128)(2,1)S(1)}, u32[]{:S(2)}, u32[]{:S(2)}) collective-permute-start(bf16[128,256]{1,0:T(8,128)(2,1)S(1)} %constant_dynamic-update-slice_fusion), channel_id=1, source_target_pairs={{0,8},{8,0},{16,24},{24,16},{32,40},{40,32},{48,56},{56,48},{64,72... | collective-permute-start | bytes 196616 | tf_op jit(solution)/shard_map/ppermute | solution.py:299
  5.7 10.5 %collective-permute-start.3 = (bf16[256,256]{1,0:T(8,128)(2,1)S(1)}, bf16[256,256]{1,0:T(8,128)(2,1)S(1)}, u32[]{:S(2)}, u32[]{:S(2)}) collective-permute-start(bf16[256,256]{1,0:T(8,128)(2,1)S(1)} %pad_maximum_fusion.refs_0_), channel_id=1, source_target_pairs={{0,48},{8,88},{16,64},{24,104},{32,80},{40,120},{48,96},{56,8},{64... | collective-permute-start | bytes 393224 | tf_op jit(solution)/shard_map/ppermute | solution.py:299
  10.5 8.2 %collective-permute-start.2 = (bf16[256,256]{1,0:T(8,128)(2,1)S(1)}, bf16[256,256]{1,0:T(8,128)(2,1)S(1)}, u32[]{:S(2)}, u32[]{:S(2)}) collective-permute-start(bf16[256,256]{1,0:T(8,128)(2,1)S(1)} %pad_maximum_fusion.refs_0_), channel_id=1, source_target_pairs={{0,32},{8,104},{16,48},{24,120},{32,64},{40,8},{48,80},{56,24},{64... | collective-permute-start | bytes 393224 | tf_op jit(solution)/shard_map/ppermute | solution.py:299
  10.8 11.5 %collective-permute-start.1 = (bf16[256,256]{1,0:T(8,128)(2,1)S(1)}, bf16[256,256]{1,0:T(8,128)(2,1)S(1)}, u32[]{:S(2)}, u32[]{:S(2)}) collective-permute-start(bf16[256,256]{1,0:T(8,128)(2,1)S(1)} %pad_maximum_fusion.refs_0_), channel_id=1, source_target_pairs={{0,16},{8,120},{16,32},{24,8},{32,48},{40,24},{48,64},{56,40},{64,... | collective-permute-start | bytes 393224 | tf_op jit(solution)/shard_map/ppermute | solution.py:299
  11.3 12.3 %collective-permute-start.4 = (bf16[128,256]{1,0:T(8,128)(2,1)S(1)}, bf16[128,256]{1,0:T(8,128)(2,1)S(1)}, u32[]{:S(2)}, u32[]{:S(2)}) collective-permute-start(bf16[128,256]{1,0:T(8,128)(2,1)S(1)} %constant_dynamic-update-slice_fusion), channel_id=1, source_target_pairs={{0,64},{8,72},{16,80},{24,88},{32,96},{40,104},{48,112},{56,120},{... | collective-permute-start | bytes 196616 | tf_op jit(solution)/shard_map/ppermute | solution.py:299
  16.2 10.8 %collective-permute-start.7 = (bf16[256,256]{1,0:T(8,128)(2,1)S(1)}, bf16[256,256]{1,0:T(8,128)(2,1)S(1)}, u32[]{:S(2)}, u32[]{:S(2)}) collective-permute-start(bf16[256,256]{1,0:T(8,128)(2,1)S(1)} %collective-permute-done.3.refs_3_), channel_id=1, source_target_pairs={{0,8},{8,0},{16,24},{24,16},{32,40},{40,32},{48,56},{56,48},{64,72... | collective-permute-start | bytes 393224 | tf_op jit(solution)/shard_map/ppermute | solution.py:299
  18.8 8.2 %collective-permute-start.6 = (bf16[256,256]{1,0:T(8,128)(2,1)S(1)}, bf16[256,256]{1,0:T(8,128)(2,1)S(1)}, u32[]{:S(2)}, u32[]{:S(2)}) collective-permute-start(bf16[256,256]{1,0:T(8,128)(2,1)S(1)} %collective-permute-done.2.refs_2_), channel_id=1, source_target_pairs={{0,8},{8,0},{16,24},{24,16},{32,40},{40,32},{48,56},{56,48},{64,72... | collective-permute-start | bytes 393224 | tf_op jit(solution)/shard_map/ppermute | solution.py:299
  22.3 4.7 %collective-permute-start.5 = (bf16[256,256]{1,0:T(8,128)(2,1)S(1)}, bf16[256,256]{1,0:T(8,128)(2,1)S(1)}, u32[]{:S(2)}, u32[]{:S(2)}) collective-permute-start(bf16[256,256]{1,0:T(8,128)(2,1)S(1)} %collective-permute-done.1.refs_1_), channel_id=1, source_target_pairs={{0,8},{8,0},{16,24},{24,16},{32,40},{40,32},{48,56},{56,48},{64,72... | collective-permute-start | bytes 393224 | tf_op jit(solution)/shard_map/ppermute | solution.py:299
  23.5 3.4 %collective-permute-start.8 = (bf16[128,256]{1,0:T(8,128)(2,1)S(1)}, bf16[128,256]{1,0:T(8,128)(2,1)S(1)}, u32[]{:S(2)}, u32[]{:S(2)}) collective-permute-start(bf16[128,256]{1,0:T(8,128)(2,1)S(1)} %collective-permute-done.4.refs_4_), channel_id=1, source_target_pairs={{0,8},{8,0},{16,24},{24,16},{32,40},{40,32},{48,56},{56,48},{64,72... | collective-permute-start | bytes 196616 | tf_op jit(solution)/shard_map/ppermute | solution.py:299
  27.0 1.0 %copy-start = (bf16[256,1024]{1,0:T(8,128)(2,1)S(1)}, bf16[256,1024]{1,0:T(8,128)(2,1)}, u32[]{:S(2)}) copy-start(bf16[256,1024]{1,0:T(8,128)(2,1)} %q_ref.1) | copy-start | bytes 1572868
  28.1 1.0 %copy-start.1 = (bf16[256,1024]{1,0:T(8,128)(2,1)S(1)}, bf16[256,1024]{1,0:T(8,128)(2,1)}, u32[]{:S(2)}) copy-start(bf16[256,1024]{1,0:T(8,128)(2,1)} %g_ref.1) | copy-start | bytes 1572868
  48.6 0.8 %copy-start.2 = (bf16[896,256]{1,0:T(8,128)(2,1)}, bf16[896,256]{1,0:T(8,128)(2,1)S(1)}, u32[]{:S(2)}) copy-start(bf16[896,256]{1,0:T(8,128)(2,1)S(1)} %get-tuple-element.26.direct_ref) | copy-start | bytes 1376260
  49.4 0.7 copy-start.3
  50.0 0.6 copy-start.7
  50.6 1.8 %collective-permute-start.9 = (bf16[912,256]{1,0:T(8,128)(2,1)S(1)}, bf16[912,256]{1,0:T(8,128)(2,1)S(1)}, u32[]{:S(2)}, u32[]{:S(2)}) collective-permute-start(bf16[912,256]{1,0:T(8,128)(2,1)S(1)} %get-tuple-element.27), channel_id=1, source_target_pairs={{0,8},{8,0},{16,24},{24,16},{32,40},{40,32},{48,56},{56,48},{64,72... | collective-permute-start | bytes 1400840 | tf_op jit(solution)/shard_map/ppermute | solution.py:299
  52.5 0.8 copy-start.8
  55.2 16.1 %collective-permute-start.10 = (bf16[288,256]{1,0:T(8,128)(2,1)}, bf16[288,256]{1,0:T(8,128)(2,1)S(1)}, u32[]{:S(2)}, u32[]{:S(2)}) collective-permute-start(bf16[288,256]{1,0:T(8,128)(2,1)} %get-tuple-element.29), channel_id=1, source_target_pairs={{16,0},{120,8},{32,16},{8,24},{48,32},{24,40},{64,48},{40,56},{80,... | collective-permute-start | bytes 442376 | tf_op jit(solution)/shard_map/ppermute | solution.py:299
  55.2 16.1 %collective-permute-start.11 = (bf16[288,256]{1,0:T(8,128)(2,1)}, bf16[288,256]{1,0:T(8,128)(2,1)S(1)}, u32[]{:S(2)}, u32[]{:S(2)}) collective-permute-start(bf16[288,256]{1,0:T(8,128)(2,1)} %get-tuple-element.30), channel_id=1, source_target_pairs={{32,0},{104,8},{48,16},{120,24},{64,32},{8,40},{80,48},{24,56},{96... | collective-permute-start | bytes 442376 | tf_op jit(solution)/shard_map/ppermute | solution.py:299
  55.8 15.7 %collective-permute-start.12 = (bf16[288,256]{1,0:T(8,128)(2,1)}, bf16[288,256]{1,0:T(8,128)(2,1)S(1)}, u32[]{:S(2)}, u32[]{:S(2)}) collective-permute-start(bf16[288,256]{1,0:T(8,128)(2,1)} %get-tuple-element.31), channel_id=1, source_target_pairs={{48,0},{88,8},{64,16},{104,24},{80,32},{120,40},{96,48},{8,56},{11... | collective-permute-start | bytes 442376 | tf_op jit(solution)/shard_map/ppermute | solution.py:299
  59.6 11.7 %collective-permute-start.13 = (bf16[144,256]{1,0:T(8,128)(2,1)}, bf16[144,256]{1,0:T(8,128)(2,1)S(1)}, u32[]{:S(2)}, u32[]{:S(2)}) collective-permute-start(bf16[144,256]{1,0:T(8,128)(2,1)} %get-tuple-element.32), channel_id=1, source_target_pairs={{0,64},{8,72},{16,80},{24,88},{32,96},{40,104},{48,112},{56,120},{... | collective-permute-start | bytes 221192 | tf_op jit(solution)/shard_map/ppermute | solution.py:299
  71.3 0.6 copy-start.13
  71.3 0.7 copy-start.9
  71.3 0.7 copy-start.10
  71.5 0.7 copy-start.11
  74.0 1.7 %collective-permute-start.14 = (bf16[240,256]{1,0:T(8,128)(2,1)}, bf16[240,256]{1,0:T(8,128)(2,1)S(1)}, u32[]{:S(2)}, u32[]{:S(2)}) collective-permute-start(bf16[240,256]{1,0:T(8,128)(2,1)} %get-tuple-element.34.sent_ref), channel_id=1, source_target_pairs={{0,8},{8,0},{16,24},{24,16},{32,40},{40,32},{48,56},{56,48},{64,72... | collective-permute-start | bytes 368648 | tf_op jit(solution)/shard_map/ppermute | solution.py:299
  75.7 0.7 copy-start.12

commit v2 on v0

v2 whole, which is shorter than its diff:
```python
import functools

import jax
import jax.numpy as jnp
from jax import lax
from jax.experimental import pallas as pl
from jax.experimental.pallas import tpu as pltpu
from jax.sharding import PartitionSpec as P

F32 = jnp.float32
BF16 = jnp.bfloat16
HEAD_DIM = 128
SCALING = HEAD_DIM**-0.5
LOG2E = 1.4426950408889634
HEADS_PER_STEP = 2
CHUNK = 256
RTILE = 16
NT = (((1,), (1,)), ((), ()))
NN = (((1,), (0,)), ((), ()))
VMEM = pl.BlockSpec(memory_space=pltpu.VMEM)
SMEM = pl.BlockSpec(memory_space=pltpu.SMEM)
ANY = pl.BlockSpec(memory_space=pltpu.HBM)
SMALL = pltpu.CompilerParams(vmem_limit_bytes=8 * 1024 * 1024)


def ring_moves(n_resp):
    chips = n_resp // 2
    places = [(chip, core) for chip in range(chips) for core in range(2)]

    def along(step):
        return [
            (z * 2 + c, (z + step if c == 0 else z - step) % chips * 2 + c) for z, c in places
        ]

    pair = [(z * 2 + c, z * 2 + 1 - c) for z, c in places]
    return pair, along


def columns_of(ref, group):
    parts = []
    for i in range(HEADS_PER_STEP):
        at = (group * HEADS_PER_STEP + i) * HEAD_DIM
        parts.append(ref[:, at : at + HEAD_DIM])
    return jnp.concatenate(parts, axis=0)


def scores_kernel(n_blocks, has_resp, q_ref, g_ref, *refs):
    block_refs = refs[:n_blocks]
    resp_refs = refs[n_blocks : n_blocks + 2 * has_resp]
    low_ref, dp_ref, stat_ref, keys_t_ref, *score_refs = refs[n_blocks + 2 * has_resp :]
    rows = q_ref.shape[0]
    width = HEADS_PER_STEP * rows
    factor = SCALING * LOG2E
    pieces = []
    at = 0
    for ref in block_refs:
        n = ref.shape[0]
        pieces.append((at, n, ref.at[:, :HEAD_DIM], ref.at[:, HEAD_DIM:], False))
        at += n
    if has_resp:
        pieces.append((at, rows, resp_refs[0], resp_refs[1], True))
    for at, n, key_ref, _, _ in pieces:
        keys_t_ref[:, at : at + n] = key_ref[...].T
    for group in range(q_ref.shape[1] // (HEADS_PER_STEP * HEAD_DIM)):
        s_scr = score_refs[group % 2]
        cols = slice(group * width, (group + 1) * width)
        q = columns_of(q_ref, group)
        g = columns_of(g_ref, group)
        top = jnp.full((8, width), -1e30, F32)
        for at, n, key_ref, _, is_resp in pieces:
            s = lax.dot_general(key_ref[...], q, NT, preferred_element_type=F32)
            if is_resp:
                key_pos = lax.broadcasted_iota(jnp.int32, (n, width), 0)
                query_pos = lax.broadcasted_iota(jnp.int32, (n, width), 1) % rows
                s = jnp.where(key_pos <= query_pos, s, -1e30)
            s_scr[at : at + n, :] = s
            top = jnp.maximum(top, jnp.max(s.reshape(n // 8, 8, width), axis=0))
        row_max = jnp.max(top, axis=0, keepdims=True) * factor
        total = jnp.zeros((8, width), F32)
        dot = jnp.zeros((8, width), F32)
        for at, n, _, value_ref, _ in pieces:
            p = jnp.exp2(s_scr[at : at + n, :] * factor - row_max)
            dp = lax.dot_general(value_ref[...], g, NT, preferred_element_type=F32)
            total = total + jnp.sum(p.reshape(n // 8, 8, width), axis=0)
            dot = dot + jnp.sum((p * dp).reshape(n // 8, 8, width), axis=0)
            low_ref[at : at + n, cols] = p.astype(BF16)
            dp_ref[at : at + n, cols] = dp
        stat_ref[0:1, cols] = row_max
        stat_ref[1:2, cols] = jnp.sum(total, axis=0, keepdims=True)
        stat_ref[2:3, cols] = jnp.sum(dot, axis=0, keepdims=True)


def scores(biased, masked, blocks, resp=()):
    rows, columns = biased.shape
    n = sum(b.shape[0] for b in blocks) + (rows if resp else 0)
    queries = rows * columns // HEAD_DIM
    shape = jax.ShapeDtypeStruct
    return pl.pallas_call(
        functools.partial(scores_kernel, len(blocks), bool(resp)),
        out_shape=[
            shape((n, queries), BF16),
            shape((n, queries), F32),
            shape((8, queries), F32),
            shape((HEAD_DIM, n), BF16),
        ],
        in_specs=[VMEM] * (2 + len(blocks) + len(resp)),
        out_specs=[VMEM] * 4,
        scratch_shapes=[pltpu.VMEM((n, HEADS_PER_STEP * rows), F32)] * 2,
        compiler_params=SMALL,
        cost_estimate=pl.CostEstimate(
            flops=4 * n * queries * HEAD_DIM, bytes_accessed=0, transcendentals=n * queries
        ),
        name="scores",
    )(biased, masked, *blocks, *resp)


def query_kernel(count, id_ref, *refs):
    low_refs = refs[:count]
    dp_refs = refs[count : 2 * count]
    stat_refs = refs[2 * count : 3 * count]
    key_refs = refs[3 * count : 4 * count]
    ds_refs = refs[4 * count : 5 * count]
    dq_ref, scale_ref, r_ref, sum_scr, delta_scr = refs[5 * count :]
    rows, columns = dq_ref.shape
    width = HEADS_PER_STEP * rows
    top = stat_refs[0][0:1, :]
    for ref in stat_refs[1:]:
        top = jnp.maximum(top, ref[0:1, :])
    total = dot = 0.0
    for i, ref in enumerate(stat_refs):
        shift = jnp.exp2(ref[0:1, :] - top)
        scale_ref[i : i + 1, :] = shift
        total = total + ref[1:2, :] * shift
        dot = dot + ref[2:3, :] * shift
    inverse = 1.0 / total
    delta_scr[...] = dot * inverse
    for i in range(count):
        scale_ref[i : i + 1, :] = scale_ref[i : i + 1, :] * inverse
    for group in range(columns // (HEADS_PER_STEP * HEAD_DIM)):
        cols = slice(group * width, (group + 1) * width)
        delta = delta_scr[:, cols]
        dq = jnp.zeros((HEAD_DIM, width), F32)
        for i in range(count):
            ds = low_refs[i][:, cols] * (dp_refs[i][:, cols] - delta).astype(BF16)
            ds_refs[i][:, cols] = ds
            part = lax.dot_general(key_refs[i][...], ds, NN, preferred_element_type=F32)
            dq = dq + part * scale_ref[i : i + 1, cols]
        dq = dq.T * SCALING
        for i in range(HEADS_PER_STEP):
            at = (group * HEADS_PER_STEP + i) * HEAD_DIM
            part = dq[i * rows : (i + 1) * rows]
            dq_ref[:, at : at + HEAD_DIM] = part.astype(BF16)
            sum_scr[:, at : at + HEAD_DIM] = jnp.sum(part, axis=0, keepdims=True)
    lanes = 2 * HEAD_DIM
    pieces = [sum_scr[:, j * lanes : (j + 1) * lanes] for j in range(columns // lanes)]
    hot = (lax.broadcasted_iota(jnp.int32, (1, lanes), 1) == id_ref[0]).astype(F32)
    blank = jnp.zeros((RTILE - columns // lanes - 1, lanes), F32)
    r_ref[...] = jnp.concatenate(pieces + [hot, blank], axis=0).astype(BF16)


def query_side(pref_ids, lows, dps, stats, keys_t, rows, columns):
    count = len(lows)
    queries = lows[0].shape[1]
    shape = jax.ShapeDtypeStruct
    keys = sum(low.shape[0] for low in lows)
    return pl.pallas_call(
        functools.partial(query_kernel, count),
        out_shape=[shape(low.shape, BF16) for low in lows]
        + [
            shape((rows, columns), BF16),
            shape((8, queries), F32),
            shape((RTILE, 2 * HEAD_DIM), BF16),
        ],
        in_specs=[SMEM] + [VMEM] * (4 * count),
        out_specs=[VMEM] * (count + 3),
        scratch_shapes=[pltpu.VMEM((1, columns), F32), pltpu.VMEM((1, queries), F32)],
        compiler_params=SMALL,
        cost_estimate=pl.CostEstimate(
            flops=2 * keys * queries * HEAD_DIM, bytes_accessed=0, transcendentals=0
        ),
        name="query_side",
    )(pref_ids, *lows, *dps, *stats, *keys_t)


def key_kernel(picks, has_r, scale_ref, q_ref, g_ref, *refs):
    count = len(picks)
    ds_refs = refs[:count]
    low_refs = refs[count : 2 * count]
    r_refs = refs[2 * count : 2 * count + has_r]
    *out_refs, q_scr, g_scr = refs[2 * count + has_r :]
    rows = q_ref.shape[0]
    results = []
    for i, pick in enumerate(picks):
        for head in range(q_ref.shape[1] // HEAD_DIM):
            at = slice(head * rows, (head + 1) * rows)
            cols = slice(head * HEAD_DIM, (head + 1) * HEAD_DIM)
            scale = jnp.broadcast_to(scale_ref[pick : pick + 1, at], (HEAD_DIM, rows)).T
            q_scr[i, at, :] = (q_ref[:, cols].astype(F32) * scale).astype(BF16)
            g_scr[i, at, :] = (g_ref[:, cols].astype(F32) * scale).astype(BF16)
        dk = lax.dot_general(ds_refs[i][...], q_scr[i], NN, preferred_element_type=F32) * SCALING
        dv = lax.dot_general(low_refs[i][...], g_scr[i], NN, preferred_element_type=F32)
        results.append((dk.astype(BF16), dv.astype(BF16)))
    if has_r or count > 1:
        for ref, (dk, dv) in zip(out_refs, results):
            n = dk.shape[0]
            ref[:n, :HEAD_DIM] = dk
            ref[:n, HEAD_DIM:] = dv
        if has_r:
            out_refs[-1][n:, :] = r_refs[0][...]
    else:
        near_ref, drk_ref, drv_ref = out_refs
        n = near_ref.shape[0]
        dk, dv = results[0]
        near_ref[:, :HEAD_DIM] = dk[:n, :]
        near_ref[:, HEAD_DIM:] = dv[:n, :]
        drk_ref[...] = dk[n:, :]
        drv_ref[...] = dv[n:, :]


def key_side(picks, scale, biased, masked, ds, lows, r_tile=()):
    rows, columns = biased.shape
    queries = rows * columns // HEAD_DIM
    lanes = 2 * HEAD_DIM
    if len(picks) > 1:
        counts = [d.shape[0] for d in ds]
        counts[-1] += RTILE * len(r_tile)
        shapes = [(n, lanes) for n in counts]
    else:
        shapes = [(ds[0].shape[0] - rows, lanes), (rows, HEAD_DIM), (rows, HEAD_DIM)]
    keys = sum(d.shape[0] for d in ds)
    return pl.pallas_call(
        functools.partial(key_kernel, picks, len(r_tile)),
        out_shape=[jax.ShapeDtypeStruct(s, BF16) for s in shapes],
        in_specs=[VMEM] * (3 + 2 * len(picks) + len(r_tile)),
        out_specs=[VMEM] * len(shapes),
        scratch_shapes=[pltpu.VMEM((len(picks), queries, HEAD_DIM), BF16)] * 2,
        compiler_params=SMALL,
        cost_estimate=pl.CostEstimate(
            flops=4 * keys * queries * HEAD_DIM, bytes_accessed=0, transcendentals=0
        ),
        name="key_side",
    )(scale, biased, masked, *ds, *lows, *r_tile)


def pack_kernel(k_ref, v_ref, own_ref, sems):
    copies = [
        pltpu.make_async_copy(k_ref, own_ref.at[:, :HEAD_DIM], sems.at[0]),
        pltpu.make_async_copy(v_ref, own_ref.at[:, HEAD_DIM:], sems.at[1]),
    ]
    for copy in copies:
        copy.start()
    for copy in copies:
        copy.wait()


def pack(keys, values):
    return pl.pallas_call(
        pack_kernel,
        out_shape=jax.ShapeDtypeStruct((keys.shape[0], 2 * HEAD_DIM), BF16),
        in_specs=[ANY, ANY],
        out_specs=VMEM,
        scratch_shapes=[pltpu.SemaphoreType.DMA((2,))],
        compiler_params=SMALL,
        name="pack",
    )(keys, values)


def prepare_kernel(
    id_ref,
    len_ref,
    q_hbm,
    g_hbm,
    table_hbm,
    rk_hbm,
    rv_hbm,
    biased_ref,
    masked_ref,
    rk_ref,
    rv_ref,
    table_ref,
    sems,
):
    arrays = [
        (table_hbm, table_ref),
        (q_hbm, biased_ref),
        (g_hbm, masked_ref),
        (rk_hbm, rk_ref),
        (rv_hbm, rv_ref),
    ]
    copies = [pltpu.make_async_copy(a, b, sems.at[i]) for i, (a, b) in enumerate(arrays)]
    for copy in copies:
        copy.start()
    copies[0].wait()
    chosen = lax.broadcasted_iota(jnp.int32, table_ref.shape, 0) == id_ref[0]
    pref = jnp.sum(jnp.where(chosen, table_ref[...].astype(F32), 0.0), axis=0, keepdims=True)
    copies[1].wait()
    biased_ref[...] = (biased_ref[...].astype(F32) + pref).astype(BF16)
    copies[2].wait()
    live = lax.broadcasted_iota(jnp.int32, masked_ref.shape, 0) < len_ref[0]
    masked_ref[...] = jnp.where(live, masked_ref[...], jnp.zeros((), BF16))
    copies[3].wait()
    copies[4].wait()


def prepare(pref_ids, resp_len, queries, out_grad, table, resp_keys, resp_values):
    wide = jax.ShapeDtypeStruct(queries.shape, BF16)
    slim = jax.ShapeDtypeStruct(resp_keys.shape, BF16)
    return pl.pallas_call(
        prepare_kernel,
        out_shape=[wide, wide, slim, slim],
        in_specs=[SMEM, SMEM] + [ANY] * 5,
        out_specs=[VMEM] * 4,
        scratch_shapes=[pltpu.VMEM(table.shape, BF16), pltpu.SemaphoreType.DMA((5,))],
        compiler_params=SMALL,
        cost_estimate=pl.CostEstimate(
            flops=4 * queries.size, bytes_accessed=8 * queries.size, transcendentals=0
        ),
        name="prepare",
    )(pref_ids, resp_len, queries, out_grad, table, resp_keys, resp_values)


def pair_sum_kernel(tiles, direct_ref, got_ref, r_ref, mate_ref, *out_refs):
    at = 0
    for out, count in zip(out_refs, tiles):
        n = out.shape[0] - count * RTILE
        total = direct_ref[at : at + n, :].astype(F32) + got_ref[at : at + n, :].astype(F32)
        out[:n, :] = total.astype(out.dtype)
        if count:
            out[n : n + RTILE, :] = r_ref[...]
        if count == 2:
            out[n + RTILE :, :] = mate_ref[mate_ref.shape[0] - RTILE :, :]
        at += n


def pair_sum(direct, got, r_tile, mate, sizes, tiles):
    lanes = direct.shape[1]
    return pl.pallas_call(
        functools.partial(pair_sum_kernel, tiles),
        out_shape=[
            jax.ShapeDtypeStruct((n + t * RTILE, lanes), BF16 if t else F32)
            for n, t in zip(sizes, tiles)
        ],
        in_specs=[VMEM] * 4,
        out_specs=[VMEM] * len(sizes),
        compiler_params=SMALL,
        name="pair_sum",
    )(direct, got, r_tile, mate)


def middle_sum_kernel(two_ref, three_ref, four_ref, r_ref, got_ref, out_ref):
    rows = two_ref.shape[0]
    block = rows // 2
    total = two_ref[...] + three_ref[:rows, :].astype(F32)
    out_ref[:block, :] = (total[:block, :] + four_ref[:block, :].astype(F32)).astype(BF16)
    out_ref[block:rows, :] = total[block:, :].astype(BF16)
    out_ref[rows : rows + RTILE, :] = r_ref[...]
    out_ref[rows + RTILE : rows + 2 * RTILE, :] = got_ref[got_ref.shape[0] - RTILE :, :]
    out_ref[rows + 2 * RTILE : rows + 4 * RTILE, :] = three_ref[rows:, :]
    out_ref[rows + 4 * RTILE :, :] = four_ref[block:, :]


def middle_sum(two, three, four, r_tile, got):
    return pl.pallas_call(
        middle_sum_kernel,
        out_shape=jax.ShapeDtypeStruct((two.shape[0] + 5 * RTILE, two.shape[1]), BF16),
        in_specs=[VMEM] * 5,
        out_specs=VMEM,
        compiler_params=SMALL,
        name="middle_sum",
    )(two, three, four, r_tile, got)


def chip_sum_kernel(near_ref, one_ref, two_ref, mine_ref, other_ref):
    rows = near_ref.shape[0]
    block = rows // 2
    total = near_ref[...].astype(F32) + one_ref[:rows, :].astype(F32) + two_ref[:rows, :].astype(F32)
    mine_ref[...] = total[:block, :]
    other_ref[:block, :] = total[block:, :].astype(BF16)
    split = block + one_ref.shape[0] - rows
    other_ref[block:split, :] = one_ref[rows:, :]
    other_ref[split:, :] = two_ref[rows:, :]


def chip_sum(near, one, two):
    rows, lanes = near.shape
    block = rows // 2
    sent = block + one.shape[0] + two.shape[0] - 2 * rows
    return pl.pallas_call(
        chip_sum_kernel,
        out_shape=[
            jax.ShapeDtypeStruct((block, lanes), F32),
            jax.ShapeDtypeStruct((sent, lanes), BF16),
        ],
        in_specs=[VMEM] * 3,
        out_specs=[VMEM] * 2,
        compiler_params=SMALL,
        name="chip_sum",
    )(near, one, two)


def last_sum_kernel(mine_ref, sent_ref, last_ref, r_ref, got_ref, dk_ref, dv_ref, pref_ref):
    block = mine_ref.shape[0]
    total = mine_ref[...] + last_ref[:block, :].astype(F32)
    dk_ref[...] = total[:, :HEAD_DIM].astype(BF16)
    dv_ref[...] = total[:, HEAD_DIM:].astype(BF16)
    n_pref, columns = pref_ref.shape
    lanes = mine_ref.shape[1]
    tiles = [r_ref[...], got_ref[got_ref.shape[0] - RTILE :, :]]
    for ref in (sent_ref, last_ref):
        for at in range(block, ref.shape[0], RTILE):
            tiles.append(ref[at : at + RTILE, :])
    tiles = [t.astype(F32) for t in tiles]
    count = columns // lanes
    hot = jnp.concatenate([t[count : count + 1, :n_pref] for t in tiles], axis=0)
    hot = hot.astype(BF16)
    for j in range(count):
        sums = jnp.concatenate([t[j : j + 1, :] for t in tiles], axis=0).astype(BF16)
        pref_ref[:, j * lanes : (j + 1) * lanes] = lax.dot_general(
            hot, sums, (((0,), (0,)), ((), ())), preferred_element_type=F32
        )


def last_sum(mine, sent, last, r_tile, got, n_pref, columns):
    block = mine.shape[0]
    return pl.pallas_call(
        last_sum_kernel,
        out_shape=[
            jax.ShapeDtypeStruct((block, HEAD_DIM), BF16),
            jax.ShapeDtypeStruct((block, HEAD_DIM), BF16),
            jax.ShapeDtypeStruct((n_pref, columns), F32),
        ],
        in_specs=[VMEM] * 5,
        out_specs=[VMEM] * 3,
        compiler_params=SMALL,
        name="last_sum",
    )(mine, sent, last, r_tile, got)


def in_hbm(array):
    return pltpu.with_memory_space_constraint(array, pltpu.HBM)


def shards(
    n_resp,
    queries,
    resp_keys,
    resp_values,
    prompt_keys,
    prompt_values,
    out_grad,
    pref_table,
    pref_ids,
    resp_len,
):
    pair, along = ring_moves(n_resp)

    def move(array, moves):
        return lax.ppermute(array, "resp", moves)

    block = prompt_keys.shape[0]
    arrays = (queries, out_grad, pref_table, resp_keys, resp_values)
    biased, masked, resp_keys, resp_values = prepare(
        pref_ids, resp_len, *[in_hbm(array) for array in arrays]
    )
    own = pack(in_hbm(prompt_keys), in_hbm(prompt_values))
    chip = jnp.concatenate([own, move(own, pair)], axis=0)
    chip, biased, masked = lax.optimization_barrier((chip, biased, masked))
    second = move(chip, along(2))
    first = move(chip, along(1))
    part0 = scores(biased, masked, [chip], (resp_keys, resp_values))
    second, part0 = lax.optimization_barrier((second, part0))
    third = move(second, along(1))
    fourth = move(second[:block], along(2))
    part1 = scores(biased, masked, [first, second])
    part2 = scores(biased, masked, [move(first, pair), move(second, pair)])
    third, fourth, part1, part2 = lax.optimization_barrier((third, fourth, part1, part2))
    part3 = scores(biased, masked, [third, fourth])
    part4 = scores(biased, masked, [move(third, pair), move(fourth, pair)])
    parts = [part0, part1, part2, part3, part4]
    lows, dps, stats, keys_t = zip(*parts)
    *ds, query_grad, scale, r_tile = query_side(
        pref_ids, lows, dps, stats, keys_t, queries.shape[0], queries.shape[1]
    )

    def keys_of(picks, *tile):
        return key_side(
            picks, scale, biased, masked, [ds[i] for i in picks], [lows[i] for i in picks], tile
        )

    direct_far, via_far = keys_of((3, 4), r_tile)
    got = move(via_far, pair)
    three, four = pair_sum(direct_far, got, r_tile, got, (2 * block, block), (2, 1))
    direct_close, via_close = keys_of((1, 2))
    one, two = pair_sum(
        direct_close, move(via_close, pair), r_tile, got, (2 * block, 2 * block), (2, 0)
    )
    near, resp_key_grad, resp_value_grad = keys_of((0,))
    four = move(four, along(-2))
    three = move(three, along(-1))
    one = move(one, along(-1))
    two = move(middle_sum(two, three, four, r_tile, got), along(-2))
    mine, sent = chip_sum(near, one, two)
    last = move(sent, pair)
    prompt_key_grad, prompt_value_grad, pref_grad = last_sum(
        mine, sent, last, r_tile, got, pref_table.shape[0], queries.shape[1]
    )
    return (
        query_grad,
        resp_key_grad,
        resp_value_grad,
        prompt_key_grad,
        prompt_value_grad,
        pref_grad,
    )


def solution(mesh):
    rows = P(("dp", "resp"), "tensor")
    in_specs = (rows,) * 6 + (P(None, "tensor"), P(("dp", "resp")), P(("dp", "resp")))
    out_specs = (rows,) * 5 + (P("dp", "tensor"),)
    return jax.shard_map(
        functools.partial(shards, mesh.shape["resp"]),
        mesh=mesh,
        in_specs=in_specs,
        out_specs=out_specs,
        check_vma=False,
    )
```

time: 189 us -> 58.2 us (0.31); the launches traced: 186 us -> 58 us
  blocking collectives: 84 us -> 0 us
  matrix products: 53.2 us -> 0 us
  Pallas kernels: 0 us -> 21.9 us
  starting transfers between devices: 0.04 us -> 20.6 us
  other arithmetic: 14.5 us -> 0.01 us
  between operations: 15.6 us -> 2.1 us
  local copies, waits for them, and re-layouts: 13.4 us -> 0.01 us
  waiting for transfers between devices: 4.49 us -> 13.4 us
    dot_general x24 -> x0, matrix products: 53.2 us -> none  [the longest x4 13 us: pair_step(): jnp.dot(low_weights.T, grad_rows, preferred_element_type=jnp.float32)]
    psum x1 -> x0, blocking collectives: 43.9 us -> none  [shards(): lax.psum((chosen[:, None] * row_sums[None, :]).astype(jnp.bfloat16), 'resp')]
    all_gather x2 -> x0, blocking collectives: 40 us -> none  [the longest x1 22.8 us: shards(): lax.all_gather(prompt_keys, 'resp', axis=0, tiled=True)]
    pallas_call x0 -> x16, Pallas kernels: none -> 21.9 us  [the longest x5 8.29 us: scores(): pl.pallas_call(functools.partial(scores_kernel, len(blocks), bool(resp)),...]
    ppermute x0 -> x16, starting transfers between devices: none -> 20.6 us  [move(): return lax.ppermute(array, 'resp', moves)]
    ppermute x0 -> x16, waiting for transfers between devices: none -> 13.4 us  [move(): return lax.ppermute(array, 'resp', moves)]
    while x72 -> x0, local copies, waits for them, and re-layouts: 4.77 us -> none
    reduce_sum x6 -> x0, other arithmetic: 4.64 us -> none  [the longest x4 3.09 us: pair_step(): row_total = jnp.sum(exponent, axis=1, keepdims=True)]
  transfers between devices with their start and end apart: 1 -> 16, of which waited for: 1 -> 5; matrix products, arithmetic and copies ran while one was open for 3% -> 0% of each run, Pallas kernels for 0% -> 22%
where the time goes in v2:
time: 58.2 us; the launch traced here: 58 us
  Pallas kernels  21.9 us (38%)
  starting transfers between devices  20.6 us (35%)
  waiting for transfers between devices  13.4 us (23%)
  between operations  2.1 us (4%)
    ppermute x16, starting transfers between devices, move(): return lax.ppermute(array, 'resp', moves)  20.6 us
    ppermute x16, waiting for transfers between devices, move(): return lax.ppermute(array, 'resp', moves)  13.4 us
    pallas_call x5, Pallas kernels, scores(): pl.pallas_call(functools.partial(scores_kernel, len(blocks), bool(resp)),...  8.29 us
    pallas_call x3, Pallas kernels, key_side(): pl.pallas_call(functools.partial(key_kernel, picks, len(r_tile)), out_sha...  6.71 us
    pallas_call x1, Pallas kernels, query_side(): pl.pallas_call(functools.partial(query_kernel, count), out_shape=[shape(l...  3.8 us
    pallas_call x1, Pallas kernels, prepare(): pl.pallas_call(prepare_kernel, out_shape=[wide, wide, slim, slim], in_spe...  1.31 us
  transfers between devices with their start and end apart: 16, of which 5 were waited for; matrix products, arithmetic and copies ran while one was open for 0% of the time, Pallas kernels for 22%

profile of v2, /device:TPU:1, one launch (start us, length us, event | category | flops | bytes accessed | tf_op | source)
XLA Modules:
  0.0 58.0 jit_solution(5723797803842149815)
XLA Ops:
  0.6 0.8 %pack.1 = bf16[128,256]{1,0:T(8,128)(2,1)S(1)} custom-call(bf16[128,128]{1,0:T(8,128)(2,1)} %k_ref.1, bf16[128,128]{1,0:T(8,128)(2,1)} %v_ref.1), custom_call_target="tpu_custom_call" | custom-call | tf_op jit(solution)/shard_map/pack/pallas_call | solution.py:257
  1.4 3.3 %collective-permute-start = (bf16[128,256]{1,0:T(8,128)(2,1)S(1)}, bf16[128,256]{1,0:T(8,128)(2,1)S(1)}, u32[]{:S(2)}, u32[]{:S(2)}) collective-permute-start(bf16[128,256]{1,0:T(8,128)(2,1)S(1)} %pack.1), channel_id=1, source_target_pairs={{0,8},{8,0},{16,24},{24,16},{32,40},{40,32},{48,56},{56,48},{64,72... | collective-permute-start | bytes 196616 | tf_op jit(solution)/shard_map/ppermute | solution.py:458
  6.1 1.3 %prepare.1 = (bf16[256,1024]{1,0:T(8,128)(2,1)S(1)}, bf16[256,1024]{1,0:T(8,128)(2,1)S(1)}, bf16[256,128]{1,0:T(8,128)(2,1)S(1)}, bf16[256,128]{1,0:T(8,128)(2,1)S(1)}) custom-call(s32[1]{0:T(128)S(6)} %copy.15.id_ref, s32[1]{0:T(128)S(6)} %copy.16.len_ref, bf16[256,1024]{1,0:T(8,128)(2,1)} %q_hbm.1, bf16[256,1024]{1,0:T(8,128)(2,1)} %g_hbm.1, ...), custom_call_target="tpu_custom_call" | custom-call | flops 1048576 | bytes 2097152 | tf_op jit(solution)/shard_map/prepare/pallas_call | solution.py:308
  7.4 0.0 collective-permute-done
  7.4 4.4 %collective-permute-start.1 = (bf16[256,256]{1,0:T(8,128)(2,1)S(1)}, bf16[256,256]{1,0:T(8,128)(2,1)S(1)}, u32[]{:S(2)}, u32[]{:S(2)}) collective-permute-start(bf16[256,256]{1,0:T(8,128)(2,1)S(1)} %pad_maximum_fusion.refs_0_), channel_id=1, source_target_pairs={{0,32},{8,104},{16,48},{24,120},{32,64},{40,8},{48,80},{56,24},{64... | collective-permute-start | bytes 393224 | tf_op jit(solution)/shard_map/ppermute | solution.py:458
  11.8 0.7 %collective-permute-start.4 = (bf16[256,256]{1,0:T(8,128)(2,1)S(1)}, bf16[256,256]{1,0:T(8,128)(2,1)S(1)}, u32[]{:S(2)}, u32[]{:S(2)}) collective-permute-start(bf16[256,256]{1,0:T(8,128)(2,1)S(1)} %pad_maximum_fusion.refs_0_), channel_id=1, source_target_pairs={{0,16},{8,120},{16,32},{24,8},{32,48},{40,24},{48,64},{56,40},{64,... | collective-permute-start | bytes 393224 | tf_op jit(solution)/shard_map/ppermute | solution.py:458
  12.5 1.7 %scores.5 = (bf16[512,2048]{1,0:T(8,128)(2,1)S(1)}, f32[512,2048]{1,0:T(8,128)S(1)}, f32[8,2048]{1,0:T(8,128)S(1)}, bf16[128,512]{1,0:T(8,128)(2,1)S(1)}) custom-call(bf16[256,1024]{1,0:T(8,128)(2,1)S(1)} %get-tuple-element.75.q_ref, bf16[256,1024]{1,0:T(8,128)(2,1)S(1)} %get-tuple-element.76.g_ref, bf16[256,256]{1,0:T(8,128)(2,1)S(1)} %pad_maximum_fusion.refs_0_, ...), custom_call_target="tpu_custom_call" | custom-call | flops 536870912 | tf_op jit(solution)/shard_map/scores/pallas_call | solution.py:98
  14.2 0.8 %collective-permute-done.1.refs_1_ = bf16[256,256]{1,0:T(8,128)(2,1)S(1)} collective-permute-done((bf16[256,256]{1,0:T(8,128)(2,1)S(1)}, bf16[256,256]{1,0:T(8,128)(2,1)S(1)}, u32[]{:S(2)}, u32[]{:S(2)}) %collective-permute-start.1) | collective-permute-done | bytes 131104 | tf_op jit(solution)/shard_map/ppermute | solution.py:458
  15.1 1.7 %collective-permute-done.4.refs_0_ = bf16[256,256]{1,0:T(8,128)(2,1)S(1)} collective-permute-done((bf16[256,256]{1,0:T(8,128)(2,1)S(1)}, bf16[256,256]{1,0:T(8,128)(2,1)S(1)}, u32[]{:S(2)}, u32[]{:S(2)}) %collective-permute-start.4) | collective-permute-done | bytes 131104 | tf_op jit(solution)/shard_map/ppermute | solution.py:458
  16.8 0.6 %collective-permute-start.5 = (bf16[256,256]{1,0:T(8,128)(2,1)S(1)}, bf16[256,256]{1,0:T(8,128)(2,1)S(1)}, u32[]{:S(2)}, u32[]{:S(2)}) collective-permute-start(bf16[256,256]{1,0:T(8,128)(2,1)S(1)} %collective-permute-done.4.refs_0_), channel_id=1, source_target_pairs={{0,8},{8,0},{16,24},{24,16},{32,40},{40,32},{48,56},{56,48},{64,72... | collective-permute-start | bytes 393224 | tf_op jit(solution)/shard_map/ppermute | solution.py:458
  17.4 0.0 collective-permute-start.6
  17.4 2.7 %collective-permute-start.2 = (bf16[256,256]{1,0:T(8,128)(2,1)S(1)}, bf16[256,256]{1,0:T(8,128)(2,1)S(1)}, u32[]{:S(2)}, u32[]{:S(2)}) collective-permute-start(bf16[256,256]{1,0:T(8,128)(2,1)S(1)} %collective-permute-done.1.refs_1_), channel_id=1, source_target_pairs={{0,16},{8,120},{16,32},{24,8},{32,48},{40,24},{48,64},{56,40},{64,... | collective-permute-start | bytes 393224 | tf_op jit(solution)/shard_map/ppermute | solution.py:458
  20.1 0.9 %collective-permute-start.3 = (bf16[128,256]{1,0:T(8,128)(2,1)S(1)}, bf16[128,256]{1,0:T(8,128)(2,1)S(1)}, u32[]{:S(2)}, u32[]{:S(2)}) collective-permute-start(bf16[128,256]{1,0:T(8,128)(2,1)S(1)} %slice.3), channel_id=1, source_target_pairs={{0,32},{8,104},{16,48},{24,120},{32,64},{40,8},{48,80},{56,24},{64... | collective-permute-start | bytes 196616 | tf_op jit(solution)/shard_map/ppermute | solution.py:458
  21.0 1.8 %scores.6 = (bf16[512,2048]{1,0:T(8,128)(2,1)S(1)}, f32[512,2048]{1,0:T(8,128)S(1)}, f32[8,2048]{1,0:T(8,128)S(1)}, bf16[128,512]{1,0:T(8,128)(2,1)S(1)}) custom-call(bf16[256,1024]{1,0:T(8,128)(2,1)S(1)} %get-tuple-element.75.q_ref, bf16[256,1024]{1,0:T(8,128)(2,1)S(1)} %get-tuple-element.76.g_ref, bf16[256,256]{1,0:T(8,128)(2,1)S(1)} %collective-permute-done.4.refs_0_, ...), custom_call_target="tpu_custom_call" | custom-call | flops 536870912 | tf_op jit(solution)/shard_map/scores/pallas_call | solution.py:98
  22.9 0.0 collective-permute-done.5.refs_0_
  22.9 0.0 collective-permute-done.6.refs_1_
  22.9 1.8 %scores.7 = (bf16[512,2048]{1,0:T(8,128)(2,1)S(1)}, f32[512,2048]{1,0:T(8,128)S(1)}, f32[8,2048]{1,0:T(8,128)S(1)}, bf16[128,512]{1,0:T(8,128)(2,1)S(1)}) custom-call(bf16[256,1024]{1,0:T(8,128)(2,1)S(1)} %get-tuple-element.75.q_ref, bf16[256,1024]{1,0:T(8,128)(2,1)S(1)} %get-tuple-element.76.g_ref, bf16[256,256]{1,0:T(8,128)(2,1)S(1)} %collective-permute-done.5.refs_0_, ...), custom_call_target="tpu_custom_call" | custom-call | flops 536870912 | tf_op jit(solution)/shard_map/scores/pallas_call | solution.py:98
  24.7 0.0 collective-permute-done.3.refs_1_
  24.7 0.0 collective-permute-done.2.refs_0_
  24.7 1.5 %collective-permute-start.7 = (bf16[256,256]{1,0:T(8,128)(2,1)S(1)}, bf16[256,256]{1,0:T(8,128)(2,1)S(1)}, u32[]{:S(2)}, u32[]{:S(2)}) collective-permute-start(bf16[256,256]{1,0:T(8,128)(2,1)S(1)} %collective-permute-done.2.refs_0_), channel_id=1, source_target_pairs={{0,8},{8,0},{16,24},{24,16},{32,40},{40,32},{48,56},{56,48},{64,72... | collective-permute-start | bytes 393224 | tf_op jit(solution)/shard_map/ppermute | solution.py:458
  26.2 0.0 collective-permute-start.8
  26.2 1.4 %scores.8 = (bf16[384,2048]{1,0:T(8,128)(2,1)S(1)}, f32[384,2048]{1,0:T(8,128)S(1)}, f32[8,2048]{1,0:T(8,128)S(1)}, bf16[128,384]{1,0:T(8,128)(2,1)S(1)}) custom-call(bf16[256,1024]{1,0:T(8,128)(2,1)S(1)} %get-tuple-element.75.q_ref, bf16[256,1024]{1,0:T(8,128)(2,1)S(1)} %get-tuple-element.76.g_ref, bf16[256,256]{1,0:T(8,128)(2,1)S(1)} %collective-permute-done.2.refs_0_, ...), custom_call_target="tpu_custom_call" | custom-call | flops 402653184 | tf_op jit(solution)/shard_map/scores/pallas_call | solution.py:98
  27.7 0.0 collective-permute-done.8.refs_1_
  27.7 0.0 collective-permute-done.7.refs_0_
  27.7 1.4 %scores.9 = (bf16[384,2048]{1,0:T(8,128)(2,1)S(1)}, f32[384,2048]{1,0:T(8,128)S(1)}, f32[8,2048]{1,0:T(8,128)S(1)}, bf16[128,384]{1,0:T(8,128)(2,1)S(1)}) custom-call(bf16[256,1024]{1,0:T(8,128)(2,1)S(1)} %get-tuple-element.75.q_ref, bf16[256,1024]{1,0:T(8,128)(2,1)S(1)} %get-tuple-element.76.g_ref, bf16[256,256]{1,0:T(8,128)(2,1)S(1)} %collective-permute-done.7.refs_0_, ...), custom_call_target="tpu_custom_call" | custom-call | flops 402653184 | tf_op jit(solution)/shard_map/scores/pallas_call | solution.py:98
  29.1 3.8 %query_side.1 = (bf16[512,2048]{1,0:T(8,128)(2,1)S(1)}, bf16[512,2048]{1,0:T(8,128)(2,1)S(1)}, bf16[512,2048]{1,0:T(8,128)(2,1)S(1)}, bf16[384,2048]{1,0:T(8,128...) custom-call(s32[1]{0:T(128)S(6)} %copy.15.id_ref, ...), custom_call_target="tpu_custom_call" | custom-call | flops 1207959552 | tf_op jit(solution)/shard_map/query_side/pallas_call | solution.py:166
  32.9 2.0 %key_side.5 = (bf16[384,256]{1,0:T(8,128)(2,1)S(1)}, bf16[400,256]{1,0:T(8,128)(2,1)S(1)}) custom-call(f32[8,2048]{1,0:T(8,128)S(1)} %get-tuple-element.115.scale_ref, bf16[256,1024]{1,0:T(8,128)(2,1)S(1)} %get-tuple-element.75.q_ref, bf16[256,1024]{1,0:T(8,128)(2,1)S(1)} %get-tuple-element.76.g_ref, bf16[384,2048]{1,0:T(8,128)(2,1)S(1)} %get-tuple-element.125.refs_0_, ...), custom_call_target="tpu_custom_call" | custom-call | flops 805306368 | tf_op jit(solution)/shard_map/key_side/pallas_call | solution.py:231
  34.9 0.6 %collective-permute-start.10 = (bf16[400,256]{1,0:T(8,128)(2,1)S(1)}, bf16[400,256]{1,0:T(8,128)(2,1)S(1)}, u32[]{:S(2)}, u32[]{:S(2)}) collective-permute-start(bf16[400,256]{1,0:T(8,128)(2,1)S(1)} %get-tuple-element.127), channel_id=1, source_target_pairs={{0,8},{8,0},{16,24},{24,16},{32,40},{40,32},{48,56},{56,48},{64,72... | collective-permute-start | bytes 614408 | tf_op jit(solution)/shard_map/ppermute | solution.py:458
  35.5 2.6 %key_side.4 = (bf16[512,256]{1,0:T(8,128)(2,1)S(1)}, bf16[512,256]{1,0:T(8,128)(2,1)S(1)}) custom-call(f32[8,2048]{1,0:T(8,128)S(1)} %get-tuple-element.115.scale_ref, bf16[256,1024]{1,0:T(8,128)(2,1)S(1)} %get-tuple-element.75.q_ref, bf16[256,1024]{1,0:T(8,128)(2,1)S(1)} %get-tuple-element.76.g_ref, bf16[512,2048]{1,0:T(8,128)(2,1)S(1)} %get-tuple-element.120.refs_0_, ...), custom_call_target="tpu_custom_call" | custom-call | flops 1073741824 | tf_op jit(solution)/shard_map/key_side/pallas_call | solution.py:231
  38.2 0.1 collective-permute-start.9
  38.3 0.0 collective-permute-done.10.mate_ref.got_ref
  38.3 0.1 pair_sum.3
  38.3 1.7 %collective-permute-start.12 = (bf16[288,256]{1,0:T(8,128)(2,1)S(1)}, bf16[288,256]{1,0:T(8,128)(2,1)S(1)}, u32[]{:S(2)}, u32[]{:S(2)}) collective-permute-start(bf16[288,256]{1,0:T(8,128)(2,1)S(1)} %get-tuple-element.131), channel_id=1, source_target_pairs={{0,112},{8,24},{16,0},{24,40},{32,16},{40,56},{48,32},{56,72},{64,... | collective-permute-start | bytes 442376 | tf_op jit(solution)/shard_map/ppermute | solution.py:458
  40.0 0.8 %collective-permute-start.13 = (bf16[144,256]{1,0:T(8,128)(2,1)S(1)}, bf16[144,256]{1,0:T(8,128)(2,1)S(1)}, u32[]{:S(2)}, u32[]{:S(2)}) collective-permute-start(bf16[144,256]{1,0:T(8,128)(2,1)S(1)} %get-tuple-element.132), channel_id=1, source_target_pairs={{0,96},{8,40},{16,112},{24,56},{32,0},{40,72},{48,16},{56,88},{64,... | collective-permute-start | bytes 221192 | tf_op jit(solution)/shard_map/ppermute | solution.py:458
  40.8 0.0 collective-permute-done.9.got_ref
  40.8 0.1 pair_sum.2
  40.9 5.2 %collective-permute-done.13.four_ref = bf16[144,256]{1,0:T(8,128)(2,1)S(1)} collective-permute-done((bf16[144,256]{1,0:T(8,128)(2,1)S(1)}, bf16[144,256]{1,0:T(8,128)(2,1)S(1)}, u32[]{:S(2)}, u32[]{:S(2)}) %collective-permute-start.13) | collective-permute-done | bytes 73760 | tf_op jit(solution)/shard_map/ppermute | solution.py:458
  46.1 0.0 collective-permute-done.12.three_ref
  46.2 0.3 collective-permute-start.14
  46.5 1.3 %collective-permute-start.11 = (bf16[288,256]{1,0:T(8,128)(2,1)S(1)}, bf16[288,256]{1,0:T(8,128)(2,1)S(1)}, u32[]{:S(2)}, u32[]{:S(2)}) collective-permute-start(bf16[288,256]{1,0:T(8,128)(2,1)S(1)} %get-tuple-element.128), channel_id=1, source_target_pairs={{0,112},{8,24},{16,0},{24,40},{32,16},{40,56},{48,32},{56,72},{64,... | collective-permute-start | bytes 442376 | tf_op jit(solution)/shard_map/ppermute | solution.py:458
  47.8 2.1 %key_side.3 = (bf16[256,256]{1,0:T(8,128)(2,1)S(1)}, bf16[256,128]{1,0:T(8,128)(2,1)}, bf16[256,128]{1,0:T(8,128)(2,1)}) custom-call(f32[8,2048]{1,0:T(8,128)S(1)} %get-tuple-element.115.scale_ref, bf16[256,1024]{1,0:T(8,128)(2,1)S(1)} %get-tuple-element.75.q_ref, bf16[256,1024]{1,0:T(8,128)(2,1)S(1)} %get-tuple-element.76.g_ref, ...), custom_call_target="tpu_custom_call" | custom-call | flops 536870912 | tf_op jit(solution)/shard_map/key_side/pallas_call | solution.py:231
  49.9 4.7 %collective-permute-done.11.one_ref = bf16[288,256]{1,0:T(8,128)(2,1)S(1)} collective-permute-done((bf16[288,256]{1,0:T(8,128)(2,1)S(1)}, bf16[288,256]{1,0:T(8,128)(2,1)S(1)}, u32[]{:S(2)}, u32[]{:S(2)}) %collective-permute-start.11) | collective-permute-done | bytes 147488 | tf_op jit(solution)/shard_map/ppermute | solution.py:458
  54.5 0.0 collective-permute-done.14.two_ref
  54.5 0.1 chip_sum.1
  54.6 1.6 %collective-permute-start.15 = (bf16[240,256]{1,0:T(8,128)(2,1)S(1)}, bf16[240,256]{1,0:T(8,128)(2,1)S(1)}, u32[]{:S(2)}, u32[]{:S(2)}) collective-permute-start(bf16[240,256]{1,0:T(8,128)(2,1)S(1)} %get-tuple-element.134.sent_ref), channel_id=1, source_target_pairs={{0,8},{8,0},{16,24},{24,16},{32,40},{40,32},{48,56},{56,48},{64,72... | collective-permute-start | bytes 368648 | tf_op jit(solution)/shard_map/ppermute | solution.py:458
  56.3 1.0 %collective-permute-done.15.last_ref = bf16[240,256]{1,0:T(8,128)(2,1)S(1)} collective-permute-done((bf16[240,256]{1,0:T(8,128)(2,1)S(1)}, bf16[240,256]{1,0:T(8,128)(2,1)S(1)}, u32[]{:S(2)}, u32[]{:S(2)}) %collective-permute-start.15) | collective-permute-done | bytes 122912 | tf_op jit(solution)/shard_map/ppermute | solution.py:458
  57.2 0.8 %last_sum.1 = (bf16[128,128]{1,0:T(8,128)(2,1)}, bf16[128,128]{1,0:T(8,128)(2,1)}, f32[16,1024]{1,0:T(8,128)}) custom-call(f32[128,256]{1,0:T(8,128)S(1)} %get-tuple-element.133.mine_ref, bf16[240,256]{1,0:T(8,128)(2,1)S(1)} %get-tuple-element.134.sent_ref, bf16[240,256]{1,0:T(8,128)(2,1)S(1)} %collective-permute-done.15.last_ref, ...), custom_call_target="tpu_custom_call" | custom-call | tf_op jit(solution)/shard_map/last_sum/pallas_call | solution.py:425
  (3 shorter events, 0.1 us)
Async XLA Ops:
  1.4 6.0 %collective-permute-start = (bf16[128,256]{1,0:T(8,128)(2,1)S(1)}, bf16[128,256]{1,0:T(8,128)(2,1)S(1)}, u32[]{:S(2)}, u32[]{:S(2)}) collective-permute-start(bf16[128,256]{1,0:T(8,128)(2,1)S(1)} %pack.1), channel_id=1, source_target_pairs={{0,8},{8,0},{16,24},{24,16},{32,40},{40,32},{48,56},{56,48},{64,72... | collective-permute-start | bytes 196616 | tf_op jit(solution)/shard_map/ppermute | solution.py:458
  7.4 7.7 %collective-permute-start.1 = (bf16[256,256]{1,0:T(8,128)(2,1)S(1)}, bf16[256,256]{1,0:T(8,128)(2,1)S(1)}, u32[]{:S(2)}, u32[]{:S(2)}) collective-permute-start(bf16[256,256]{1,0:T(8,128)(2,1)S(1)} %pad_maximum_fusion.refs_0_), channel_id=1, source_target_pairs={{0,32},{8,104},{16,48},{24,120},{32,64},{40,8},{48,80},{56,24},{64... | collective-permute-start | bytes 393224 | tf_op jit(solution)/shard_map/ppermute | solution.py:458
  11.8 5.0 %collective-permute-start.4 = (bf16[256,256]{1,0:T(8,128)(2,1)S(1)}, bf16[256,256]{1,0:T(8,128)(2,1)S(1)}, u32[]{:S(2)}, u32[]{:S(2)}) collective-permute-start(bf16[256,256]{1,0:T(8,128)(2,1)S(1)} %pad_maximum_fusion.refs_0_), channel_id=1, source_target_pairs={{0,16},{8,120},{16,32},{24,8},{32,48},{40,24},{48,64},{56,40},{64,... | collective-permute-start | bytes 393224 | tf_op jit(solution)/shard_map/ppermute | solution.py:458
  16.8 6.1 %collective-permute-start.5 = (bf16[256,256]{1,0:T(8,128)(2,1)S(1)}, bf16[256,256]{1,0:T(8,128)(2,1)S(1)}, u32[]{:S(2)}, u32[]{:S(2)}) collective-permute-start(bf16[256,256]{1,0:T(8,128)(2,1)S(1)} %collective-permute-done.4.refs_0_), channel_id=1, source_target_pairs={{0,8},{8,0},{16,24},{24,16},{32,40},{40,32},{48,56},{56,48},{64,72... | collective-permute-start | bytes 393224 | tf_op jit(solution)/shard_map/ppermute | solution.py:458
  17.4 5.5 %collective-permute-start.6 = (bf16[256,256]{1,0:T(8,128)(2,1)S(1)}, bf16[256,256]{1,0:T(8,128)(2,1)S(1)}, u32[]{:S(2)}, u32[]{:S(2)}) collective-permute-start(bf16[256,256]{1,0:T(8,128)(2,1)S(1)} %collective-permute-done.1.refs_1_), channel_id=1, source_target_pairs={{0,8},{8,0},{16,24},{24,16},{32,40},{40,32},{48,56},{56,48},{64,72... | collective-permute-start | bytes 393224 | tf_op jit(solution)/shard_map/ppermute | solution.py:458
  17.4 7.4 %collective-permute-start.2 = (bf16[256,256]{1,0:T(8,128)(2,1)S(1)}, bf16[256,256]{1,0:T(8,128)(2,1)S(1)}, u32[]{:S(2)}, u32[]{:S(2)}) collective-permute-start(bf16[256,256]{1,0:T(8,128)(2,1)S(1)} %collective-permute-done.1.refs_1_), channel_id=1, source_target_pairs={{0,16},{8,120},{16,32},{24,8},{32,48},{40,24},{48,64},{56,40},{64,... | collective-permute-start | bytes 393224 | tf_op jit(solution)/shard_map/ppermute | solution.py:458
  20.1 4.6 %collective-permute-start.3 = (bf16[128,256]{1,0:T(8,128)(2,1)S(1)}, bf16[128,256]{1,0:T(8,128)(2,1)S(1)}, u32[]{:S(2)}, u32[]{:S(2)}) collective-permute-start(bf16[128,256]{1,0:T(8,128)(2,1)S(1)} %slice.3), channel_id=1, source_target_pairs={{0,32},{8,104},{16,48},{24,120},{32,64},{40,8},{48,80},{56,24},{64... | collective-permute-start | bytes 196616 | tf_op jit(solution)/shard_map/ppermute | solution.py:458
  24.7 2.9 %collective-permute-start.7 = (bf16[256,256]{1,0:T(8,128)(2,1)S(1)}, bf16[256,256]{1,0:T(8,128)(2,1)S(1)}, u32[]{:S(2)}, u32[]{:S(2)}) collective-permute-start(bf16[256,256]{1,0:T(8,128)(2,1)S(1)} %collective-permute-done.2.refs_0_), channel_id=1, source_target_pairs={{0,8},{8,0},{16,24},{24,16},{32,40},{40,32},{48,56},{56,48},{64,72... | collective-permute-start | bytes 393224 | tf_op jit(solution)/shard_map/ppermute | solution.py:458
  26.2 1.4 %collective-permute-start.8 = (bf16[128,256]{1,0:T(8,128)(2,1)S(1)}, bf16[128,256]{1,0:T(8,128)(2,1)S(1)}, u32[]{:S(2)}, u32[]{:S(2)}) collective-permute-start(bf16[128,256]{1,0:T(8,128)(2,1)S(1)} %collective-permute-done.3.refs_1_), channel_id=1, source_target_pairs={{0,8},{8,0},{16,24},{24,16},{32,40},{40,32},{48,56},{56,48},{64,72... | collective-permute-start | bytes 196616 | tf_op jit(solution)/shard_map/ppermute | solution.py:458
  34.9 3.3 %collective-permute-start.10 = (bf16[400,256]{1,0:T(8,128)(2,1)S(1)}, bf16[400,256]{1,0:T(8,128)(2,1)S(1)}, u32[]{:S(2)}, u32[]{:S(2)}) collective-permute-start(bf16[400,256]{1,0:T(8,128)(2,1)S(1)} %get-tuple-element.127), channel_id=1, source_target_pairs={{0,8},{8,0},{16,24},{24,16},{32,40},{40,32},{48,56},{56,48},{64,72... | collective-permute-start | bytes 614408 | tf_op jit(solution)/shard_map/ppermute | solution.py:458
  38.2 2.7 %collective-permute-start.9 = (bf16[512,256]{1,0:T(8,128)(2,1)S(1)}, bf16[512,256]{1,0:T(8,128)(2,1)S(1)}, u32[]{:S(2)}, u32[]{:S(2)}) collective-permute-start(bf16[512,256]{1,0:T(8,128)(2,1)S(1)} %get-tuple-element.123), channel_id=1, source_target_pairs={{0,8},{8,0},{16,24},{24,16},{32,40},{40,32},{48,56},{56,48},{64,72... | collective-permute-start | bytes 786440 | tf_op jit(solution)/shard_map/ppermute | solution.py:458
  38.3 7.8 %collective-permute-start.12 = (bf16[288,256]{1,0:T(8,128)(2,1)S(1)}, bf16[288,256]{1,0:T(8,128)(2,1)S(1)}, u32[]{:S(2)}, u32[]{:S(2)}) collective-permute-start(bf16[288,256]{1,0:T(8,128)(2,1)S(1)} %get-tuple-element.131), channel_id=1, source_target_pairs={{0,112},{8,24},{16,0},{24,40},{32,16},{40,56},{48,32},{56,72},{64,... | collective-permute-start | bytes 442376 | tf_op jit(solution)/shard_map/ppermute | solution.py:458
  40.0 6.1 %collective-permute-start.13 = (bf16[144,256]{1,0:T(8,128)(2,1)S(1)}, bf16[144,256]{1,0:T(8,128)(2,1)S(1)}, u32[]{:S(2)}, u32[]{:S(2)}) collective-permute-start(bf16[144,256]{1,0:T(8,128)(2,1)S(1)} %get-tuple-element.132), channel_id=1, source_target_pairs={{0,96},{8,40},{16,112},{24,56},{32,0},{40,72},{48,16},{56,88},{64,... | collective-permute-start | bytes 221192 | tf_op jit(solution)/shard_map/ppermute | solution.py:458
  46.2 8.4 %collective-permute-start.14 = (bf16[336,256]{1,0:T(8,128)(2,1)S(1)}, bf16[336,256]{1,0:T(8,128)(2,1)S(1)}, u32[]{:S(2)}, u32[]{:S(2)}) collective-permute-start(bf16[336,256]{1,0:T(8,128)(2,1)S(1)} %middle_sum.1), channel_id=1, source_target_pairs={{0,96},{8,40},{16,112},{24,56},{32,0},{40,72},{48,16},{56,88},{64,... | collective-permute-start | bytes 516104 | tf_op jit(solution)/shard_map/ppermute | solution.py:458
  46.5 8.1 %collective-permute-start.11 = (bf16[288,256]{1,0:T(8,128)(2,1)S(1)}, bf16[288,256]{1,0:T(8,128)(2,1)S(1)}, u32[]{:S(2)}, u32[]{:S(2)}) collective-permute-start(bf16[288,256]{1,0:T(8,128)(2,1)S(1)} %get-tuple-element.128), channel_id=1, source_target_pairs={{0,112},{8,24},{16,0},{24,40},{32,16},{40,56},{48,32},{56,72},{64,... | collective-permute-start | bytes 442376 | tf_op jit(solution)/shard_map/ppermute | solution.py:458
  54.6 2.6 %collective-permute-start.15 = (bf16[240,256]{1,0:T(8,128)(2,1)S(1)}, bf16[240,256]{1,0:T(8,128)(2,1)S(1)}, u32[]{:S(2)}, u32[]{:S(2)}) collective-permute-start(bf16[240,256]{1,0:T(8,128)(2,1)S(1)} %get-tuple-element.134.sent_ref), channel_id=1, source_target_pairs={{0,8},{8,0},{16,24},{24,16},{32,40},{40,32},{48,56},{56,48},{64,72... | collective-permute-start | bytes 368648 | tf_op jit(solution)/shard_map/ppermute | solution.py:458

commit v3 on v2

--- a/solution.py
+++ b/solution.py
@@ -27,21 +27,27 @@
     chips = n_resp // 2
     places = [(chip, core) for chip in range(chips) for core in range(2)]
 
-    def along(step):
-        return [
-            (z * 2 + c, (z + step if c == 0 else z - step) % chips * 2 + c) for z, c in places
-        ]
-
-    pair = [(z * 2 + c, z * 2 + 1 - c) for z, c in places]
-    return pair, along
-
-
-def columns_of(ref, group):
-    parts = []
-    for i in range(HEADS_PER_STEP):
-        at = (group * HEADS_PER_STEP + i) * HEAD_DIM
-        parts.append(ref[:, at : at + HEAD_DIM])
-    return jnp.concatenate(parts, axis=0)
+    def index(chip, core):
+        return chip % chips * 2 + core
+
+    def sign(chip, core, period):
+        return 1 if (chip % period < period // 2) == (core == 0) else -1
+
+    def reply_core(chip, neighbour):
+        return 0 if sign(neighbour, 0, 4) == neighbour - chip else 1
+
+    pair, one, two, three, four = [], [], [], [], []
+    for z, c in places:
+        me = index(z, c)
+        pair.append((me, index(z, 1 - c)))
+        one.append((me, index(z + sign(z, c, 2), c)))
+        step = sign(z, c, 4)
+        two.append((me, index(z + 2 * step, c)))
+        three.append((me, index(z - step, reply_core(z, z - step))))
+        four.append((me, index(z - 2 * step, c)))
+    for moves in (pair, one, two, three, four):
+        assert sorted(moves) == sorted((b, a) for a, b in moves)
+    return pair, one, two, three, four
 
 
 def scores_kernel(n_blocks, has_resp, q_ref, g_ref, *refs):
@@ -49,7 +55,6 @@
     resp_refs = refs[n_blocks : n_blocks + 2 * has_resp]
     low_ref, dp_ref, stat_ref, keys_t_ref, *score_refs = refs[n_blocks + 2 * has_resp :]
     rows = q_ref.shape[0]
-    width = HEADS_PER_STEP * rows
     factor = SCALING * LOG2E
     pieces = []
     at = 0
@@ -61,30 +66,40 @@
         pieces.append((at, rows, resp_refs[0], resp_refs[1], True))
     for at, n, key_ref, _, _ in pieces:
         keys_t_ref[:, at : at + n] = key_ref[...].T
-    for group in range(q_ref.shape[1] // (HEADS_PER_STEP * HEAD_DIM)):
-        s_scr = score_refs[group % 2]
-        cols = slice(group * width, (group + 1) * width)
-        q = columns_of(q_ref, group)
-        g = columns_of(g_ref, group)
-        top = jnp.full((8, width), -1e30, F32)
-        for at, n, key_ref, _, is_resp in pieces:
-            s = lax.dot_general(key_ref[...], q, NT, preferred_element_type=F32)
-            if is_resp:
-                key_pos = lax.broadcasted_iota(jnp.int32, (n, width), 0)
-                query_pos = lax.broadcasted_iota(jnp.int32, (n, width), 1) % rows
-                s = jnp.where(key_pos <= query_pos, s, -1e30)
-            s_scr[at : at + n, :] = s
-            top = jnp.maximum(top, jnp.max(s.reshape(n // 8, 8, width), axis=0))
+
+    def score(head, piece, top):
+        at, n, key_ref, _, is_resp = piece
+        q = q_ref[:, head * HEAD_DIM : (head + 1) * HEAD_DIM]
+        s = lax.dot_general(key_ref[...], q, NT, preferred_element_type=F32)
+        if is_resp:
+            key_pos = lax.broadcasted_iota(jnp.int32, (n, rows), 0)
+            query_pos = lax.broadcasted_iota(jnp.int32, (n, rows), 1)
+            s = jnp.where(key_pos <= query_pos, s, -1e30)
+        score_refs[head % 2][at : at + n, :] = s
+        return jnp.maximum(top, jnp.max(s.reshape(n // 8, 8, rows), axis=0))
+
+    lowest = jnp.full((8, rows), -1e30, F32)
+    heads = q_ref.shape[1] // HEAD_DIM
+    top = lowest
+    for piece in pieces:
+        top = score(0, piece, top)
+    for head in range(heads):
+        cols = slice(head * rows, (head + 1) * rows)
+        g = g_ref[:, head * HEAD_DIM : (head + 1) * HEAD_DIM]
         row_max = jnp.max(top, axis=0, keepdims=True) * factor
-        total = jnp.zeros((8, width), F32)
-        dot = jnp.zeros((8, width), F32)
-        for at, n, _, value_ref, _ in pieces:
-            p = jnp.exp2(s_scr[at : at + n, :] * factor - row_max)
+        total = jnp.zeros((8, rows), F32)
+        dot = jnp.zeros((8, rows), F32)
+        top = lowest
+        for piece in pieces:
+            at, n, _, value_ref, _ = piece
+            p = jnp.exp2(score_refs[head % 2][at : at + n, :] * factor - row_max)
             dp = lax.dot_general(value_ref[...], g, NT, preferred_element_type=F32)
-            total = total + jnp.sum(p.reshape(n // 8, 8, width), axis=0)
-            dot = dot + jnp.sum((p * dp).reshape(n // 8, 8, width), axis=0)
+            total = total + jnp.sum(p.reshape(n // 8, 8, rows), axis=0)
+            dot = dot + jnp.sum((p * dp).reshape(n // 8, 8, rows), axis=0)
             low_ref[at : at + n, cols] = p.astype(BF16)
             dp_ref[at : at + n, cols] = dp
+            if head + 1 < heads:
+                top = score(head + 1, piece, top)
         stat_ref[0:1, cols] = row_max
         stat_ref[1:2, cols] = jnp.sum(total, axis=0, keepdims=True)
         stat_ref[2:3, cols] = jnp.sum(dot, axis=0, keepdims=True)
@@ -105,7 +120,7 @@
         ],
         in_specs=[VMEM] * (2 + len(blocks) + len(resp)),
         out_specs=[VMEM] * 4,
-        scratch_shapes=[pltpu.VMEM((n, HEADS_PER_STEP * rows), F32)] * 2,
+        scratch_shapes=[pltpu.VMEM((n, rows), F32)] * 2,
         compiler_params=SMALL,
         cost_estimate=pl.CostEstimate(
             flops=4 * n * queries * HEAD_DIM, bytes_accessed=0, transcendentals=n * queries
@@ -182,12 +197,16 @@
     )(pref_ids, *lows, *dps, *stats, *keys_t)
 
 
-def key_kernel(picks, has_r, scale_ref, q_ref, g_ref, *refs):
+def key_kernel(picks, extra, scale_ref, q_ref, g_ref, *refs):
     count = len(picks)
     ds_refs = refs[:count]
     low_refs = refs[count : 2 * count]
-    r_refs = refs[2 * count : 2 * count + has_r]
-    *out_refs, q_scr, g_scr = refs[2 * count + has_r :]
+    extra_refs = refs[2 * count : 2 * count + extra]
+    *out_refs, q_scr, g_scr, sem = refs[2 * count + extra :]
+    is_near = len(out_refs) > 2
+    if is_near:
+        flush = pltpu.make_async_copy(extra_refs[0], out_refs[3], sem)
+        flush.start()
     rows = q_ref.shape[0]
     results = []
     for i, pick in enumerate(picks):
@@ -200,46 +219,49 @@
         dk = lax.dot_general(ds_refs[i][...], q_scr[i], NN, preferred_element_type=F32) * SCALING
         dv = lax.dot_general(low_refs[i][...], g_scr[i], NN, preferred_element_type=F32)
         results.append((dk.astype(BF16), dv.astype(BF16)))
-    if has_r or count > 1:
+    if not is_near:
         for ref, (dk, dv) in zip(out_refs, results):
             n = dk.shape[0]
             ref[:n, :HEAD_DIM] = dk
             ref[:n, HEAD_DIM:] = dv
-        if has_r:
-            out_refs[-1][n:, :] = r_refs[0][...]
+        if extra:
+            out_refs[-1][n:, :] = extra_refs[0][...]
     else:
-        near_ref, drk_ref, drv_ref = out_refs
+        near_ref, drk_ref, drv_ref, _ = out_refs
         n = near_ref.shape[0]
         dk, dv = results[0]
         near_ref[:, :HEAD_DIM] = dk[:n, :]
         near_ref[:, HEAD_DIM:] = dv[:n, :]
         drk_ref[...] = dk[n:, :]
         drv_ref[...] = dv[n:, :]
-
-
-def key_side(picks, scale, biased, masked, ds, lows, r_tile=()):
+        flush.wait()
+
+
+def key_side(picks, scale, biased, masked, ds, lows, near, extra):
     rows, columns = biased.shape
     queries = rows * columns // HEAD_DIM
     lanes = 2 * HEAD_DIM
-    if len(picks) > 1:
+    if not near:
         counts = [d.shape[0] for d in ds]
-        counts[-1] += RTILE * len(r_tile)
+        counts[-1] += RTILE * len(extra)
         shapes = [(n, lanes) for n in counts]
     else:
         shapes = [(ds[0].shape[0] - rows, lanes), (rows, HEAD_DIM), (rows, HEAD_DIM)]
+        shapes.append((rows, columns))
     keys = sum(d.shape[0] for d in ds)
     return pl.pallas_call(
-        functools.partial(key_kernel, picks, len(r_tile)),
+        functools.partial(key_kernel, picks, len(extra)),
         out_shape=[jax.ShapeDtypeStruct(s, BF16) for s in shapes],
-        in_specs=[VMEM] * (3 + 2 * len(picks) + len(r_tile)),
-        out_specs=[VMEM] * len(shapes),
-        scratch_shapes=[pltpu.VMEM((len(picks), queries, HEAD_DIM), BF16)] * 2,
+        in_specs=[VMEM] * (3 + 2 * len(picks) + len(extra)),
+        out_specs=[VMEM] * 3 + [ANY] if near else [VMEM] * len(shapes),
+        scratch_shapes=[pltpu.VMEM((len(picks), queries, HEAD_DIM), BF16)] * 2
+        + [pltpu.SemaphoreType.DMA],
         compiler_params=SMALL,
         cost_estimate=pl.CostEstimate(
             flops=4 * keys * queries * HEAD_DIM, bytes_accessed=0, transcendentals=0
         ),
         name="key_side",
-    )(scale, biased, masked, *ds, *lows, *r_tile)
+    )(scale, biased, masked, *ds, *lows, *extra)
 
 
 def pack_kernel(k_ref, v_ref, own_ref, sems):
@@ -263,6 +285,24 @@
         compiler_params=SMALL,
         name="pack",
     )(keys, values)
+
+
+def assemble_kernel(own_ref, k_ref, v_ref, chip_ref):
+    n = own_ref.shape[0]
+    chip_ref[:n, :] = own_ref[...]
+    chip_ref[n:, :HEAD_DIM] = k_ref[...]
+    chip_ref[n:, HEAD_DIM:] = v_ref[...]
+
+
+def assemble(own, keys, values):
+    return pl.pallas_call(
+        assemble_kernel,
+        out_shape=jax.ShapeDtypeStruct((2 * own.shape[0], own.shape[1]), BF16),
+        in_specs=[VMEM] * 3,
+        out_specs=VMEM,
+        compiler_params=SMALL,
+        name="assemble",
+    )(own, keys, values)
 
 
 def prepare_kernel(
@@ -319,16 +359,22 @@
     )(pref_ids, resp_len, queries, out_grad, table, resp_keys, resp_values)
 
 
+def chip_tile(r_ref, mate_ref):
+    own = r_ref[...].astype(F32)[: RTILE // 2]
+    mate = mate_ref[mate_ref.shape[0] - RTILE :, :].astype(F32)[: RTILE // 2]
+    return jnp.concatenate([own, mate], axis=0).astype(BF16)
+
+
 def pair_sum_kernel(tiles, direct_ref, got_ref, r_ref, mate_ref, *out_refs):
     at = 0
     for out, count in zip(out_refs, tiles):
-        n = out.shape[0] - count * RTILE
+        n = out.shape[0] - (RTILE if count else 0)
         total = direct_ref[at : at + n, :].astype(F32) + got_ref[at : at + n, :].astype(F32)
         out[:n, :] = total.astype(out.dtype)
-        if count:
-            out[n : n + RTILE, :] = r_ref[...]
+        if count == 1:
+            out[n:, :] = r_ref[...]
         if count == 2:
-            out[n + RTILE :, :] = mate_ref[mate_ref.shape[0] - RTILE :, :]
+            out[n:, :] = chip_tile(r_ref, mate_ref)
         at += n
 
 
@@ -337,7 +383,7 @@
     return pl.pallas_call(
         functools.partial(pair_sum_kernel, tiles),
         out_shape=[
-            jax.ShapeDtypeStruct((n + t * RTILE, lanes), BF16 if t else F32)
+            jax.ShapeDtypeStruct((n + RTILE if t else n, lanes), BF16 if t else F32)
             for n, t in zip(sizes, tiles)
         ],
         in_specs=[VMEM] * 4,
@@ -353,16 +399,15 @@
     total = two_ref[...] + three_ref[:rows, :].astype(F32)
     out_ref[:block, :] = (total[:block, :] + four_ref[:block, :].astype(F32)).astype(BF16)
     out_ref[block:rows, :] = total[block:, :].astype(BF16)
-    out_ref[rows : rows + RTILE, :] = r_ref[...]
-    out_ref[rows + RTILE : rows + 2 * RTILE, :] = got_ref[got_ref.shape[0] - RTILE :, :]
-    out_ref[rows + 2 * RTILE : rows + 4 * RTILE, :] = three_ref[rows:, :]
-    out_ref[rows + 4 * RTILE :, :] = four_ref[block:, :]
+    out_ref[rows : rows + RTILE, :] = chip_tile(r_ref, got_ref)
+    out_ref[rows + RTILE : rows + 2 * RTILE, :] = three_ref[rows:, :]
+    out_ref[rows + 2 * RTILE :, :] = four_ref[block:, :]
 
 
 def middle_sum(two, three, four, r_tile, got):
     return pl.pallas_call(
         middle_sum_kernel,
-        out_shape=jax.ShapeDtypeStruct((two.shape[0] + 5 * RTILE, two.shape[1]), BF16),
+        out_shape=jax.ShapeDtypeStruct((two.shape[0] + 3 * RTILE, two.shape[1]), BF16),
         in_specs=[VMEM] * 5,
         out_specs=VMEM,
         compiler_params=SMALL,
@@ -405,12 +450,14 @@
     dv_ref[...] = total[:, HEAD_DIM:].astype(BF16)
     n_pref, columns = pref_ref.shape
     lanes = mine_ref.shape[1]
-    tiles = [r_ref[...], got_ref[got_ref.shape[0] - RTILE :, :]]
+    tiles = [chip_tile(r_ref, got_ref)]
     for ref in (sent_ref, last_ref):
         for at in range(block, ref.shape[0], RTILE):
             tiles.append(ref[at : at + RTILE, :])
     tiles = [t.astype(F32) for t in tiles]
     count = columns // lanes
+    half = RTILE // 2
+    tiles = [t[at : at + half, :] for t in tiles for at in (0, half)]
     hot = jnp.concatenate([t[count : count + 1, :n_pref] for t in tiles], axis=0)
     hot = hot.astype(BF16)
     for j in range(count):
@@ -452,7 +499,7 @@
     pref_ids,
     resp_len,
 ):
-    pair, along = ring_moves(n_resp)
+    pair, to_one, to_two, to_three, to_four = ring_moves(n_resp)
 
     def move(array, moves):
         return lax.ppermute(array, "resp", moves)
@@ -462,15 +509,14 @@
     biased, masked, resp_keys, resp_values = prepare(
         pref_ids, resp_len, *[in_hbm(array) for array in arrays]
     )
-    own = pack(in_hbm(prompt_keys), in_hbm(prompt_values))
-    chip = jnp.concatenate([own, move(own, pair)], axis=0)
-    chip, biased, masked = lax.optimization_barrier((chip, biased, masked))
-    second = move(chip, along(2))
-    first = move(chip, along(1))
+    mate = [move(prompt_keys, pair), move(prompt_values, pair)]
+    chip = assemble(pack(in_hbm(prompt_keys), in_hbm(prompt_values)), *mate)
+    second = move(chip, to_two)
+    first = move(chip, to_one)
     part0 = scores(biased, masked, [chip], (resp_keys, resp_values))
     second, part0 = lax.optimization_barrier((second, part0))
-    third = move(second, along(1))
-    fourth = move(second[:block], along(2))
+    third = move(second, to_three)
+    fourth = move(second[:block], to_four)
     part1 = scores(biased, masked, [first, second])
     part2 = scores(biased, masked, [move(first, pair), move(second, pair)])
     third, fourth, part1, part2 = lax.optimization_barrier((third, fourth, part1, part2))
@@ -482,23 +528,23 @@
         pref_ids, lows, dps, stats, keys_t, queries.shape[0], queries.shape[1]
     )
 
-    def keys_of(picks, *tile):
-        return key_side(
-            picks, scale, biased, masked, [ds[i] for i in picks], [lows[i] for i in picks], tile
-        )
-
-    direct_far, via_far = keys_of((3, 4), r_tile)
+    def keys_of(picks, near, *extra):
+        some_ds, some_lows = [ds[i] for i in picks], [lows[i] for i in picks]
+        return key_side(picks, scale, biased, masked, some_ds, some_lows, near, extra)
+
+    direct_far, via_far = keys_of((3, 4), False, r_tile)
     got = move(via_far, pair)
     three, four = pair_sum(direct_far, got, r_tile, got, (2 * block, block), (2, 1))
-    direct_close, via_close = keys_of((1, 2))
+    (via_close,) = keys_of((2,), False)
+    (direct_close,) = keys_of((1,), False)
     one, two = pair_sum(
         direct_close, move(via_close, pair), r_tile, got, (2 * block, 2 * block), (2, 0)
     )
-    near, resp_key_grad, resp_value_grad = keys_of((0,))
-    four = move(four, along(-2))
-    three = move(three, along(-1))
-    one = move(one, along(-1))
-    two = move(middle_sum(two, three, four, r_tile, got), along(-2))
+    near, resp_key_grad, resp_value_grad, query_grad = keys_of((0,), True, query_grad)
+    four = move(four, to_four)
+    three = move(three, to_three)
+    one = move(one, to_one)
+    two = move(middle_sum(two, three, four, r_tile, got), to_two)
     mine, sent = chip_sum(near, one, two)
     last = move(sent, pair)
     prompt_key_grad, prompt_value_grad, pref_grad = last_sum(

time: 58.2 us -> 53 us (0.911)
  waiting for transfers between devices: 13.4 us -> 9.84 us
  starting transfers between devices: 20.6 us -> 19.2 us
    ppermute x16 -> x17, waiting for transfers between devices: 13.4 us -> 9.84 us  [move(): return lax.ppermute(array, 'resp', moves)]
    ppermute x16 -> x17, starting transfers between devices: 20.6 us -> 19.2 us  [move(): return lax.ppermute(array, 'resp', moves)]
    pallas_call x3 -> x5, Pallas kernels: 6.71 us -> 7.69 us  [the longest x4 7.67 us: key_side(): pl.pallas_call(functools.partial(key_kernel, picks, len(extra)), out_shap...]
    pallas_call x1, Pallas kernels: 3.8 us -> 3.06 us  [query_side(): pl.pallas_call(functools.partial(query_kernel, count), out_shape=[shape(l...]
  transfers between devices with their start and end apart: 16 -> 17, of which waited for: 5 -> 8; matrix products, arithmetic and copies ran while one was open for 0% -> 0% of each run, Pallas kernels for 22% -> 27%
where the time goes in v3:
time: 53 us; the launch traced here: 52.8 us
  Pallas kernels  21.7 us (41%)
  starting transfers between devices  19.2 us (36%)
  waiting for transfers between devices  9.84 us (19%)
  between operations  2.12 us (4%)
    ppermute x17, starting transfers between devices, move(): return lax.ppermute(array, 'resp', moves)  19.2 us
    ppermute x17, waiting for transfers between devices, move(): return lax.ppermute(array, 'resp', moves)  9.84 us
    pallas_call x5, Pallas kernels, scores(): pl.pallas_call(functools.partial(scores_kernel, len(blocks), bool(resp)),...  7.82 us
    pallas_call x4, Pallas kernels, key_side(): pl.pallas_call(functools.partial(key_kernel, picks, len(extra)), out_shap...  7.67 us
    pallas_call x1, Pallas kernels, query_side(): pl.pallas_call(functools.partial(query_kernel, count), out_shape=[shape(l...  3.06 us
    pallas_call x1, Pallas kernels, prepare(): pl.pallas_call(prepare_kernel, out_shape=[wide, wide, slim, slim], in_spe...  1.31 us
  transfers between devices with their start and end apart: 17, of which 8 were waited for; matrix products, arithmetic and copies ran while one was open for 0% of the time, Pallas kernels for 27%

profile of v3, /device:TPU:1, one launch (start us, length us, event | category | flops | bytes accessed | tf_op | source)
XLA Modules:
  0.0 52.8 jit_solution(9333053997619490991)
XLA Ops:
  0.6 3.3 %collective-permute-start = (bf16[128,128]{1,0:T(8,128)(2,1)}, bf16[128,128]{1,0:T(8,128)(2,1)S(1)}, u32[]{:S(2)}, u32[]{:S(2)}) collective-permute-start(bf16[128,128]{1,0:T(8,128)(2,1)} %k_ref.1), channel_id=1, source_target_pairs={{0,8},{8,0},{16,24},{24,16},{32,40},{40,32},{48,56},{56,48},{64,72... | collective-permute-start | bytes 98312 | tf_op jit(solution)/shard_map/ppermute | solution.py:505
  4.0 0.1 collective-permute-start.1
  4.1 0.8 %pack.1.own_ref = bf16[128,256]{1,0:T(8,128)(2,1)S(1)} custom-call(bf16[128,128]{1,0:T(8,128)(2,1)} %k_ref.1, bf16[128,128]{1,0:T(8,128)(2,1)} %v_ref.1), custom_call_target="tpu_custom_call" | custom-call | tf_op jit(solution)/shard_map/pack/pallas_call | solution.py:279
  4.9 0.2 collective-permute-done.k_ref
  5.0 0.3 collective-permute-done.1.v_ref
  5.4 4.4 %collective-permute-start.2 = (bf16[256,256]{1,0:T(8,128)(2,1)S(1)}, bf16[256,256]{1,0:T(8,128)(2,1)S(1)}, u32[]{:S(2)}, u32[]{:S(2)}) collective-permute-start(bf16[256,256]{1,0:T(8,128)(2,1)S(1)} %assemble.1.refs_0_), channel_id=1, source_target_pairs={{0,32},{8,104},{16,48},{24,120},{32,0},{40,72},{48,16},{56,88},{64... | collective-permute-start | bytes 393224 | tf_op jit(solution)/shard_map/ppermute | solution.py:505
  9.8 0.0 collective-permute-start.5
  11.1 1.3 %prepare.1 = (bf16[256,1024]{1,0:T(8,128)(2,1)S(1)}, bf16[256,1024]{1,0:T(8,128)(2,1)S(1)}, bf16[256,128]{1,0:T(8,128)(2,1)S(1)}, bf16[256,128]{1,0:T(8,128)(2,1)S(1)}) custom-call(s32[1]{0:T(128)S(6)} %copy.15.id_ref, s32[1]{0:T(128)S(6)} %copy.16.len_ref, bf16[256,1024]{1,0:T(8,128)(2,1)} %q_hbm.1, bf16[256,1024]{1,0:T(8,128)(2,1)} %g_hbm.1, ...), custom_call_target="tpu_custom_call" | custom-call | flops 1048576 | bytes 2097152 | tf_op jit(solution)/shard_map/prepare/pallas_call | solution.py:348
  12.4 1.6 %scores.5 = (bf16[512,2048]{1,0:T(8,128)(2,1)S(1)}, f32[512,2048]{1,0:T(8,128)S(1)}, f32[8,2048]{1,0:T(8,128)S(1)}, bf16[128,512]{1,0:T(8,128)(2,1)S(1)}) custom-call(bf16[256,1024]{1,0:T(8,128)(2,1)S(1)} %get-tuple-element.68.q_ref, bf16[256,1024]{1,0:T(8,128)(2,1)S(1)} %get-tuple-element.69.g_ref, bf16[256,256]{1,0:T(8,128)(2,1)S(1)} %assemble.1.refs_0_, ...), custom_call_target="tpu_custom_call" | custom-call | flops 536870912 | tf_op jit(solution)/shard_map/scores/pallas_call | solution.py:113
  14.0 0.0 collective-permute-done.2.refs_1_
  14.0 0.8 %collective-permute-done.5.refs_0_ = bf16[256,256]{1,0:T(8,128)(2,1)S(1)} collective-permute-done((bf16[256,256]{1,0:T(8,128)(2,1)S(1)}, bf16[256,256]{1,0:T(8,128)(2,1)S(1)}, u32[]{:S(2)}, u32[]{:S(2)}) %collective-permute-start.5) | collective-permute-done | bytes 131104 | tf_op jit(solution)/shard_map/ppermute | solution.py:505
  14.8 0.0 collective-permute-start.6
  14.8 0.5 collective-permute-start.7
  15.3 0.7 %collective-permute-start.3 = (bf16[256,256]{1,0:T(8,128)(2,1)S(1)}, bf16[256,256]{1,0:T(8,128)(2,1)S(1)}, u32[]{:S(2)}, u32[]{:S(2)}) collective-permute-start(bf16[256,256]{1,0:T(8,128)(2,1)S(1)} %collective-permute-done.2.refs_1_), channel_id=1, source_target_pairs={{0,112},{8,16},{16,8},{24,40},{32,56},{40,24},{48,64},{56,32},{64,... | collective-permute-start | bytes 393224 | tf_op jit(solution)/shard_map/ppermute | solution.py:505
  16.1 1.2 %collective-permute-start.4 = (bf16[128,256]{1,0:T(8,128)(2,1)S(1)}, bf16[128,256]{1,0:T(8,128)(2,1)S(1)}, u32[]{:S(2)}, u32[]{:S(2)}) collective-permute-start(bf16[128,256]{1,0:T(8,128)(2,1)S(1)} %slice.3), channel_id=1, source_target_pairs={{0,96},{8,40},{16,112},{24,56},{32,64},{40,8},{48,80},{56,24},{64,... | collective-permute-start | bytes 196616 | tf_op jit(solution)/shard_map/ppermute | solution.py:505
  17.3 1.7 %scores.6 = (bf16[512,2048]{1,0:T(8,128)(2,1)S(1)}, f32[512,2048]{1,0:T(8,128)S(1)}, f32[8,2048]{1,0:T(8,128)S(1)}, bf16[128,512]{1,0:T(8,128)(2,1)S(1)}) custom-call(bf16[256,1024]{1,0:T(8,128)(2,1)S(1)} %get-tuple-element.68.q_ref, bf16[256,1024]{1,0:T(8,128)(2,1)S(1)} %get-tuple-element.69.g_ref, bf16[256,256]{1,0:T(8,128)(2,1)S(1)} %collective-permute-done.5.refs_0_, ...), custom_call_target="tpu_custom_call" | custom-call | flops 536870912 | tf_op jit(solution)/shard_map/scores/pallas_call | solution.py:113
  18.9 0.0 collective-permute-done.6.refs_0_
  18.9 0.0 collective-permute-done.7.refs_1_
  18.9 1.7 %scores.7 = (bf16[512,2048]{1,0:T(8,128)(2,1)S(1)}, f32[512,2048]{1,0:T(8,128)S(1)}, f32[8,2048]{1,0:T(8,128)S(1)}, bf16[128,512]{1,0:T(8,128)(2,1)S(1)}) custom-call(bf16[256,1024]{1,0:T(8,128)(2,1)S(1)} %get-tuple-element.68.q_ref, bf16[256,1024]{1,0:T(8,128)(2,1)S(1)} %get-tuple-element.69.g_ref, bf16[256,256]{1,0:T(8,128)(2,1)S(1)} %collective-permute-done.6.refs_0_, ...), custom_call_target="tpu_custom_call" | custom-call | flops 536870912 | tf_op jit(solution)/shard_map/scores/pallas_call | solution.py:113
  20.6 0.5 collective-permute-done.4.refs_1_
  21.1 0.0 collective-permute-done.3.refs_0_
  21.1 3.7 %collective-permute-start.8 = (bf16[256,256]{1,0:T(8,128)(2,1)S(1)}, bf16[256,256]{1,0:T(8,128)(2,1)S(1)}, u32[]{:S(2)}, u32[]{:S(2)}) collective-permute-start(bf16[256,256]{1,0:T(8,128)(2,1)S(1)} %collective-permute-done.3.refs_0_), channel_id=1, source_target_pairs={{0,8},{8,0},{16,24},{24,16},{32,40},{40,32},{48,56},{56,48},{64,72... | collective-permute-start | bytes 393224 | tf_op jit(solution)/shard_map/ppermute | solution.py:505
  24.8 0.0 collective-permute-start.9
  24.8 1.5 %scores.8 = (bf16[384,2048]{1,0:T(8,128)(2,1)S(1)}, f32[384,2048]{1,0:T(8,128)S(1)}, f32[8,2048]{1,0:T(8,128)S(1)}, bf16[128,384]{1,0:T(8,128)(2,1)S(1)}) custom-call(bf16[256,1024]{1,0:T(8,128)(2,1)S(1)} %get-tuple-element.68.q_ref, bf16[256,1024]{1,0:T(8,128)(2,1)S(1)} %get-tuple-element.69.g_ref, bf16[256,256]{1,0:T(8,128)(2,1)S(1)} %collective-permute-done.3.refs_0_, ...), custom_call_target="tpu_custom_call" | custom-call | flops 402653184 | tf_op jit(solution)/shard_map/scores/pallas_call | solution.py:113
  26.3 0.0 collective-permute-done.9.refs_1_
  26.3 0.0 collective-permute-done.8.refs_0_
  26.3 1.5 %scores.9 = (bf16[384,2048]{1,0:T(8,128)(2,1)S(1)}, f32[384,2048]{1,0:T(8,128)S(1)}, f32[8,2048]{1,0:T(8,128)S(1)}, bf16[128,384]{1,0:T(8,128)(2,1)S(1)}) custom-call(bf16[256,1024]{1,0:T(8,128)(2,1)S(1)} %get-tuple-element.68.q_ref, bf16[256,1024]{1,0:T(8,128)(2,1)S(1)} %get-tuple-element.69.g_ref, bf16[256,256]{1,0:T(8,128)(2,1)S(1)} %collective-permute-done.8.refs_0_, ...), custom_call_target="tpu_custom_call" | custom-call | flops 402653184 | tf_op jit(solution)/shard_map/scores/pallas_call | solution.py:113
  27.7 3.1 %query_side.1 = (bf16[512,2048]{1,0:T(8,128)(2,1)S(1)}, bf16[512,2048]{1,0:T(8,128)(2,1)S(1)}, bf16[512,2048]{1,0:T(8,128)(2,1)S(1)}, bf16[384,2048]{1,0:T(8,128...) custom-call(s32[1]{0:T(128)S(6)} %copy.15.id_ref, ...), custom_call_target="tpu_custom_call" | custom-call | flops 1207959552 | tf_op jit(solution)/shard_map/query_side/pallas_call | solution.py:181
  30.8 2.0 %key_side.7 = (bf16[384,256]{1,0:T(8,128)(2,1)S(1)}, bf16[400,256]{1,0:T(8,128)(2,1)S(1)}) custom-call(f32[8,2048]{1,0:T(8,128)S(1)} %get-tuple-element.107.scale_ref, bf16[256,1024]{1,0:T(8,128)(2,1)S(1)} %get-tuple-element.68.q_ref, bf16[256,1024]{1,0:T(8,128)(2,1)S(1)} %get-tuple-element.69.g_ref, bf16[384,2048]{1,0:T(8,128)(2,1)S(1)} %get-tuple-element.117.refs_0_, ...), custom_call_target="tpu_custom_call" | custom-call | flops 805306368 | tf_op jit(solution)/shard_map/key_side/pallas_call | solution.py:252
  32.8 0.6 %collective-permute-start.11 = (bf16[400,256]{1,0:T(8,128)(2,1)S(1)}, bf16[400,256]{1,0:T(8,128)(2,1)S(1)}, u32[]{:S(2)}, u32[]{:S(2)}) collective-permute-start(bf16[400,256]{1,0:T(8,128)(2,1)S(1)} %get-tuple-element.119), channel_id=1, source_target_pairs={{0,8},{8,0},{16,24},{24,16},{32,40},{40,32},{48,56},{56,48},{64,72... | collective-permute-start | bytes 614408 | tf_op jit(solution)/shard_map/ppermute | solution.py:505
  33.4 1.5 %key_side.6 = bf16[512,256]{1,0:T(8,128)(2,1)S(1)} custom-call(f32[8,2048]{1,0:T(8,128)S(1)} %get-tuple-element.107.scale_ref, bf16[256,1024]{1,0:T(8,128)(2,1)S(1)} %get-tuple-element.68.q_ref, bf16[256,1024]{1,0:T(8,128)(2,1)S(1)} %get-tuple-element.69.g_ref, bf16[512,2048]{1,0:T(8,128)(2,1)S(1)} %get-tuple-element.115.refs_0_, ...), custom_call_target="tpu_custom_call" | custom-call | flops 536870912 | tf_op jit(solution)/shard_map/key_side/pallas_call | solution.py:252
  34.9 0.1 collective-permute-start.10
  35.0 0.0 collective-permute-done.11.mate_ref.got_ref
  35.0 0.1 pair_sum.3
  35.0 0.1 collective-permute-start.13
  35.1 0.1 collective-permute-start.14
  35.2 1.5 %key_side.5.direct_ref = bf16[512,256]{1,0:T(8,128)(2,1)S(1)} custom-call(f32[8,2048]{1,0:T(8,128)S(1)} %get-tuple-element.107.scale_ref, bf16[256,1024]{1,0:T(8,128)(2,1)S(1)} %get-tuple-element.68.q_ref, bf16[256,1024]{1,0:T(8,128)(2,1)S(1)} %get-tuple-element.69.g_ref, bf16[512,2048]{1,0:T(8,128)(2,1)S(1)} %get-tuple-element.114.refs_0_, ...), custom_call_target="tpu_custom_call" | custom-call | flops 536870912 | tf_op jit(solution)/shard_map/key_side/pallas_call | solution.py:252
  36.7 0.0 collective-permute-done.10.got_ref
  36.7 0.1 pair_sum.2
  36.8 3.6 %collective-permute-done.14.four_ref = bf16[144,256]{1,0:T(8,128)(2,1)S(1)} collective-permute-done((bf16[144,256]{1,0:T(8,128)(2,1)S(1)}, bf16[144,256]{1,0:T(8,128)(2,1)S(1)}, u32[]{:S(2)}, u32[]{:S(2)}) %collective-permute-start.14) | collective-permute-done | bytes 73760 | tf_op jit(solution)/shard_map/ppermute | solution.py:505
  40.4 0.3 collective-permute-done.13.three_ref
  40.7 1.9 %collective-permute-start.15 = (bf16[304,256]{1,0:T(8,128)(2,1)S(1)}, bf16[304,256]{1,0:T(8,128)(2,1)S(1)}, u32[]{:S(2)}, u32[]{:S(2)}) collective-permute-start(bf16[304,256]{1,0:T(8,128)(2,1)S(1)} %middle_sum.1), channel_id=1, source_target_pairs={{0,32},{8,104},{16,48},{24,120},{32,0},{40,72},{48,16},{56,88},{64... | collective-permute-start | bytes 466952 | tf_op jit(solution)/shard_map/ppermute | solution.py:505
  42.6 0.3 collective-permute-start.12
  42.9 2.8 %key_side.4 = (bf16[256,256]{1,0:T(8,128)(2,1)S(1)}, bf16[256,128]{1,0:T(8,128)(2,1)}, bf16[256,128]{1,0:T(8,128)(2,1)}, bf16[256,1024]{1,0:T(8,128)(2,1)}) custom-call(f32[8,2048]{1,0:T(8,128)S(1)} %get-tuple-element.107.scale_ref, bf16[256,1024]{1,0:T(8,128)(2,1)S(1)} %get-tuple-element.68.q_ref, bf16[256,1024]{1,0:T(8,128)(2,1)S(1)} %get-tuple-element.69.g_ref, ...), custom_call_target="tpu_custom_call" | custom-call | flops 536870912 | tf_op jit(solution)/shard_map/key_side/pallas_call | solution.py:252
  45.7 3.1 %collective-permute-done.12.one_ref = bf16[272,256]{1,0:T(8,128)(2,1)S(1)} collective-permute-done((bf16[272,256]{1,0:T(8,128)(2,1)S(1)}, bf16[272,256]{1,0:T(8,128)(2,1)S(1)}, u32[]{:S(2)}, u32[]{:S(2)}) %collective-permute-start.12) | collective-permute-done | bytes 139296 | tf_op jit(solution)/shard_map/ppermute | solution.py:505
  48.9 2.2 %collective-permute-start.16 = (bf16[192,256]{1,0:T(8,128)(2,1)S(1)}, bf16[192,256]{1,0:T(8,128)(2,1)S(1)}, u32[]{:S(2)}, u32[]{:S(2)}) collective-permute-start(bf16[192,256]{1,0:T(8,128)(2,1)S(1)} %get-tuple-element.126.sent_ref), channel_id=1, source_target_pairs={{0,8},{8,0},{16,24},{24,16},{32,40},{40,32},{48,56},{56,48},{64,72... | collective-permute-start | bytes 294920 | tf_op jit(solution)/shard_map/ppermute | solution.py:505
  51.1 0.9 %collective-permute-done.16.last_ref = bf16[192,256]{1,0:T(8,128)(2,1)S(1)} collective-permute-done((bf16[192,256]{1,0:T(8,128)(2,1)S(1)}, bf16[192,256]{1,0:T(8,128)(2,1)S(1)}, u32[]{:S(2)}, u32[]{:S(2)}) %collective-permute-start.16) | collective-permute-done | bytes 98336 | tf_op jit(solution)/shard_map/ppermute | solution.py:505
  52.0 0.8 %last_sum.1 = (bf16[128,128]{1,0:T(8,128)(2,1)}, bf16[128,128]{1,0:T(8,128)(2,1)}, f32[16,1024]{1,0:T(8,128)}) custom-call(f32[128,256]{1,0:T(8,128)S(1)} %get-tuple-element.125.mine_ref, bf16[192,256]{1,0:T(8,128)(2,1)S(1)} %get-tuple-element.126.sent_ref, bf16[192,256]{1,0:T(8,128)(2,1)S(1)} %collective-permute-done.16.last_ref, ...), custom_call_target="tpu_custom_call" | custom-call | tf_op jit(solution)/shard_map/last_sum/pallas_call | solution.py:472
  (5 shorter events, 0.1 us)
Async XLA Ops:
  0.6 4.4 %collective-permute-start = (bf16[128,128]{1,0:T(8,128)(2,1)}, bf16[128,128]{1,0:T(8,128)(2,1)S(1)}, u32[]{:S(2)}, u32[]{:S(2)}) collective-permute-start(bf16[128,128]{1,0:T(8,128)(2,1)} %k_ref.1), channel_id=1, source_target_pairs={{0,8},{8,0},{16,24},{24,16},{32,40},{40,32},{48,56},{56,48},{64,72... | collective-permute-start | bytes 98312 | tf_op jit(solution)/shard_map/ppermute | solution.py:505
  4.0 1.4 %collective-permute-start.1 = (bf16[128,128]{1,0:T(8,128)(2,1)}, bf16[128,128]{1,0:T(8,128)(2,1)S(1)}, u32[]{:S(2)}, u32[]{:S(2)}) collective-permute-start(bf16[128,128]{1,0:T(8,128)(2,1)} %v_ref.1), channel_id=1, source_target_pairs={{0,8},{8,0},{16,24},{24,16},{32,40},{40,32},{48,56},{56,48},{64,72... | collective-permute-start | bytes 98312 | tf_op jit(solution)/shard_map/ppermute | solution.py:505
  5.4 8.6 %collective-permute-start.2 = (bf16[256,256]{1,0:T(8,128)(2,1)S(1)}, bf16[256,256]{1,0:T(8,128)(2,1)S(1)}, u32[]{:S(2)}, u32[]{:S(2)}) collective-permute-start(bf16[256,256]{1,0:T(8,128)(2,1)S(1)} %assemble.1.refs_0_), channel_id=1, source_target_pairs={{0,32},{8,104},{16,48},{24,120},{32,0},{40,72},{48,16},{56,88},{64... | collective-permute-start | bytes 393224 | tf_op jit(solution)/shard_map/ppermute | solution.py:505
  9.8 5.0 %collective-permute-start.5 = (bf16[256,256]{1,0:T(8,128)(2,1)S(1)}, bf16[256,256]{1,0:T(8,128)(2,1)S(1)}, u32[]{:S(2)}, u32[]{:S(2)}) collective-permute-start(bf16[256,256]{1,0:T(8,128)(2,1)S(1)} %assemble.1.refs_0_), channel_id=1, source_target_pairs={{0,16},{8,120},{16,0},{24,40},{32,48},{40,24},{48,32},{56,72},{64,... | collective-permute-start | bytes 393224 | tf_op jit(solution)/shard_map/ppermute | solution.py:505
  14.8 4.1 %collective-permute-start.6 = (bf16[256,256]{1,0:T(8,128)(2,1)S(1)}, bf16[256,256]{1,0:T(8,128)(2,1)S(1)}, u32[]{:S(2)}, u32[]{:S(2)}) collective-permute-start(bf16[256,256]{1,0:T(8,128)(2,1)S(1)} %collective-permute-done.5.refs_0_), channel_id=1, source_target_pairs={{0,8},{8,0},{16,24},{24,16},{32,40},{40,32},{48,56},{56,48},{64,72... | collective-permute-start | bytes 393224 | tf_op jit(solution)/shard_map/ppermute | solution.py:505
  14.8 4.1 %collective-permute-start.7 = (bf16[256,256]{1,0:T(8,128)(2,1)S(1)}, bf16[256,256]{1,0:T(8,128)(2,1)S(1)}, u32[]{:S(2)}, u32[]{:S(2)}) collective-permute-start(bf16[256,256]{1,0:T(8,128)(2,1)S(1)} %collective-permute-done.2.refs_1_), channel_id=1, source_target_pairs={{0,8},{8,0},{16,24},{24,16},{32,40},{40,32},{48,56},{56,48},{64,72... | collective-permute-start | bytes 393224 | tf_op jit(solution)/shard_map/ppermute | solution.py:505
  15.3 5.8 %collective-permute-start.3 = (bf16[256,256]{1,0:T(8,128)(2,1)S(1)}, bf16[256,256]{1,0:T(8,128)(2,1)S(1)}, u32[]{:S(2)}, u32[]{:S(2)}) collective-permute-start(bf16[256,256]{1,0:T(8,128)(2,1)S(1)} %collective-permute-done.2.refs_1_), channel_id=1, source_target_pairs={{0,112},{8,16},{16,8},{24,40},{32,56},{40,24},{48,64},{56,32},{64,... | collective-permute-start | bytes 393224 | tf_op jit(solution)/shard_map/ppermute | solution.py:505
  16.1 5.0 %collective-permute-start.4 = (bf16[128,256]{1,0:T(8,128)(2,1)S(1)}, bf16[128,256]{1,0:T(8,128)(2,1)S(1)}, u32[]{:S(2)}, u32[]{:S(2)}) collective-permute-start(bf16[128,256]{1,0:T(8,128)(2,1)S(1)} %slice.3), channel_id=1, source_target_pairs={{0,96},{8,40},{16,112},{24,56},{32,64},{40,8},{48,80},{56,24},{64,... | collective-permute-start | bytes 196616 | tf_op jit(solution)/shard_map/ppermute | solution.py:505
  21.1 5.2 %collective-permute-start.8 = (bf16[256,256]{1,0:T(8,128)(2,1)S(1)}, bf16[256,256]{1,0:T(8,128)(2,1)S(1)}, u32[]{:S(2)}, u32[]{:S(2)}) collective-permute-start(bf16[256,256]{1,0:T(8,128)(2,1)S(1)} %collective-permute-done.3.refs_0_), channel_id=1, source_target_pairs={{0,8},{8,0},{16,24},{24,16},{32,40},{40,32},{48,56},{56,48},{64,72... | collective-permute-start | bytes 393224 | tf_op jit(solution)/shard_map/ppermute | solution.py:505
  24.8 1.5 %collective-permute-start.9 = (bf16[128,256]{1,0:T(8,128)(2,1)S(1)}, bf16[128,256]{1,0:T(8,128)(2,1)S(1)}, u32[]{:S(2)}, u32[]{:S(2)}) collective-permute-start(bf16[128,256]{1,0:T(8,128)(2,1)S(1)} %collective-permute-done.4.refs_1_), channel_id=1, source_target_pairs={{0,8},{8,0},{16,24},{24,16},{32,40},{40,32},{48,56},{56,48},{64,72... | collective-permute-start | bytes 196616 | tf_op jit(solution)/shard_map/ppermute | solution.py:505
  32.8 2.2 %collective-permute-start.11 = (bf16[400,256]{1,0:T(8,128)(2,1)S(1)}, bf16[400,256]{1,0:T(8,128)(2,1)S(1)}, u32[]{:S(2)}, u32[]{:S(2)}) collective-permute-start(bf16[400,256]{1,0:T(8,128)(2,1)S(1)} %get-tuple-element.119), channel_id=1, source_target_pairs={{0,8},{8,0},{16,24},{24,16},{32,40},{40,32},{48,56},{56,48},{64,72... | collective-permute-start | bytes 614408 | tf_op jit(solution)/shard_map/ppermute | solution.py:505
  34.9 1.8 %collective-permute-start.10 = (bf16[512,256]{1,0:T(8,128)(2,1)S(1)}, bf16[512,256]{1,0:T(8,128)(2,1)S(1)}, u32[]{:S(2)}, u32[]{:S(2)}) collective-permute-start(bf16[512,256]{1,0:T(8,128)(2,1)S(1)} %key_side.6), channel_id=1, source_target_pairs={{0,8},{8,0},{16,24},{24,16},{32,40},{40,32},{48,56},{56,48},{64,72... | collective-permute-start | bytes 786440 | tf_op jit(solution)/shard_map/ppermute | solution.py:505
  35.0 5.7 %collective-permute-start.13 = (bf16[272,256]{1,0:T(8,128)(2,1)S(1)}, bf16[272,256]{1,0:T(8,128)(2,1)S(1)}, u32[]{:S(2)}, u32[]{:S(2)}) collective-permute-start(bf16[272,256]{1,0:T(8,128)(2,1)S(1)} %get-tuple-element.123), channel_id=1, source_target_pairs={{0,112},{8,16},{16,8},{24,40},{32,56},{40,24},{48,64},{56,32},{64,... | collective-permute-start | bytes 417800 | tf_op jit(solution)/shard_map/ppermute | solution.py:505
  35.1 5.3 %collective-permute-start.14 = (bf16[144,256]{1,0:T(8,128)(2,1)S(1)}, bf16[144,256]{1,0:T(8,128)(2,1)S(1)}, u32[]{:S(2)}, u32[]{:S(2)}) collective-permute-start(bf16[144,256]{1,0:T(8,128)(2,1)S(1)} %get-tuple-element.124), channel_id=1, source_target_pairs={{0,96},{8,40},{16,112},{24,56},{32,64},{40,8},{48,80},{56,24},{64,... | collective-permute-start | bytes 221192 | tf_op jit(solution)/shard_map/ppermute | solution.py:505
  40.7 8.1 %collective-permute-start.15 = (bf16[304,256]{1,0:T(8,128)(2,1)S(1)}, bf16[304,256]{1,0:T(8,128)(2,1)S(1)}, u32[]{:S(2)}, u32[]{:S(2)}) collective-permute-start(bf16[304,256]{1,0:T(8,128)(2,1)S(1)} %middle_sum.1), channel_id=1, source_target_pairs={{0,32},{8,104},{16,48},{24,120},{32,0},{40,72},{48,16},{56,88},{64... | collective-permute-start | bytes 466952 | tf_op jit(solution)/shard_map/ppermute | solution.py:505
  42.6 6.2 %collective-permute-start.12 = (bf16[272,256]{1,0:T(8,128)(2,1)S(1)}, bf16[272,256]{1,0:T(8,128)(2,1)S(1)}, u32[]{:S(2)}, u32[]{:S(2)}) collective-permute-start(bf16[272,256]{1,0:T(8,128)(2,1)S(1)} %get-tuple-element.120), channel_id=1, source_target_pairs={{0,16},{8,120},{16,0},{24,40},{32,48},{40,24},{48,32},{56,72},{64,... | collective-permute-start | bytes 417800 | tf_op jit(solution)/shard_map/ppermute | solution.py:505
  48.9 3.2 %collective-permute-start.16 = (bf16[192,256]{1,0:T(8,128)(2,1)S(1)}, bf16[192,256]{1,0:T(8,128)(2,1)S(1)}, u32[]{:S(2)}, u32[]{:S(2)}) collective-permute-start(bf16[192,256]{1,0:T(8,128)(2,1)S(1)} %get-tuple-element.126.sent_ref), channel_id=1, source_target_pairs={{0,8},{8,0},{16,24},{24,16},{32,40},{40,32},{48,56},{56,48},{64,72... | collective-permute-start | bytes 294920 | tf_op jit(solution)/shard_map/ppermute | solution.py:505

commit v4 on v3

--- a/solution.py
+++ b/solution.py
@@ -75,31 +75,31 @@
             key_pos = lax.broadcasted_iota(jnp.int32, (n, rows), 0)
             query_pos = lax.broadcasted_iota(jnp.int32, (n, rows), 1)
             s = jnp.where(key_pos <= query_pos, s, -1e30)
-        score_refs[head % 2][at : at + n, :] = s
+        score_refs[head % 3][at : at + n, :] = s
         return jnp.maximum(top, jnp.max(s.reshape(n // 8, 8, rows), axis=0))
 
     lowest = jnp.full((8, rows), -1e30, F32)
     heads = q_ref.shape[1] // HEAD_DIM
-    top = lowest
-    for piece in pieces:
-        top = score(0, piece, top)
+    tops = [lowest] * heads
+    for head in range(2):
+        for piece in pieces:
+            tops[head] = score(head, piece, tops[head])
     for head in range(heads):
         cols = slice(head * rows, (head + 1) * rows)
         g = g_ref[:, head * HEAD_DIM : (head + 1) * HEAD_DIM]
-        row_max = jnp.max(top, axis=0, keepdims=True) * factor
+        row_max = jnp.max(tops[head], axis=0, keepdims=True) * factor
         total = jnp.zeros((8, rows), F32)
         dot = jnp.zeros((8, rows), F32)
-        top = lowest
         for piece in pieces:
             at, n, _, value_ref, _ = piece
-            p = jnp.exp2(score_refs[head % 2][at : at + n, :] * factor - row_max)
+            p = jnp.exp2(score_refs[head % 3][at : at + n, :] * factor - row_max)
             dp = lax.dot_general(value_ref[...], g, NT, preferred_element_type=F32)
             total = total + jnp.sum(p.reshape(n // 8, 8, rows), axis=0)
             dot = dot + jnp.sum((p * dp).reshape(n // 8, 8, rows), axis=0)
             low_ref[at : at + n, cols] = p.astype(BF16)
             dp_ref[at : at + n, cols] = dp
-            if head + 1 < heads:
-                top = score(head + 1, piece, top)
+            if head + 2 < heads:
+                tops[head + 2] = score(head + 2, piece, tops[head + 2])
         stat_ref[0:1, cols] = row_max
         stat_ref[1:2, cols] = jnp.sum(total, axis=0, keepdims=True)
         stat_ref[2:3, cols] = jnp.sum(dot, axis=0, keepdims=True)
@@ -120,7 +120,7 @@
         ],
         in_specs=[VMEM] * (2 + len(blocks) + len(resp)),
         out_specs=[VMEM] * 4,
-        scratch_shapes=[pltpu.VMEM((n, rows), F32)] * 2,
+        scratch_shapes=[pltpu.VMEM((n, rows), F32)] * 3,
         compiler_params=SMALL,
         cost_estimate=pl.CostEstimate(
             flops=4 * n * queries * HEAD_DIM, bytes_accessed=0, transcendentals=n * queries
@@ -540,11 +540,12 @@
     one, two = pair_sum(
         direct_close, move(via_close, pair), r_tile, got, (2 * block, 2 * block), (2, 0)
     )
-    near, resp_key_grad, resp_value_grad, query_grad = keys_of((0,), True, query_grad)
     four = move(four, to_four)
     three = move(three, to_three)
     one = move(one, to_one)
     two = move(middle_sum(two, three, four, r_tile, got), to_two)
+    scale, one = lax.optimization_barrier((scale, one))
+    near, resp_key_grad, resp_value_grad, query_grad = keys_of((0,), True, query_grad)
     mine, sent = chip_sum(near, one, two)
     last = move(sent, pair)
     prompt_key_grad, prompt_value_grad, pref_grad = last_sum(

time: 53 us -> 51.4 us (0.970)
  waiting for transfers between devices: 9.84 us -> 5.19 us
  starting transfers between devices: 19.2 us -> 22.6 us
    ppermute x17, waiting for transfers between devices: 9.84 us -> 5.19 us  [move(): return lax.ppermute(array, 'resp', moves)]
    ppermute x17, starting transfers between devices: 19.2 us -> 22.6 us  [move(): return lax.ppermute(array, 'resp', moves)]
  transfers between devices with their start and end apart: 17 -> 17, of which waited for: 8 -> 9; matrix products, arithmetic and copies ran while one was open for 0% -> 0% of each run, Pallas kernels for 27% -> 28%
where the time goes in v4:
time: 51.4 us; the launch traced here: 51.2 us
  starting transfers between devices  22.6 us (44%)
  Pallas kernels  21.3 us (41%)
  waiting for transfers between devices  5.19 us (10%)
  between operations  2.12 us (4%)
    ppermute x17, starting transfers between devices, move(): return lax.ppermute(array, 'resp', moves)  22.6 us
    pallas_call x4, Pallas kernels, key_side(): pl.pallas_call(functools.partial(key_kernel, picks, len(extra)), out_shap...  7.68 us
    pallas_call x5, Pallas kernels, scores(): pl.pallas_call(functools.partial(scores_kernel, len(blocks), bool(resp)),...  7.49 us
    ppermute x17, waiting for transfers between devices, move(): return lax.ppermute(array, 'resp', moves)  5.19 us
    pallas_call x1, Pallas kernels, query_side(): pl.pallas_call(functools.partial(query_kernel, count), out_shape=[shape(l...  3.05 us
    pallas_call x1, Pallas kernels, prepare(): pl.pallas_call(prepare_kernel, out_shape=[wide, wide, slim, slim], in_spe...  1.31 us
  transfers between devices with their start and end apart: 17, of which 9 were waited for; matrix products, arithmetic and copies ran while one was open for 0% of the time, Pallas kernels for 28%

profile of v4, /device:TPU:1, one launch (start us, length us, event | category | flops | bytes accessed | tf_op | source)
XLA Modules:
  0.0 51.2 jit_solution(4882881631978865851)
XLA Ops:
  0.6 3.3 %collective-permute-start = (bf16[128,128]{1,0:T(8,128)(2,1)}, bf16[128,128]{1,0:T(8,128)(2,1)S(1)}, u32[]{:S(2)}, u32[]{:S(2)}) collective-permute-start(bf16[128,128]{1,0:T(8,128)(2,1)} %k_ref.1), channel_id=1, source_target_pairs={{0,8},{8,0},{16,24},{24,16},{32,40},{40,32},{48,56},{56,48},{64,72... | collective-permute-start | bytes 98312 | tf_op jit(solution)/shard_map/ppermute | solution.py:505
  4.0 0.1 collective-permute-start.1
  4.1 0.8 %pack.1.own_ref = bf16[128,256]{1,0:T(8,128)(2,1)S(1)} custom-call(bf16[128,128]{1,0:T(8,128)(2,1)} %k_ref.1, bf16[128,128]{1,0:T(8,128)(2,1)} %v_ref.1), custom_call_target="tpu_custom_call" | custom-call | tf_op jit(solution)/shard_map/pack/pallas_call | solution.py:279
  4.9 0.2 collective-permute-done.k_ref
  5.0 0.3 collective-permute-done.1.v_ref
  5.4 4.4 %collective-permute-start.2 = (bf16[256,256]{1,0:T(8,128)(2,1)S(1)}, bf16[256,256]{1,0:T(8,128)(2,1)S(1)}, u32[]{:S(2)}, u32[]{:S(2)}) collective-permute-start(bf16[256,256]{1,0:T(8,128)(2,1)S(1)} %assemble.1.refs_0_), channel_id=1, source_target_pairs={{0,32},{8,104},{16,48},{24,120},{32,0},{40,72},{48,16},{56,88},{64... | collective-permute-start | bytes 393224 | tf_op jit(solution)/shard_map/ppermute | solution.py:505
  9.8 0.0 collective-permute-start.5
  11.1 1.3 %prepare.1 = (bf16[256,1024]{1,0:T(8,128)(2,1)S(1)}, bf16[256,1024]{1,0:T(8,128)(2,1)S(1)}, bf16[256,128]{1,0:T(8,128)(2,1)S(1)}, bf16[256,128]{1,0:T(8,128)(2,1)S(1)}) custom-call(s32[1]{0:T(128)S(6)} %copy.15.id_ref, s32[1]{0:T(128)S(6)} %copy.16.len_ref, bf16[256,1024]{1,0:T(8,128)(2,1)} %q_hbm.1, bf16[256,1024]{1,0:T(8,128)(2,1)} %g_hbm.1, ...), custom_call_target="tpu_custom_call" | custom-call | flops 1048576 | bytes 2097152 | tf_op jit(solution)/shard_map/prepare/pallas_call | solution.py:348
  12.4 1.6 %scores.5 = (bf16[512,2048]{1,0:T(8,128)(2,1)S(1)}, f32[512,2048]{1,0:T(8,128)S(1)}, f32[8,2048]{1,0:T(8,128)S(1)}, bf16[128,512]{1,0:T(8,128)(2,1)S(1)}) custom-call(bf16[256,1024]{1,0:T(8,128)(2,1)S(1)} %get-tuple-element.70.q_ref, bf16[256,1024]{1,0:T(8,128)(2,1)S(1)} %get-tuple-element.71.g_ref, bf16[256,256]{1,0:T(8,128)(2,1)S(1)} %assemble.1.refs_0_, ...), custom_call_target="tpu_custom_call" | custom-call | flops 536870912 | tf_op jit(solution)/shard_map/scores/pallas_call | solution.py:113
  14.0 0.0 collective-permute-done.2.refs_1_
  14.0 0.8 %collective-permute-done.5.refs_0_ = bf16[256,256]{1,0:T(8,128)(2,1)S(1)} collective-permute-done((bf16[256,256]{1,0:T(8,128)(2,1)S(1)}, bf16[256,256]{1,0:T(8,128)(2,1)S(1)}, u32[]{:S(2)}, u32[]{:S(2)}) %collective-permute-start.5) | collective-permute-done | bytes 131104 | tf_op jit(solution)/shard_map/ppermute | solution.py:505
  14.8 0.0 collective-permute-start.6
  14.8 0.5 collective-permute-start.7
  15.3 0.7 %collective-permute-start.3 = (bf16[256,256]{1,0:T(8,128)(2,1)S(1)}, bf16[256,256]{1,0:T(8,128)(2,1)S(1)}, u32[]{:S(2)}, u32[]{:S(2)}) collective-permute-start(bf16[256,256]{1,0:T(8,128)(2,1)S(1)} %collective-permute-done.2.refs_1_), channel_id=1, source_target_pairs={{0,112},{8,16},{16,8},{24,40},{32,56},{40,24},{48,64},{56,32},{64,... | collective-permute-start | bytes 393224 | tf_op jit(solution)/shard_map/ppermute | solution.py:505
  16.1 1.2 %collective-permute-start.4 = (bf16[128,256]{1,0:T(8,128)(2,1)S(1)}, bf16[128,256]{1,0:T(8,128)(2,1)S(1)}, u32[]{:S(2)}, u32[]{:S(2)}) collective-permute-start(bf16[128,256]{1,0:T(8,128)(2,1)S(1)} %slice.3), channel_id=1, source_target_pairs={{0,96},{8,40},{16,112},{24,56},{32,64},{40,8},{48,80},{56,24},{64,... | collective-permute-start | bytes 196616 | tf_op jit(solution)/shard_map/ppermute | solution.py:505
  17.3 1.6 %scores.6 = (bf16[512,2048]{1,0:T(8,128)(2,1)S(1)}, f32[512,2048]{1,0:T(8,128)S(1)}, f32[8,2048]{1,0:T(8,128)S(1)}, bf16[128,512]{1,0:T(8,128)(2,1)S(1)}) custom-call(bf16[256,1024]{1,0:T(8,128)(2,1)S(1)} %get-tuple-element.70.q_ref, bf16[256,1024]{1,0:T(8,128)(2,1)S(1)} %get-tuple-element.71.g_ref, bf16[256,256]{1,0:T(8,128)(2,1)S(1)} %collective-permute-done.5.refs_0_, ...), custom_call_target="tpu_custom_call" | custom-call | flops 536870912 | tf_op jit(solution)/shard_map/scores/pallas_call | solution.py:113
  18.9 0.0 collective-permute-done.6.refs_0_
  18.9 0.0 collective-permute-done.7.refs_1_
  18.9 1.7 %scores.7 = (bf16[512,2048]{1,0:T(8,128)(2,1)S(1)}, f32[512,2048]{1,0:T(8,128)S(1)}, f32[8,2048]{1,0:T(8,128)S(1)}, bf16[128,512]{1,0:T(8,128)(2,1)S(1)}) custom-call(bf16[256,1024]{1,0:T(8,128)(2,1)S(1)} %get-tuple-element.70.q_ref, bf16[256,1024]{1,0:T(8,128)(2,1)S(1)} %get-tuple-element.71.g_ref, bf16[256,256]{1,0:T(8,128)(2,1)S(1)} %collective-permute-done.6.refs_0_, ...), custom_call_target="tpu_custom_call" | custom-call | flops 536870912 | tf_op jit(solution)/shard_map/scores/pallas_call | solution.py:113
  20.6 0.5 collective-permute-done.4.refs_1_
  21.1 0.0 collective-permute-done.3.refs_0_
  21.1 3.7 %collective-permute-start.8 = (bf16[256,256]{1,0:T(8,128)(2,1)S(1)}, bf16[256,256]{1,0:T(8,128)(2,1)S(1)}, u32[]{:S(2)}, u32[]{:S(2)}) collective-permute-start(bf16[256,256]{1,0:T(8,128)(2,1)S(1)} %collective-permute-done.3.refs_0_), channel_id=1, source_target_pairs={{0,8},{8,0},{16,24},{24,16},{32,40},{40,32},{48,56},{56,48},{64,72... | collective-permute-start | bytes 393224 | tf_op jit(solution)/shard_map/ppermute | solution.py:505
  24.8 0.0 collective-permute-start.9
  24.8 1.3 %scores.8 = (bf16[384,2048]{1,0:T(8,128)(2,1)S(1)}, f32[384,2048]{1,0:T(8,128)S(1)}, f32[8,2048]{1,0:T(8,128)S(1)}, bf16[128,384]{1,0:T(8,128)(2,1)S(1)}) custom-call(bf16[256,1024]{1,0:T(8,128)(2,1)S(1)} %get-tuple-element.70.q_ref, bf16[256,1024]{1,0:T(8,128)(2,1)S(1)} %get-tuple-element.71.g_ref, bf16[256,256]{1,0:T(8,128)(2,1)S(1)} %collective-permute-done.3.refs_0_, ...), custom_call_target="tpu_custom_call" | custom-call | flops 402653184 | tf_op jit(solution)/shard_map/scores/pallas_call | solution.py:113
  26.1 0.0 collective-permute-done.9.refs_1_
  26.1 1.3 %scores.9 = (bf16[384,2048]{1,0:T(8,128)(2,1)S(1)}, f32[384,2048]{1,0:T(8,128)S(1)}, f32[8,2048]{1,0:T(8,128)S(1)}, bf16[128,384]{1,0:T(8,128)(2,1)S(1)}) custom-call(bf16[256,1024]{1,0:T(8,128)(2,1)S(1)} %get-tuple-element.70.q_ref, bf16[256,1024]{1,0:T(8,128)(2,1)S(1)} %get-tuple-element.71.g_ref, bf16[256,256]{1,0:T(8,128)(2,1)S(1)} %collective-permute-done.8.refs_0_, ...), custom_call_target="tpu_custom_call" | custom-call | flops 402653184 | tf_op jit(solution)/shard_map/scores/pallas_call | solution.py:113
  27.4 3.1 %query_side.1 = (bf16[512,2048]{1,0:T(8,128)(2,1)S(1)}, bf16[512,2048]{1,0:T(8,128)(2,1)S(1)}, bf16[512,2048]{1,0:T(8,128)(2,1)S(1)}, bf16[384,2048]{1,0:T(8,128...) custom-call(s32[1]{0:T(128)S(6)} %copy.15.id_ref, ...), custom_call_target="tpu_custom_call" | custom-call | flops 1207959552 | tf_op jit(solution)/shard_map/query_side/pallas_call | solution.py:181
  30.5 2.0 %key_side.6 = (bf16[384,256]{1,0:T(8,128)(2,1)S(1)}, bf16[400,256]{1,0:T(8,128)(2,1)S(1)}) custom-call(f32[8,2048]{1,0:T(8,128)S(1)} %get-tuple-element.117.scale_ref, bf16[256,1024]{1,0:T(8,128)(2,1)S(1)} %get-tuple-element.70.q_ref, bf16[256,1024]{1,0:T(8,128)(2,1)S(1)} %get-tuple-element.71.g_ref, bf16[384,2048]{1,0:T(8,128)(2,1)S(1)} %get-tuple-element.113.refs_0_, ...), custom_call_target="tpu_custom_call" | custom-call | flops 805306368 | tf_op jit(solution)/shard_map/key_side/pallas_call | solution.py:252
  32.5 0.6 %collective-permute-start.11 = (bf16[400,256]{1,0:T(8,128)(2,1)S(1)}, bf16[400,256]{1,0:T(8,128)(2,1)S(1)}, u32[]{:S(2)}, u32[]{:S(2)}) collective-permute-start(bf16[400,256]{1,0:T(8,128)(2,1)S(1)} %get-tuple-element.115), channel_id=1, source_target_pairs={{0,8},{8,0},{16,24},{24,16},{32,40},{40,32},{48,56},{56,48},{64,72... | collective-permute-start | bytes 614408 | tf_op jit(solution)/shard_map/ppermute | solution.py:505
  33.1 1.5 %key_side.5 = bf16[512,256]{1,0:T(8,128)(2,1)S(1)} custom-call(f32[8,2048]{1,0:T(8,128)S(1)} %get-tuple-element.117.scale_ref, bf16[256,1024]{1,0:T(8,128)(2,1)S(1)} %get-tuple-element.70.q_ref, bf16[256,1024]{1,0:T(8,128)(2,1)S(1)} %get-tuple-element.71.g_ref, bf16[512,2048]{1,0:T(8,128)(2,1)S(1)} %get-tuple-element.111.refs_0_, ...), custom_call_target="tpu_custom_call" | custom-call | flops 536870912 | tf_op jit(solution)/shard_map/key_side/pallas_call | solution.py:252
  34.6 0.1 collective-permute-start.10
  34.7 0.0 collective-permute-done.11.mate_ref.got_ref
  34.7 0.1 pair_sum.3
  34.7 0.1 collective-permute-start.13
  34.8 0.1 collective-permute-start.14
  34.9 1.5 %key_side.4.direct_ref = bf16[512,256]{1,0:T(8,128)(2,1)S(1)} custom-call(f32[8,2048]{1,0:T(8,128)S(1)} %get-tuple-element.117.scale_ref, bf16[256,1024]{1,0:T(8,128)(2,1)S(1)} %get-tuple-element.70.q_ref, bf16[256,1024]{1,0:T(8,128)(2,1)S(1)} %get-tuple-element.71.g_ref, bf16[512,2048]{1,0:T(8,128)(2,1)S(1)} %get-tuple-element.110.refs_0_, ...), custom_call_target="tpu_custom_call" | custom-call | flops 536870912 | tf_op jit(solution)/shard_map/key_side/pallas_call | solution.py:252
  36.4 0.1 pair_sum.2
  36.5 3.2 %collective-permute-start.12 = (bf16[272,256]{1,0:T(8,128)(2,1)S(1)}, bf16[272,256]{1,0:T(8,128)(2,1)S(1)}, u32[]{:S(2)}, u32[]{:S(2)}) collective-permute-start(bf16[272,256]{1,0:T(8,128)(2,1)S(1)} %get-tuple-element.116), channel_id=1, source_target_pairs={{0,16},{8,120},{16,0},{24,40},{32,48},{40,24},{48,32},{56,72},{64,... | collective-permute-start | bytes 417800 | tf_op jit(solution)/shard_map/ppermute | solution.py:505
  39.7 0.4 collective-permute-done.14.four_ref
  40.1 0.3 collective-permute-done.13.three_ref
  40.4 1.9 %collective-permute-start.15 = (bf16[304,256]{1,0:T(8,128)(2,1)S(1)}, bf16[304,256]{1,0:T(8,128)(2,1)S(1)}, u32[]{:S(2)}, u32[]{:S(2)}) collective-permute-start(bf16[304,256]{1,0:T(8,128)(2,1)S(1)} %middle_sum.1), channel_id=1, source_target_pairs={{0,32},{8,104},{16,48},{24,120},{32,0},{40,72},{48,16},{56,88},{64... | collective-permute-start | bytes 466952 | tf_op jit(solution)/shard_map/ppermute | solution.py:505
  42.3 1.6 %collective-permute-done.12.one_ref = bf16[272,256]{1,0:T(8,128)(2,1)S(1)} collective-permute-done((bf16[272,256]{1,0:T(8,128)(2,1)S(1)}, bf16[272,256]{1,0:T(8,128)(2,1)S(1)}, u32[]{:S(2)}, u32[]{:S(2)}) %collective-permute-start.12) | collective-permute-done | bytes 139296 | tf_op jit(solution)/shard_map/ppermute | solution.py:505
  43.9 2.8 %key_side.7 = (bf16[256,256]{1,0:T(8,128)(2,1)S(1)}, bf16[256,128]{1,0:T(8,128)(2,1)}, bf16[256,128]{1,0:T(8,128)(2,1)}, bf16[256,1024]{1,0:T(8,128)(2,1)}) custom-call(f32[8,2048]{1,0:T(8,128)S(1)} %get-tuple-element.117.scale_ref, bf16[256,1024]{1,0:T(8,128)(2,1)S(1)} %get-tuple-element.70.q_ref, bf16[256,1024]{1,0:T(8,128)(2,1)S(1)} %get-tuple-element.71.g_ref, ...), custom_call_target="tpu_custom_call" | custom-call | flops 536870912 | tf_op jit(solution)/shard_map/key_side/pallas_call | solution.py:252
  46.7 0.1 collective-permute-done.15.two_ref
  46.8 0.1 chip_sum.1
  46.9 2.6 %collective-permute-start.16 = (bf16[192,256]{1,0:T(8,128)(2,1)S(1)}, bf16[192,256]{1,0:T(8,128)(2,1)S(1)}, u32[]{:S(2)}, u32[]{:S(2)}) collective-permute-start(bf16[192,256]{1,0:T(8,128)(2,1)S(1)} %get-tuple-element.130.sent_ref), channel_id=1, source_target_pairs={{0,8},{8,0},{16,24},{24,16},{32,40},{40,32},{48,56},{56,48},{64,72... | collective-permute-start | bytes 294920 | tf_op jit(solution)/shard_map/ppermute | solution.py:505
  49.5 0.9 %collective-permute-done.16.last_ref = bf16[192,256]{1,0:T(8,128)(2,1)S(1)} collective-permute-done((bf16[192,256]{1,0:T(8,128)(2,1)S(1)}, bf16[192,256]{1,0:T(8,128)(2,1)S(1)}, u32[]{:S(2)}, u32[]{:S(2)}) %collective-permute-start.16) | collective-permute-done | bytes 98336 | tf_op jit(solution)/shard_map/ppermute | solution.py:505
  50.4 0.8 %last_sum.1 = (bf16[128,128]{1,0:T(8,128)(2,1)}, bf16[128,128]{1,0:T(8,128)(2,1)}, f32[16,1024]{1,0:T(8,128)}) custom-call(f32[128,256]{1,0:T(8,128)S(1)} %get-tuple-element.129.mine_ref, bf16[192,256]{1,0:T(8,128)(2,1)S(1)} %get-tuple-element.130.sent_ref, bf16[192,256]{1,0:T(8,128)(2,1)S(1)} %collective-permute-done.16.last_ref, ...), custom_call_target="tpu_custom_call" | custom-call | tf_op jit(solution)/shard_map/last_sum/pallas_call | solution.py:472
  (5 shorter events, 0.1 us)
Async XLA Ops:
  0.6 4.4 %collective-permute-start = (bf16[128,128]{1,0:T(8,128)(2,1)}, bf16[128,128]{1,0:T(8,128)(2,1)S(1)}, u32[]{:S(2)}, u32[]{:S(2)}) collective-permute-start(bf16[128,128]{1,0:T(8,128)(2,1)} %k_ref.1), channel_id=1, source_target_pairs={{0,8},{8,0},{16,24},{24,16},{32,40},{40,32},{48,56},{56,48},{64,72... | collective-permute-start | bytes 98312 | tf_op jit(solution)/shard_map/ppermute | solution.py:505
  4.0 1.4 %collective-permute-start.1 = (bf16[128,128]{1,0:T(8,128)(2,1)}, bf16[128,128]{1,0:T(8,128)(2,1)S(1)}, u32[]{:S(2)}, u32[]{:S(2)}) collective-permute-start(bf16[128,128]{1,0:T(8,128)(2,1)} %v_ref.1), channel_id=1, source_target_pairs={{0,8},{8,0},{16,24},{24,16},{32,40},{40,32},{48,56},{56,48},{64,72... | collective-permute-start | bytes 98312 | tf_op jit(solution)/shard_map/ppermute | solution.py:505
  5.4 8.6 %collective-permute-start.2 = (bf16[256,256]{1,0:T(8,128)(2,1)S(1)}, bf16[256,256]{1,0:T(8,128)(2,1)S(1)}, u32[]{:S(2)}, u32[]{:S(2)}) collective-permute-start(bf16[256,256]{1,0:T(8,128)(2,1)S(1)} %assemble.1.refs_0_), channel_id=1, source_target_pairs={{0,32},{8,104},{16,48},{24,120},{32,0},{40,72},{48,16},{56,88},{64... | collective-permute-start | bytes 393224 | tf_op jit(solution)/shard_map/ppermute | solution.py:505
  9.8 5.0 %collective-permute-start.5 = (bf16[256,256]{1,0:T(8,128)(2,1)S(1)}, bf16[256,256]{1,0:T(8,128)(2,1)S(1)}, u32[]{:S(2)}, u32[]{:S(2)}) collective-permute-start(bf16[256,256]{1,0:T(8,128)(2,1)S(1)} %assemble.1.refs_0_), channel_id=1, source_target_pairs={{0,16},{8,120},{16,0},{24,40},{32,48},{40,24},{48,32},{56,72},{64,... | collective-permute-start | bytes 393224 | tf_op jit(solution)/shard_map/ppermute | solution.py:505
  14.8 4.1 %collective-permute-start.6 = (bf16[256,256]{1,0:T(8,128)(2,1)S(1)}, bf16[256,256]{1,0:T(8,128)(2,1)S(1)}, u32[]{:S(2)}, u32[]{:S(2)}) collective-permute-start(bf16[256,256]{1,0:T(8,128)(2,1)S(1)} %collective-permute-done.5.refs_0_), channel_id=1, source_target_pairs={{0,8},{8,0},{16,24},{24,16},{32,40},{40,32},{48,56},{56,48},{64,72... | collective-permute-start | bytes 393224 | tf_op jit(solution)/shard_map/ppermute | solution.py:505
  14.8 4.1 %collective-permute-start.7 = (bf16[256,256]{1,0:T(8,128)(2,1)S(1)}, bf16[256,256]{1,0:T(8,128)(2,1)S(1)}, u32[]{:S(2)}, u32[]{:S(2)}) collective-permute-start(bf16[256,256]{1,0:T(8,128)(2,1)S(1)} %collective-permute-done.2.refs_1_), channel_id=1, source_target_pairs={{0,8},{8,0},{16,24},{24,16},{32,40},{40,32},{48,56},{56,48},{64,72... | collective-permute-start | bytes 393224 | tf_op jit(solution)/shard_map/ppermute | solution.py:505
  15.3 5.8 %collective-permute-start.3 = (bf16[256,256]{1,0:T(8,128)(2,1)S(1)}, bf16[256,256]{1,0:T(8,128)(2,1)S(1)}, u32[]{:S(2)}, u32[]{:S(2)}) collective-permute-start(bf16[256,256]{1,0:T(8,128)(2,1)S(1)} %collective-permute-done.2.refs_1_), channel_id=1, source_target_pairs={{0,112},{8,16},{16,8},{24,40},{32,56},{40,24},{48,64},{56,32},{64,... | collective-permute-start | bytes 393224 | tf_op jit(solution)/shard_map/ppermute | solution.py:505
  16.1 5.0 %collective-permute-start.4 = (bf16[128,256]{1,0:T(8,128)(2,1)S(1)}, bf16[128,256]{1,0:T(8,128)(2,1)S(1)}, u32[]{:S(2)}, u32[]{:S(2)}) collective-permute-start(bf16[128,256]{1,0:T(8,128)(2,1)S(1)} %slice.3), channel_id=1, source_target_pairs={{0,96},{8,40},{16,112},{24,56},{32,64},{40,8},{48,80},{56,24},{64,... | collective-permute-start | bytes 196616 | tf_op jit(solution)/shard_map/ppermute | solution.py:505
  21.1 5.0 %collective-permute-start.8 = (bf16[256,256]{1,0:T(8,128)(2,1)S(1)}, bf16[256,256]{1,0:T(8,128)(2,1)S(1)}, u32[]{:S(2)}, u32[]{:S(2)}) collective-permute-start(bf16[256,256]{1,0:T(8,128)(2,1)S(1)} %collective-permute-done.3.refs_0_), channel_id=1, source_target_pairs={{0,8},{8,0},{16,24},{24,16},{32,40},{40,32},{48,56},{56,48},{64,72... | collective-permute-start | bytes 393224 | tf_op jit(solution)/shard_map/ppermute | solution.py:505
  24.8 1.3 %collective-permute-start.9 = (bf16[128,256]{1,0:T(8,128)(2,1)S(1)}, bf16[128,256]{1,0:T(8,128)(2,1)S(1)}, u32[]{:S(2)}, u32[]{:S(2)}) collective-permute-start(bf16[128,256]{1,0:T(8,128)(2,1)S(1)} %collective-permute-done.4.refs_1_), channel_id=1, source_target_pairs={{0,8},{8,0},{16,24},{24,16},{32,40},{40,32},{48,56},{56,48},{64,72... | collective-permute-start | bytes 196616 | tf_op jit(solution)/shard_map/ppermute | solution.py:505
  32.5 2.2 %collective-permute-start.11 = (bf16[400,256]{1,0:T(8,128)(2,1)S(1)}, bf16[400,256]{1,0:T(8,128)(2,1)S(1)}, u32[]{:S(2)}, u32[]{:S(2)}) collective-permute-start(bf16[400,256]{1,0:T(8,128)(2,1)S(1)} %get-tuple-element.115), channel_id=1, source_target_pairs={{0,8},{8,0},{16,24},{24,16},{32,40},{40,32},{48,56},{56,48},{64,72... | collective-permute-start | bytes 614408 | tf_op jit(solution)/shard_map/ppermute | solution.py:505
  34.6 1.8 %collective-permute-start.10 = (bf16[512,256]{1,0:T(8,128)(2,1)S(1)}, bf16[512,256]{1,0:T(8,128)(2,1)S(1)}, u32[]{:S(2)}, u32[]{:S(2)}) collective-permute-start(bf16[512,256]{1,0:T(8,128)(2,1)S(1)} %key_side.5), channel_id=1, source_target_pairs={{0,8},{8,0},{16,24},{24,16},{32,40},{40,32},{48,56},{56,48},{64,72... | collective-permute-start | bytes 786440 | tf_op jit(solution)/shard_map/ppermute | solution.py:505
  34.7 5.7 %collective-permute-start.13 = (bf16[272,256]{1,0:T(8,128)(2,1)S(1)}, bf16[272,256]{1,0:T(8,128)(2,1)S(1)}, u32[]{:S(2)}, u32[]{:S(2)}) collective-permute-start(bf16[272,256]{1,0:T(8,128)(2,1)S(1)} %get-tuple-element.127), channel_id=1, source_target_pairs={{0,112},{8,16},{16,8},{24,40},{32,56},{40,24},{48,64},{56,32},{64,... | collective-permute-start | bytes 417800 | tf_op jit(solution)/shard_map/ppermute | solution.py:505
  34.8 5.3 %collective-permute-start.14 = (bf16[144,256]{1,0:T(8,128)(2,1)S(1)}, bf16[144,256]{1,0:T(8,128)(2,1)S(1)}, u32[]{:S(2)}, u32[]{:S(2)}) collective-permute-start(bf16[144,256]{1,0:T(8,128)(2,1)S(1)} %get-tuple-element.128), channel_id=1, source_target_pairs={{0,96},{8,40},{16,112},{24,56},{32,64},{40,8},{48,80},{56,24},{64,... | collective-permute-start | bytes 221192 | tf_op jit(solution)/shard_map/ppermute | solution.py:505
  36.5 7.5 %collective-permute-start.12 = (bf16[272,256]{1,0:T(8,128)(2,1)S(1)}, bf16[272,256]{1,0:T(8,128)(2,1)S(1)}, u32[]{:S(2)}, u32[]{:S(2)}) collective-permute-start(bf16[272,256]{1,0:T(8,128)(2,1)S(1)} %get-tuple-element.116), channel_id=1, source_target_pairs={{0,16},{8,120},{16,0},{24,40},{32,48},{40,24},{48,32},{56,72},{64,... | collective-permute-start | bytes 417800 | tf_op jit(solution)/shard_map/ppermute | solution.py:505
  40.4 6.4 %collective-permute-start.15 = (bf16[304,256]{1,0:T(8,128)(2,1)S(1)}, bf16[304,256]{1,0:T(8,128)(2,1)S(1)}, u32[]{:S(2)}, u32[]{:S(2)}) collective-permute-start(bf16[304,256]{1,0:T(8,128)(2,1)S(1)} %middle_sum.1), channel_id=1, source_target_pairs={{0,32},{8,104},{16,48},{24,120},{32,0},{40,72},{48,16},{56,88},{64... | collective-permute-start | bytes 466952 | tf_op jit(solution)/shard_map/ppermute | solution.py:505
  46.9 3.5 %collective-permute-start.16 = (bf16[192,256]{1,0:T(8,128)(2,1)S(1)}, bf16[192,256]{1,0:T(8,128)(2,1)S(1)}, u32[]{:S(2)}, u32[]{:S(2)}) collective-permute-start(bf16[192,256]{1,0:T(8,128)(2,1)S(1)} %get-tuple-element.130.sent_ref), channel_id=1, source_target_pairs={{0,8},{8,0},{16,24},{24,16},{32,40},{40,32},{48,56},{56,48},{64,72... | collective-permute-start | bytes 294920 | tf_op jit(solution)/shard_map/ppermute | solution.py:505

commit v5 on v4

--- a/solution.py
+++ b/solution.py
@@ -12,7 +12,7 @@
 HEAD_DIM = 128
 SCALING = HEAD_DIM**-0.5
 LOG2E = 1.4426950408889634
-HEADS_PER_STEP = 2
+HEADS_PER_STEP = 4
 CHUNK = 256
 RTILE = 16
 NT = (((1,), (1,)), ((), ()))
@@ -202,11 +202,8 @@
     ds_refs = refs[:count]
     low_refs = refs[count : 2 * count]
     extra_refs = refs[2 * count : 2 * count + extra]
-    *out_refs, q_scr, g_scr, sem = refs[2 * count + extra :]
+    *out_refs, q_scr, g_scr = refs[2 * count + extra :]
     is_near = len(out_refs) > 2
-    if is_near:
-        flush = pltpu.make_async_copy(extra_refs[0], out_refs[3], sem)
-        flush.start()
     rows = q_ref.shape[0]
     results = []
     for i, pick in enumerate(picks):
@@ -227,14 +224,13 @@
         if extra:
             out_refs[-1][n:, :] = extra_refs[0][...]
     else:
-        near_ref, drk_ref, drv_ref, _ = out_refs
+        near_ref, drk_ref, drv_ref = out_refs
         n = near_ref.shape[0]
         dk, dv = results[0]
         near_ref[:, :HEAD_DIM] = dk[:n, :]
         near_ref[:, HEAD_DIM:] = dv[:n, :]
         drk_ref[...] = dk[n:, :]
         drv_ref[...] = dv[n:, :]
-        flush.wait()
 
 
 def key_side(picks, scale, biased, masked, ds, lows, near, extra):
@@ -247,15 +243,13 @@
         shapes = [(n, lanes) for n in counts]
     else:
         shapes = [(ds[0].shape[0] - rows, lanes), (rows, HEAD_DIM), (rows, HEAD_DIM)]
-        shapes.append((rows, columns))
     keys = sum(d.shape[0] for d in ds)
     return pl.pallas_call(
         functools.partial(key_kernel, picks, len(extra)),
         out_shape=[jax.ShapeDtypeStruct(s, BF16) for s in shapes],
         in_specs=[VMEM] * (3 + 2 * len(picks) + len(extra)),
-        out_specs=[VMEM] * 3 + [ANY] if near else [VMEM] * len(shapes),
-        scratch_shapes=[pltpu.VMEM((len(picks), queries, HEAD_DIM), BF16)] * 2
-        + [pltpu.SemaphoreType.DMA],
+        out_specs=[VMEM] * len(shapes),
+        scratch_shapes=[pltpu.VMEM((len(picks), queries, HEAD_DIM), BF16)] * 2,
         compiler_params=SMALL,
         cost_estimate=pl.CostEstimate(
             flops=4 * keys * queries * HEAD_DIM, bytes_accessed=0, transcendentals=0
@@ -443,6 +437,30 @@
     )(near, one, two)
 
 
+def flush_kernel(*refs):
+    count = len(refs) // 2
+    sems = refs[-1]
+    copies = [
+        pltpu.make_async_copy(refs[i], refs[count + i], sems.at[i]) for i in range(count)
+    ]
+    for copy in copies:
+        copy.start()
+    for copy in copies:
+        copy.wait()
+
+
+def flush(arrays):
+    return pl.pallas_call(
+        flush_kernel,
+        out_shape=[jax.ShapeDtypeStruct(a.shape, a.dtype) for a in arrays],
+        in_specs=[VMEM] * len(arrays),
+        out_specs=[ANY] * len(arrays),
+        scratch_shapes=[pltpu.SemaphoreType.DMA((len(arrays),))],
+        compiler_params=SMALL,
+        name="flush",
+    )(*arrays)
+
+
 def last_sum_kernel(mine_ref, sent_ref, last_ref, r_ref, got_ref, dk_ref, dv_ref, pref_ref):
     block = mine_ref.shape[0]
     total = mine_ref[...] + last_ref[:block, :].astype(F32)
@@ -545,8 +563,11 @@
     one = move(one, to_one)
     two = move(middle_sum(two, three, four, r_tile, got), to_two)
     scale, one = lax.optimization_barrier((scale, one))
-    near, resp_key_grad, resp_value_grad, query_grad = keys_of((0,), True, query_grad)
+    near, resp_key_grad, resp_value_grad = keys_of((0,), True)
     mine, sent = chip_sum(near, one, two)
+    results = (query_grad, resp_key_grad, resp_value_grad)
+    sent, results = lax.optimization_barrier((sent, results))
+    query_grad, resp_key_grad, resp_value_grad = flush(results)
     last = move(sent, pair)
     prompt_key_grad, prompt_value_grad, pref_grad = last_sum(
         mine, sent, last, r_tile, got, pref_table.shape[0], queries.shape[1]

time: 51.4 us -> 51.2 us (level)
  Pallas kernels: 21.3 us -> 20.6 us
  waiting for transfers between devices: 5.19 us -> 5.85 us
    pallas_call x4, Pallas kernels: 7.68 us -> 6.25 us  [key_side(): pl.pallas_call(functools.partial(key_kernel, picks, len(extra)), out_shap...]
    pallas_call x0 -> x1, Pallas kernels: none -> 0.85 us  [flush(): pl.pallas_call(flush_kernel, out_shape=[jax.ShapeDtypeStruct(a.shape, a.d...]
    ppermute x17, waiting for transfers between devices: 5.19 us -> 5.85 us  [move(): return lax.ppermute(array, 'resp', moves)]
  transfers between devices with their start and end apart: 17 -> 17, of which waited for: 9 -> 9; matrix products, arithmetic and copies ran while one was open for 0% -> 0% of each run, Pallas kernels for 28% -> 26%
where the time goes in v5:
time: 51.2 us; the launch traced here: 51.1 us
  starting transfers between devices  22.5 us (44%)
  Pallas kernels  20.6 us (40%)
  waiting for transfers between devices  5.85 us (11%)
  between operations  2.13 us (4%)
    ppermute x17, starting transfers between devices, move(): return lax.ppermute(array, 'resp', moves)  22.5 us
    pallas_call x5, Pallas kernels, scores(): pl.pallas_call(functools.partial(scores_kernel, len(blocks), bool(resp)),...  7.34 us
    pallas_call x4, Pallas kernels, key_side(): pl.pallas_call(functools.partial(key_kernel, picks, len(extra)), out_shap...  6.25 us
    ppermute x17, waiting for transfers between devices, move(): return lax.ppermute(array, 'resp', moves)  5.85 us
    pallas_call x1, Pallas kernels, query_side(): pl.pallas_call(functools.partial(query_kernel, count), out_shape=[shape(l...  2.99 us
    pallas_call x1, Pallas kernels, prepare(): pl.pallas_call(prepare_kernel, out_shape=[wide, wide, slim, slim], in_spe...  1.31 us
  transfers between devices with their start and end apart: 17, of which 9 were waited for; matrix products, arithmetic and copies ran while one was open for 0% of the time, Pallas kernels for 26%

profile of v5, /device:TPU:1, one launch (start us, length us, event | category | flops | bytes accessed | tf_op | source)
XLA Modules:
  0.0 51.1 jit_solution(10702519373305045238)
XLA Ops:
  0.6 3.3 %collective-permute-start = (bf16[128,128]{1,0:T(8,128)(2,1)}, bf16[128,128]{1,0:T(8,128)(2,1)S(1)}, u32[]{:S(2)}, u32[]{:S(2)}) collective-permute-start(bf16[128,128]{1,0:T(8,128)(2,1)} %k_ref.1), channel_id=1, source_target_pairs={{0,8},{8,0},{16,24},{24,16},{32,40},{40,32},{48,56},{56,48},{64,72... | collective-permute-start | bytes 98312 | tf_op jit(solution)/shard_map/ppermute | solution.py:523
  4.0 0.1 collective-permute-start.1
  4.1 0.8 %pack.1.own_ref = bf16[128,256]{1,0:T(8,128)(2,1)S(1)} custom-call(bf16[128,128]{1,0:T(8,128)(2,1)} %k_ref.1, bf16[128,128]{1,0:T(8,128)(2,1)} %v_ref.1), custom_call_target="tpu_custom_call" | custom-call | tf_op jit(solution)/shard_map/pack/pallas_call | solution.py:273
  4.9 0.2 collective-permute-done.k_ref
  5.0 0.3 collective-permute-done.1.v_ref
  5.4 4.4 %collective-permute-start.2 = (bf16[256,256]{1,0:T(8,128)(2,1)S(1)}, bf16[256,256]{1,0:T(8,128)(2,1)S(1)}, u32[]{:S(2)}, u32[]{:S(2)}) collective-permute-start(bf16[256,256]{1,0:T(8,128)(2,1)S(1)} %assemble.1.refs_0_), channel_id=1, source_target_pairs={{0,32},{8,104},{16,48},{24,120},{32,0},{40,72},{48,16},{56,88},{64... | collective-permute-start | bytes 393224 | tf_op jit(solution)/shard_map/ppermute | solution.py:523
  9.8 0.0 collective-permute-start.5
  11.1 1.3 %prepare.1 = (bf16[256,1024]{1,0:T(8,128)(2,1)S(1)}, bf16[256,1024]{1,0:T(8,128)(2,1)S(1)}, bf16[256,128]{1,0:T(8,128)(2,1)S(1)}, bf16[256,128]{1,0:T(8,128)(2,1)S(1)}) custom-call(s32[1]{0:T(128)S(6)} %copy.15.id_ref, s32[1]{0:T(128)S(6)} %copy.16.len_ref, bf16[256,1024]{1,0:T(8,128)(2,1)} %q_hbm.1, bf16[256,1024]{1,0:T(8,128)(2,1)} %g_hbm.1, ...), custom_call_target="tpu_custom_call" | custom-call | flops 1048576 | bytes 2097152 | tf_op jit(solution)/shard_map/prepare/pallas_call | solution.py:342
  12.4 1.6 %scores.5 = (bf16[512,2048]{1,0:T(8,128)(2,1)S(1)}, f32[512,2048]{1,0:T(8,128)S(1)}, f32[8,2048]{1,0:T(8,128)S(1)}, bf16[128,512]{1,0:T(8,128)(2,1)S(1)}) custom-call(bf16[256,1024]{1,0:T(8,128)(2,1)S(1)} %get-tuple-element.76.q_ref, bf16[256,1024]{1,0:T(8,128)(2,1)S(1)} %get-tuple-element.77.g_ref, bf16[256,256]{1,0:T(8,128)(2,1)S(1)} %assemble.1.refs_0_, ...), custom_call_target="tpu_custom_call" | custom-call | flops 536870912 | tf_op jit(solution)/shard_map/scores/pallas_call | solution.py:113
  14.0 0.0 collective-permute-done.2.refs_1_
  14.0 0.8 %collective-permute-done.5.refs_0_ = bf16[256,256]{1,0:T(8,128)(2,1)S(1)} collective-permute-done((bf16[256,256]{1,0:T(8,128)(2,1)S(1)}, bf16[256,256]{1,0:T(8,128)(2,1)S(1)}, u32[]{:S(2)}, u32[]{:S(2)}) %collective-permute-start.5) | collective-permute-done | bytes 131104 | tf_op jit(solution)/shard_map/ppermute | solution.py:523
  14.8 0.0 collective-permute-start.6
  14.8 0.5 collective-permute-start.7
  15.3 0.7 %collective-permute-start.3 = (bf16[256,256]{1,0:T(8,128)(2,1)S(1)}, bf16[256,256]{1,0:T(8,128)(2,1)S(1)}, u32[]{:S(2)}, u32[]{:S(2)}) collective-permute-start(bf16[256,256]{1,0:T(8,128)(2,1)S(1)} %collective-permute-done.2.refs_1_), channel_id=1, source_target_pairs={{0,112},{8,16},{16,8},{24,40},{32,56},{40,24},{48,64},{56,32},{64,... | collective-permute-start | bytes 393224 | tf_op jit(solution)/shard_map/ppermute | solution.py:523
  16.0 1.2 %collective-permute-start.4 = (bf16[128,256]{1,0:T(8,128)(2,1)S(1)}, bf16[128,256]{1,0:T(8,128)(2,1)S(1)}, u32[]{:S(2)}, u32[]{:S(2)}) collective-permute-start(bf16[128,256]{1,0:T(8,128)(2,1)S(1)} %slice.3), channel_id=1, source_target_pairs={{0,96},{8,40},{16,112},{24,56},{32,64},{40,8},{48,80},{56,24},{64,... | collective-permute-start | bytes 196616 | tf_op jit(solution)/shard_map/ppermute | solution.py:523
  17.2 1.6 %scores.6 = (bf16[512,2048]{1,0:T(8,128)(2,1)S(1)}, f32[512,2048]{1,0:T(8,128)S(1)}, f32[8,2048]{1,0:T(8,128)S(1)}, bf16[128,512]{1,0:T(8,128)(2,1)S(1)}) custom-call(bf16[256,1024]{1,0:T(8,128)(2,1)S(1)} %get-tuple-element.76.q_ref, bf16[256,1024]{1,0:T(8,128)(2,1)S(1)} %get-tuple-element.77.g_ref, bf16[256,256]{1,0:T(8,128)(2,1)S(1)} %collective-permute-done.5.refs_0_, ...), custom_call_target="tpu_custom_call" | custom-call | flops 536870912 | tf_op jit(solution)/shard_map/scores/pallas_call | solution.py:113
  18.8 0.0 collective-permute-done.7.refs_1_
  18.8 1.6 %scores.7 = (bf16[512,2048]{1,0:T(8,128)(2,1)S(1)}, f32[512,2048]{1,0:T(8,128)S(1)}, f32[8,2048]{1,0:T(8,128)S(1)}, bf16[128,512]{1,0:T(8,128)(2,1)S(1)}) custom-call(bf16[256,1024]{1,0:T(8,128)(2,1)S(1)} %get-tuple-element.76.q_ref, bf16[256,1024]{1,0:T(8,128)(2,1)S(1)} %get-tuple-element.77.g_ref, bf16[256,256]{1,0:T(8,128)(2,1)S(1)} %collective-permute-done.6.refs_0_, ...), custom_call_target="tpu_custom_call" | custom-call | flops 536870912 | tf_op jit(solution)/shard_map/scores/pallas_call | solution.py:113
  20.5 0.6 %collective-permute-done.4.refs_1_ = bf16[128,256]{1,0:T(8,128)(2,1)S(1)} collective-permute-done((bf16[128,256]{1,0:T(8,128)(2,1)S(1)}, bf16[128,256]{1,0:T(8,128)(2,1)S(1)}, u32[]{:S(2)}, u32[]{:S(2)}) %collective-permute-start.4) | collective-permute-done | bytes 65568 | tf_op jit(solution)/shard_map/ppermute | solution.py:523
  21.1 0.0 collective-permute-done.3.refs_0_
  21.1 3.7 %collective-permute-start.8 = (bf16[256,256]{1,0:T(8,128)(2,1)S(1)}, bf16[256,256]{1,0:T(8,128)(2,1)S(1)}, u32[]{:S(2)}, u32[]{:S(2)}) collective-permute-start(bf16[256,256]{1,0:T(8,128)(2,1)S(1)} %collective-permute-done.3.refs_0_), channel_id=1, source_target_pairs={{0,8},{8,0},{16,24},{24,16},{32,40},{40,32},{48,56},{56,48},{64,72... | collective-permute-start | bytes 393224 | tf_op jit(solution)/shard_map/ppermute | solution.py:523
  24.8 0.0 collective-permute-start.9
  24.8 1.3 %scores.8 = (bf16[384,2048]{1,0:T(8,128)(2,1)S(1)}, f32[384,2048]{1,0:T(8,128)S(1)}, f32[8,2048]{1,0:T(8,128)S(1)}, bf16[128,384]{1,0:T(8,128)(2,1)S(1)}) custom-call(bf16[256,1024]{1,0:T(8,128)(2,1)S(1)} %get-tuple-element.76.q_ref, bf16[256,1024]{1,0:T(8,128)(2,1)S(1)} %get-tuple-element.77.g_ref, bf16[256,256]{1,0:T(8,128)(2,1)S(1)} %collective-permute-done.3.refs_0_, ...), custom_call_target="tpu_custom_call" | custom-call | flops 402653184 | tf_op jit(solution)/shard_map/scores/pallas_call | solution.py:113
  26.1 0.0 collective-permute-done.8.refs_0_
  26.1 1.3 %scores.9 = (bf16[384,2048]{1,0:T(8,128)(2,1)S(1)}, f32[384,2048]{1,0:T(8,128)S(1)}, f32[8,2048]{1,0:T(8,128)S(1)}, bf16[128,384]{1,0:T(8,128)(2,1)S(1)}) custom-call(bf16[256,1024]{1,0:T(8,128)(2,1)S(1)} %get-tuple-element.76.q_ref, bf16[256,1024]{1,0:T(8,128)(2,1)S(1)} %get-tuple-element.77.g_ref, bf16[256,256]{1,0:T(8,128)(2,1)S(1)} %collective-permute-done.8.refs_0_, ...), custom_call_target="tpu_custom_call" | custom-call | flops 402653184 | tf_op jit(solution)/shard_map/scores/pallas_call | solution.py:113
  27.4 3.0 %query_side.1 = (bf16[512,2048]{1,0:T(8,128)(2,1)S(1)}, bf16[512,2048]{1,0:T(8,128)(2,1)S(1)}, bf16[512,2048]{1,0:T(8,128)(2,1)S(1)}, bf16[384,2048]{1,0:T(8,128...) custom-call(s32[1]{0:T(128)S(6)} %copy.15.id_ref, ...), custom_call_target="tpu_custom_call" | custom-call | flops 1207959552 | tf_op jit(solution)/shard_map/query_side/pallas_call | solution.py:181
  30.4 2.0 %key_side.6 = (bf16[384,256]{1,0:T(8,128)(2,1)S(1)}, bf16[400,256]{1,0:T(8,128)(2,1)S(1)}) custom-call(f32[8,2048]{1,0:T(8,128)S(1)} %get-tuple-element.123.scale_ref, bf16[256,1024]{1,0:T(8,128)(2,1)S(1)} %get-tuple-element.76.q_ref, bf16[256,1024]{1,0:T(8,128)(2,1)S(1)} %get-tuple-element.77.g_ref, bf16[384,2048]{1,0:T(8,128)(2,1)S(1)} %get-tuple-element.119.refs_0_, ...), custom_call_target="tpu_custom_call" | custom-call | flops 805306368 | tf_op jit(solution)/shard_map/key_side/pallas_call | solution.py:247
  32.3 0.6 %collective-permute-start.11 = (bf16[400,256]{1,0:T(8,128)(2,1)S(1)}, bf16[400,256]{1,0:T(8,128)(2,1)S(1)}, u32[]{:S(2)}, u32[]{:S(2)}) collective-permute-start(bf16[400,256]{1,0:T(8,128)(2,1)S(1)} %get-tuple-element.121), channel_id=1, source_target_pairs={{0,8},{8,0},{16,24},{24,16},{32,40},{40,32},{48,56},{56,48},{64,72... | collective-permute-start | bytes 614408 | tf_op jit(solution)/shard_map/ppermute | solution.py:523
  33.0 1.4 %key_side.5 = bf16[512,256]{1,0:T(8,128)(2,1)S(1)} custom-call(f32[8,2048]{1,0:T(8,128)S(1)} %get-tuple-element.123.scale_ref, bf16[256,1024]{1,0:T(8,128)(2,1)S(1)} %get-tuple-element.76.q_ref, bf16[256,1024]{1,0:T(8,128)(2,1)S(1)} %get-tuple-element.77.g_ref, bf16[512,2048]{1,0:T(8,128)(2,1)S(1)} %get-tuple-element.117.refs_0_, ...), custom_call_target="tpu_custom_call" | custom-call | flops 536870912 | tf_op jit(solution)/shard_map/key_side/pallas_call | solution.py:247
  34.4 0.1 collective-permute-start.10
  34.5 0.0 collective-permute-done.11.mate_ref.got_ref
  34.5 0.1 pair_sum.3
  34.6 0.1 collective-permute-start.13
  34.7 0.1 collective-permute-start.14
  34.8 1.4 %key_side.4.direct_ref = bf16[512,256]{1,0:T(8,128)(2,1)S(1)} custom-call(f32[8,2048]{1,0:T(8,128)S(1)} %get-tuple-element.123.scale_ref, bf16[256,1024]{1,0:T(8,128)(2,1)S(1)} %get-tuple-element.76.q_ref, bf16[256,1024]{1,0:T(8,128)(2,1)S(1)} %get-tuple-element.77.g_ref, bf16[512,2048]{1,0:T(8,128)(2,1)S(1)} %get-tuple-element.116.refs_0_, ...), custom_call_target="tpu_custom_call" | custom-call | flops 536870912 | tf_op jit(solution)/shard_map/key_side/pallas_call | solution.py:247
  36.2 0.1 pair_sum.2
  36.3 3.2 %collective-permute-start.12 = (bf16[272,256]{1,0:T(8,128)(2,1)S(1)}, bf16[272,256]{1,0:T(8,128)(2,1)S(1)}, u32[]{:S(2)}, u32[]{:S(2)}) collective-permute-start(bf16[272,256]{1,0:T(8,128)(2,1)S(1)} %get-tuple-element.122), channel_id=1, source_target_pairs={{0,16},{8,120},{16,0},{24,40},{32,48},{40,24},{48,32},{56,72},{64,... | collective-permute-start | bytes 417800 | tf_op jit(solution)/shard_map/ppermute | solution.py:523
  39.5 0.4 collective-permute-done.14.four_ref
  39.9 0.3 collective-permute-done.13.three_ref
  40.3 1.9 %collective-permute-start.15 = (bf16[304,256]{1,0:T(8,128)(2,1)S(1)}, bf16[304,256]{1,0:T(8,128)(2,1)S(1)}, u32[]{:S(2)}, u32[]{:S(2)}) collective-permute-start(bf16[304,256]{1,0:T(8,128)(2,1)S(1)} %middle_sum.1), channel_id=1, source_target_pairs={{0,32},{8,104},{16,48},{24,120},{32,0},{40,72},{48,16},{56,88},{64... | collective-permute-start | bytes 466952 | tf_op jit(solution)/shard_map/ppermute | solution.py:523
  42.1 1.7 %collective-permute-done.12.one_ref = bf16[272,256]{1,0:T(8,128)(2,1)S(1)} collective-permute-done((bf16[272,256]{1,0:T(8,128)(2,1)S(1)}, bf16[272,256]{1,0:T(8,128)(2,1)S(1)}, u32[]{:S(2)}, u32[]{:S(2)}) %collective-permute-start.12) | collective-permute-done | bytes 139296 | tf_op jit(solution)/shard_map/ppermute | solution.py:523
  43.8 1.4 %key_side.7 = (bf16[256,256]{1,0:T(8,128)(2,1)S(1)}, bf16[256,128]{1,0:T(8,128)(2,1)S(1)}, bf16[256,128]{1,0:T(8,128)(2,1)S(1)}) custom-call(f32[8,2048]{1,0:T(8,128)S(1)} %get-tuple-element.123.scale_ref, bf16[256,1024]{1,0:T(8,128)(2,1)S(1)} %get-tuple-element.76.q_ref, bf16[256,1024]{1,0:T(8,128)(2,1)S(1)} %get-tuple-element.77.g_ref, ...), custom_call_target="tpu_custom_call" | custom-call | flops 536870912 | tf_op jit(solution)/shard_map/key_side/pallas_call | solution.py:247
  45.2 1.4 %collective-permute-done.15.two_ref = bf16[304,256]{1,0:T(8,128)(2,1)S(1)} collective-permute-done((bf16[304,256]{1,0:T(8,128)(2,1)S(1)}, bf16[304,256]{1,0:T(8,128)(2,1)S(1)}, u32[]{:S(2)}, u32[]{:S(2)}) %collective-permute-start.15) | collective-permute-done | bytes 155680 | tf_op jit(solution)/shard_map/ppermute | solution.py:523
  46.6 0.1 chip_sum.1
  46.7 2.6 %collective-permute-start.16 = (bf16[192,256]{1,0:T(8,128)(2,1)S(1)}, bf16[192,256]{1,0:T(8,128)(2,1)S(1)}, u32[]{:S(2)}, u32[]{:S(2)}) collective-permute-start(bf16[192,256]{1,0:T(8,128)(2,1)S(1)} %get-tuple-element.142.sent_ref), channel_id=1, source_target_pairs={{0,8},{8,0},{16,24},{24,16},{32,40},{40,32},{48,56},{56,48},{64,72... | collective-permute-start | bytes 294920 | tf_op jit(solution)/shard_map/ppermute | solution.py:523
  49.3 0.8 %flush.1 = (bf16[256,1024]{1,0:T(8,128)(2,1)}, bf16[256,128]{1,0:T(8,128)(2,1)}, bf16[256,128]{1,0:T(8,128)(2,1)}) custom-call(bf16[256,1024]{1,0:T(8,128)(2,1)S(1)} %get-tuple-element.135.refs_0_, bf16[256,128]{1,0:T(8,128)(2,1)S(1)} %get-tuple-element.136.refs_1_, bf16[256,128]{1,0:T(8,128)(2,1)S(1)} %get-tuple-element.137.refs_2_), custom_call_target="tpu_custom_call" | custom-call | tf_op jit(solution)/shard_map/flush/pallas_call | solution.py:453
  50.2 0.1 collective-permute-done.16.last_ref
  50.2 0.8 %last_sum.1 = (bf16[128,128]{1,0:T(8,128)(2,1)}, bf16[128,128]{1,0:T(8,128)(2,1)}, f32[16,1024]{1,0:T(8,128)}) custom-call(f32[128,256]{1,0:T(8,128)S(1)} %get-tuple-element.141.mine_ref, bf16[192,256]{1,0:T(8,128)(2,1)S(1)} %get-tuple-element.142.sent_ref, bf16[192,256]{1,0:T(8,128)(2,1)S(1)} %collective-permute-done.16.last_ref, ...), custom_call_target="tpu_custom_call" | custom-call | tf_op jit(solution)/shard_map/last_sum/pallas_call | solution.py:490
  (6 shorter events, 0.1 us)
Async XLA Ops:
  0.6 4.4 %collective-permute-start = (bf16[128,128]{1,0:T(8,128)(2,1)}, bf16[128,128]{1,0:T(8,128)(2,1)S(1)}, u32[]{:S(2)}, u32[]{:S(2)}) collective-permute-start(bf16[128,128]{1,0:T(8,128)(2,1)} %k_ref.1), channel_id=1, source_target_pairs={{0,8},{8,0},{16,24},{24,16},{32,40},{40,32},{48,56},{56,48},{64,72... | collective-permute-start | bytes 98312 | tf_op jit(solution)/shard_map/ppermute | solution.py:523
  4.0 1.4 %collective-permute-start.1 = (bf16[128,128]{1,0:T(8,128)(2,1)}, bf16[128,128]{1,0:T(8,128)(2,1)S(1)}, u32[]{:S(2)}, u32[]{:S(2)}) collective-permute-start(bf16[128,128]{1,0:T(8,128)(2,1)} %v_ref.1), channel_id=1, source_target_pairs={{0,8},{8,0},{16,24},{24,16},{32,40},{40,32},{48,56},{56,48},{64,72... | collective-permute-start | bytes 98312 | tf_op jit(solution)/shard_map/ppermute | solution.py:523
  5.4 8.6 %collective-permute-start.2 = (bf16[256,256]{1,0:T(8,128)(2,1)S(1)}, bf16[256,256]{1,0:T(8,128)(2,1)S(1)}, u32[]{:S(2)}, u32[]{:S(2)}) collective-permute-start(bf16[256,256]{1,0:T(8,128)(2,1)S(1)} %assemble.1.refs_0_), channel_id=1, source_target_pairs={{0,32},{8,104},{16,48},{24,120},{32,0},{40,72},{48,16},{56,88},{64... | collective-permute-start | bytes 393224 | tf_op jit(solution)/shard_map/ppermute | solution.py:523
  9.8 5.0 %collective-permute-start.5 = (bf16[256,256]{1,0:T(8,128)(2,1)S(1)}, bf16[256,256]{1,0:T(8,128)(2,1)S(1)}, u32[]{:S(2)}, u32[]{:S(2)}) collective-permute-start(bf16[256,256]{1,0:T(8,128)(2,1)S(1)} %assemble.1.refs_0_), channel_id=1, source_target_pairs={{0,16},{8,120},{16,0},{24,40},{32,48},{40,24},{48,32},{56,72},{64,... | collective-permute-start | bytes 393224 | tf_op jit(solution)/shard_map/ppermute | solution.py:523
  14.8 4.0 %collective-permute-start.6 = (bf16[256,256]{1,0:T(8,128)(2,1)S(1)}, bf16[256,256]{1,0:T(8,128)(2,1)S(1)}, u32[]{:S(2)}, u32[]{:S(2)}) collective-permute-start(bf16[256,256]{1,0:T(8,128)(2,1)S(1)} %collective-permute-done.5.refs_0_), channel_id=1, source_target_pairs={{0,8},{8,0},{16,24},{24,16},{32,40},{40,32},{48,56},{56,48},{64,72... | collective-permute-start | bytes 393224 | tf_op jit(solution)/shard_map/ppermute | solution.py:523
  14.8 4.0 %collective-permute-start.7 = (bf16[256,256]{1,0:T(8,128)(2,1)S(1)}, bf16[256,256]{1,0:T(8,128)(2,1)S(1)}, u32[]{:S(2)}, u32[]{:S(2)}) collective-permute-start(bf16[256,256]{1,0:T(8,128)(2,1)S(1)} %collective-permute-done.2.refs_1_), channel_id=1, source_target_pairs={{0,8},{8,0},{16,24},{24,16},{32,40},{40,32},{48,56},{56,48},{64,72... | collective-permute-start | bytes 393224 | tf_op jit(solution)/shard_map/ppermute | solution.py:523
  15.3 5.8 %collective-permute-start.3 = (bf16[256,256]{1,0:T(8,128)(2,1)S(1)}, bf16[256,256]{1,0:T(8,128)(2,1)S(1)}, u32[]{:S(2)}, u32[]{:S(2)}) collective-permute-start(bf16[256,256]{1,0:T(8,128)(2,1)S(1)} %collective-permute-done.2.refs_1_), channel_id=1, source_target_pairs={{0,112},{8,16},{16,8},{24,40},{32,56},{40,24},{48,64},{56,32},{64,... | collective-permute-start | bytes 393224 | tf_op jit(solution)/shard_map/ppermute | solution.py:523
  16.0 5.1 %collective-permute-start.4 = (bf16[128,256]{1,0:T(8,128)(2,1)S(1)}, bf16[128,256]{1,0:T(8,128)(2,1)S(1)}, u32[]{:S(2)}, u32[]{:S(2)}) collective-permute-start(bf16[128,256]{1,0:T(8,128)(2,1)S(1)} %slice.3), channel_id=1, source_target_pairs={{0,96},{8,40},{16,112},{24,56},{32,64},{40,8},{48,80},{56,24},{64,... | collective-permute-start | bytes 196616 | tf_op jit(solution)/shard_map/ppermute | solution.py:523
  21.1 5.0 %collective-permute-start.8 = (bf16[256,256]{1,0:T(8,128)(2,1)S(1)}, bf16[256,256]{1,0:T(8,128)(2,1)S(1)}, u32[]{:S(2)}, u32[]{:S(2)}) collective-permute-start(bf16[256,256]{1,0:T(8,128)(2,1)S(1)} %collective-permute-done.3.refs_0_), channel_id=1, source_target_pairs={{0,8},{8,0},{16,24},{24,16},{32,40},{40,32},{48,56},{56,48},{64,72... | collective-permute-start | bytes 393224 | tf_op jit(solution)/shard_map/ppermute | solution.py:523
  24.8 1.3 %collective-permute-start.9 = (bf16[128,256]{1,0:T(8,128)(2,1)S(1)}, bf16[128,256]{1,0:T(8,128)(2,1)S(1)}, u32[]{:S(2)}, u32[]{:S(2)}) collective-permute-start(bf16[128,256]{1,0:T(8,128)(2,1)S(1)} %collective-permute-done.4.refs_1_), channel_id=1, source_target_pairs={{0,8},{8,0},{16,24},{24,16},{32,40},{40,32},{48,56},{56,48},{64,72... | collective-permute-start | bytes 196616 | tf_op jit(solution)/shard_map/ppermute | solution.py:523
  32.3 2.2 %collective-permute-start.11 = (bf16[400,256]{1,0:T(8,128)(2,1)S(1)}, bf16[400,256]{1,0:T(8,128)(2,1)S(1)}, u32[]{:S(2)}, u32[]{:S(2)}) collective-permute-start(bf16[400,256]{1,0:T(8,128)(2,1)S(1)} %get-tuple-element.121), channel_id=1, source_target_pairs={{0,8},{8,0},{16,24},{24,16},{32,40},{40,32},{48,56},{56,48},{64,72... | collective-permute-start | bytes 614408 | tf_op jit(solution)/shard_map/ppermute | solution.py:523
  34.4 1.8 %collective-permute-start.10 = (bf16[512,256]{1,0:T(8,128)(2,1)S(1)}, bf16[512,256]{1,0:T(8,128)(2,1)S(1)}, u32[]{:S(2)}, u32[]{:S(2)}) collective-permute-start(bf16[512,256]{1,0:T(8,128)(2,1)S(1)} %key_side.5), channel_id=1, source_target_pairs={{0,8},{8,0},{16,24},{24,16},{32,40},{40,32},{48,56},{56,48},{64,72... | collective-permute-start | bytes 786440 | tf_op jit(solution)/shard_map/ppermute | solution.py:523
  34.6 5.7 %collective-permute-start.13 = (bf16[272,256]{1,0:T(8,128)(2,1)S(1)}, bf16[272,256]{1,0:T(8,128)(2,1)S(1)}, u32[]{:S(2)}, u32[]{:S(2)}) collective-permute-start(bf16[272,256]{1,0:T(8,128)(2,1)S(1)} %get-tuple-element.129), channel_id=1, source_target_pairs={{0,112},{8,16},{16,8},{24,40},{32,56},{40,24},{48,64},{56,32},{64,... | collective-permute-start | bytes 417800 | tf_op jit(solution)/shard_map/ppermute | solution.py:523
  34.7 5.3 %collective-permute-start.14 = (bf16[144,256]{1,0:T(8,128)(2,1)S(1)}, bf16[144,256]{1,0:T(8,128)(2,1)S(1)}, u32[]{:S(2)}, u32[]{:S(2)}) collective-permute-start(bf16[144,256]{1,0:T(8,128)(2,1)S(1)} %get-tuple-element.130), channel_id=1, source_target_pairs={{0,96},{8,40},{16,112},{24,56},{32,64},{40,8},{48,80},{56,24},{64,... | collective-permute-start | bytes 221192 | tf_op jit(solution)/shard_map/ppermute | solution.py:523
  36.3 7.5 %collective-permute-start.12 = (bf16[272,256]{1,0:T(8,128)(2,1)S(1)}, bf16[272,256]{1,0:T(8,128)(2,1)S(1)}, u32[]{:S(2)}, u32[]{:S(2)}) collective-permute-start(bf16[272,256]{1,0:T(8,128)(2,1)S(1)} %get-tuple-element.122), channel_id=1, source_target_pairs={{0,16},{8,120},{16,0},{24,40},{32,48},{40,24},{48,32},{56,72},{64,... | collective-permute-start | bytes 417800 | tf_op jit(solution)/shard_map/ppermute | solution.py:523
  40.3 6.4 %collective-permute-start.15 = (bf16[304,256]{1,0:T(8,128)(2,1)S(1)}, bf16[304,256]{1,0:T(8,128)(2,1)S(1)}, u32[]{:S(2)}, u32[]{:S(2)}) collective-permute-start(bf16[304,256]{1,0:T(8,128)(2,1)S(1)} %middle_sum.1), channel_id=1, source_target_pairs={{0,32},{8,104},{16,48},{24,120},{32,0},{40,72},{48,16},{56,88},{64... | collective-permute-start | bytes 466952 | tf_op jit(solution)/shard_map/ppermute | solution.py:523
  46.7 3.6 %collective-permute-start.16 = (bf16[192,256]{1,0:T(8,128)(2,1)S(1)}, bf16[192,256]{1,0:T(8,128)(2,1)S(1)}, u32[]{:S(2)}, u32[]{:S(2)}) collective-permute-start(bf16[192,256]{1,0:T(8,128)(2,1)S(1)} %get-tuple-element.142.sent_ref), channel_id=1, source_target_pairs={{0,8},{8,0},{16,24},{24,16},{32,40},{40,32},{48,56},{56,48},{64,72... | collective-permute-start | bytes 294920 | tf_op jit(solution)/shard_map/ppermute | solution.py:523
